TPU v7x, 32 devices: a whole 2x2x4 slice. The times are simulated.
32 devices in a mesh: groups: 2 (over x), along: 8 (over z, y), across: 2 (over core).
Axes of the slice: x: 2, y: 2, z: 4, core: 2. Of those that a mesh axis runs over, the one named last changes fastest.
Arguments:
- toa_bands: bfloat16 [1024, 4, 2048], P(('groups', 'along'), None, 'across'), parts along dimension 0, may hold values from 0.019897461 to 0.59765625
- dark_mask: int32 [1024, 2048], P(('groups', 'along'), 'across'), parts along dimension 0, may hold values 0 or 1
- vapour: float32 [1024, 2048], P(('groups', 'along'), 'across'), parts along dimension 0, may hold values from 0 to 7
- elev_class: int32 [1024, 2048], P(('groups', 'along'), 'across'), parts along dimension 0, may hold values from 0 to 6
- elev_frac: float32 [1024, 2048], P(('groups', 'along'), 'across'), parts along dimension 0, may hold values from 0 to 1
- kernel: float32 [61], replicated, may hold values from 0.1 to 1
- lut_gain: bfloat16 [4, 8, 16, 8], replicated, may hold values from 1 to 2
- lut_path: bfloat16 [4, 8, 16, 8], replicated, may hold values from 0 to 0.29882812
- lut_albedo: bfloat16 [4, 8, 16, 8], replicated, may hold values from 0.049804688 to 0.25
- routes: int32 [64, 2], P(('groups', 'along')), parts along dimension 0, may hold values from 0 to 7, as said below
- starts: int32 [64, 2], P(('groups', 'along')), parts along dimension 0, may hold values from 0 to 48
Outputs:
- tile_out: bfloat16 [16, 64, 4, 2048], P(('groups', 'along'), None, None, 'across'), parts along dimension 0
There are 2 independent parts, one for each index of `groups`. A program takes and returns all parts, laid end to end along the dimension named above; an argument that names none is the same for every part. Nothing has to cross between parts.
Inputs may be any that keep to these rules, and one draw needn't show every extreme that they name: `dark_mask`: 1 marks a dark pixel. `elev_class`: the class and the next one are both classes of the table. `routes`: the first block of segment s is s // 4, the block of the segment's own rows; the second lies 1 to 2 blocks before or after it; among the 4 segments of one device at most 2 have their second block at any one signed distance, and in every draw some device has exactly 2 at some distance.
All inputs are finite; a program needn't handle non-finite values. No bound on the sum of `dark_mask` on one device may be relied on, other than what follows from the above.
Results may differ from a plain program's by a relative error of at most 0.0043.
Values may be sent and summed in bfloat16 or wider, within the bound.
No kernel may reach another device: no remote copies, remote signals or barrier semaphores. Data moves between devices by JAX's collectives and lax.ppermute only.
A program may use at most 64 MiB of HBM per device.

v0:
```python
import math

import jax
import jax.numpy as jnp
from jax import lax
from jax.sharding import PartitionSpec as P

SEG = 16
REACH = 2
CAP = 2


highest = lax.Precision.HIGHEST


def with_halo(block, sides, width):
    for axis, dim in sides:
        count = lax.axis_size(axis)
        forward = [(i, i + 1) for i in range(count - 1)]
        backward = [(target, source) for source, target in forward]
        low = lax.ppermute(
            lax.slice_in_dim(block, block.shape[dim] - width, None, axis=dim), axis, forward
        )
        high = lax.ppermute(lax.slice_in_dim(block, 0, width, axis=dim), axis, backward)
        block = jnp.concatenate([low, block, high], axis=dim)
    return block


def from_behind(value, axis, steps):
    count = lax.axis_size(axis)
    initial, last = (max(0, -steps), min(count, count - steps))
    return lax.ppermute(value, axis, [(source, source + steps) for source in range(initial, last)])


def band_matrix(kernel, block_size):
    tap_count = kernel.shape[0]
    rows_at = jnp.arange(block_size + tap_count - 1)[:, None, None]
    cols_at = jnp.arange(block_size)[None, :, None]
    tap_ids = jnp.arange(tap_count)[None, None, :]
    return jnp.sum(jnp.where(rows_at - cols_at == tap_ids, kernel[None, None, :], 0.0), axis=2)


def smooth_rows(fields, kernel):
    tap_count = kernel.shape[0]
    length = fields.shape[1] - tap_count + 1
    block_size = math.gcd(length, 128)
    matrix = band_matrix(kernel, block_size)
    pieces = jnp.einsum("mr,fmc->frc", matrix, fields, precision=highest)
    return pieces


def smooth_cols(fields, kernel):
    tap_count = kernel.shape[0]
    length = fields.shape[2] - tap_count + 1
    block_size = math.gcd(length, 128)
    matrix = band_matrix(kernel, block_size)
    pieces = []
    for number in range(length // block_size):
        window = fields[
            :, :, number * block_size : number * block_size + block_size + tap_count - 1
        ]
        pieces.append(jnp.einsum("frm,mc->frc", window, matrix, precision=highest))
    return jnp.concatenate(pieces, axis=2)


def place_rows(rows, first, tile_rows):
    placed = (
        jnp.arange(tile_rows)[None, :, None]
        == first[:, None, None] + jnp.arange(SEG)[None, None, :]
    ) & (first >= 0)[:, None, None]
    summed = jnp.einsum(
        "srj,sjx->rx", placed.astype(jnp.bfloat16), rows, preferred_element_type=jnp.float32
    )
    counts = jnp.sum(placed.astype(jnp.float32), axis=(0, 2))
    return (summed, counts)


def body(
    toa_bands,
    dark_mask,
    vapour,
    elev_class,
    elev_frac,
    kernel,
    lut_gain,
    lut_path,
    lut_albedo,
    routes,
    starts,
):
    row_count, band_count, col_count = toa_bands.shape
    half_width = kernel.shape[0] // 2
    levels_e, levels_a, levels_w = (lut_gain.shape[1], lut_gain.shape[2], lut_gain.shape[3])
    darkness = dark_mask.astype(jnp.float32)
    blue_band = toa_bands[:, 0, :].astype(jnp.float32)
    red_band = toa_bands[:, 2, :].astype(jnp.float32)
    fields = jnp.stack([darkness * 8.0 * (blue_band - 0.5 * red_band), darkness])
    padded = with_halo(fields, (("along", 1), ("across", 2)), half_width)
    rowwise = smooth_rows(padded, kernel)
    smoothed = smooth_cols(rowwise, kernel)
    aerosol = smoothed[0] / jnp.maximum(smoothed[1], 1.0)
    aero_pos = (levels_a - 1) * jax.nn.sigmoid(aerosol)
    lut_table = jnp.stack([lut_gain, lut_path, lut_albedo], axis=1).reshape(
        band_count * 3 * levels_e, levels_a * levels_w
    )
    block_rows = math.gcd(row_count, 16)
    block_count = row_count // block_rows

    def correct_block(inputs):
        toa_block, pos_block, vapour_block, class_block, frac_block = inputs
        weight_a = jnp.maximum(
            0.0,
            1.0 - jnp.abs(pos_block[None] - jnp.arange(levels_a, dtype=jnp.float32)[:, None, None]),
        )
        weight_w = jnp.maximum(
            0.0,
            1.0
            - jnp.abs(vapour_block[None] - jnp.arange(levels_w, dtype=jnp.float32)[:, None, None]),
        )
        joint_weight = (
            (weight_a[:, None] * weight_w[None])
            .reshape(levels_a * levels_w, block_rows * col_count)
            .astype(jnp.bfloat16)
        )
        node_values = jnp.dot(lut_table, joint_weight, preferred_element_type=jnp.float32)
        node_values = node_values.reshape(band_count, 3, levels_e, block_rows, col_count)
        elev_ids = jnp.arange(levels_e)[:, None, None]
        weight_e = jnp.where(elev_ids == class_block[None], 1.0 - frac_block[None], 0.0)
        weight_e = weight_e + jnp.where(elev_ids == class_block[None] + 1, frac_block[None], 0.0)
        coefficient = jnp.sum(node_values * weight_e[None, None], axis=2)
        radiance = jnp.transpose(toa_block.astype(jnp.float32), (1, 0, 2))
        scaled = coefficient[:, 0] * radiance - coefficient[:, 1]
        surface = scaled / (1.0 + coefficient[:, 2] * scaled)
        return jnp.transpose(surface, (1, 0, 2)).astype(jnp.bfloat16)

    inputs = (
        toa_bands.reshape(block_count, block_rows, band_count, col_count),
        aero_pos.reshape(block_count, block_rows, col_count),
        vapour.reshape(block_count, block_rows, col_count),
        elev_class.reshape(block_count, block_rows, col_count),
        elev_frac.reshape(block_count, block_rows, col_count),
    )
    corrected = lax.map(correct_block, inputs).reshape(row_count, band_count, col_count)
    seg_dev = routes.shape[0]
    row_width = band_count * col_count
    own_tile = lax.axis_index("along")
    segment_rows = corrected.reshape(seg_dev, SEG, row_width)
    own_first = jnp.where(routes[:, 0] == own_tile, starts[:, 0], -1)
    summed, counts = place_rows(segment_rows, own_first, row_count)
    sides = [side - REACH for side in range(REACH)] + [side + 1 for side in range(REACH)]
    flat_rows = segment_rows.reshape(seg_dev, SEG * row_width)
    distance = routes[:, 1] - own_tile
    for side in sides:
        is_side = (distance == side).astype(jnp.int32)
        rank = jnp.cumsum(is_side) - is_side
        chosen = (is_side[None, :] == 1) & (rank[None, :] == jnp.arange(CAP)[:, None])
        outgoing = jnp.dot(
            chosen.astype(jnp.bfloat16), flat_rows, preferred_element_type=jnp.float32
        ).astype(jnp.bfloat16)
        slot_tag = jnp.sum(jnp.where(chosen, starts[:, 1][None, :] + 1, 0), axis=1)
        got_rows, got_tag = from_behind((outgoing, slot_tag), "along", side)
        part_sum, part_count = place_rows(
            got_rows.reshape(CAP, SEG, row_width), got_tag - 1, row_count
        )
        summed = summed + part_sum
        counts = counts + part_count
    tile_out = (summed / jnp.maximum(counts, 1.0)[:, None]).astype(jnp.bfloat16)
    return tile_out.reshape(1, row_count, band_count, col_count)


def solution(mesh):
    in_specs = (
        P(("groups", "along"), None, "across"),
        P(("groups", "along"), "across"),
        P(("groups", "along"), "across"),
        P(("groups", "along"), "across"),
        P(("groups", "along"), "across"),
        P(),
        P(),
        P(),
        P(),
        P(("groups", "along"), None),
        P(("groups", "along"), None),
    )
    out_specs = P(("groups", "along"), None, None, "across")
    return jax.shard_map(body, mesh=mesh, in_specs=in_specs, out_specs=out_specs, check_vma=False)
```

profile of v0, /device:TPU:0, one launch (start us, length us, event | category | flops | bytes accessed | tf_op | source)
XLA Modules:
  0.0 118.5 jit_solution(6398646044948553667)
XLA Ops:
  1.2 1.7 %fusion.77 = (bf16[64,1,1024]{2,1,0:T(2,128)(2,1)S(1)}, bf16[64,1,1024]{2,1,0:T(2,128)(2,1)S(1)}) fusion(bf16[64,4,1024]{2,1,0:T(4,128)(2,1)} %param.13), kind=kLoop, calls=%fused_computation.170 | loop fusion | bytes 524288 | tf_op jit(solution)/shard_map/slice | solution.py:95
  7.2 5.5 %collective-permute-start = (f32[2,30,1024]{2,0,1:T(2,128)}, f32[2,30,1024]{2,0,1:T(2,128)S(1)}, u32[]{:S(2)}, u32[]{:S(2)}) collective-permute-start(f32[2,30,1024]{2,0,1:T(2,128)} %copy.54), channel_id=1, source_target_pairs={{0,2},{2,4},{4,6},{6,8},{8,10},{10,12},{12,14},{1,3},{3,5},{5,7},{... | collective-permute-start | bytes 737288 | tf_op jit(solution)/shard_map/ppermute | solution.py:21
  13.6 4.0 %collective-permute-start.10 = (s32[2]{0:T(128)S(1)}, s32[2]{0:T(128)S(1)}, u32[]{:S(2)}, u32[]{:S(2)}) collective-permute-start(s32[2]{0:T(128)S(1)} %get-tuple-element.67), channel_id=1, source_target_pairs={{0,4},{2,6},{4,8},{6,10},{8,12},{10,14},{1,5},{3,7},{5,9},{7,11},{... | collective-permute-start | bytes 32 | tf_op jit(solution)/shard_map/ppermute | solution.py:32
  17.6 4.3 %collective-permute-start.8 = (s32[2]{0:T(128)S(1)}, s32[2]{0:T(128)S(1)}, u32[]{:S(2)}, u32[]{:S(2)}) collective-permute-start(s32[2]{0:T(128)S(1)} %get-tuple-element.66), channel_id=1, source_target_pairs={{0,2},{2,4},{4,6},{6,8},{8,10},{10,12},{12,14},{1,3},{3,5},{5,7},{... | collective-permute-start | bytes 32 | tf_op jit(solution)/shard_map/ppermute | solution.py:32
  27.4 3.9 %collective-permute-done.4 = s32[2]{0:T(128)S(1)} collective-permute-done((s32[2]{0:T(128)S(1)}, s32[2]{0:T(128)S(1)}, u32[]{:S(2)}, u32[]{:S(2)}) %collective-permute-start.4) | collective-permute-done | bytes 40 | tf_op jit(solution)/shard_map/ppermute | solution.py:32
  33.2 1.4 %copy.56 = f32[2,30,1024]{1,2,0:T(8,128)} copy(f32[2,30,1024]{2,0,1:T(2,128)S(1)} %collective-permute-done) | data formatting | bytes 491520 | tf_op jit(solution)/shard_map/ppermute | solution.py:21
  34.5 1.8 %pad_maximum_fusion.1 = f32[2,124,1024]{1,2,0:T(8,128)S(1)} fusion(f32[2,30,1024]{1,2,0:T(8,128)S(1)} %copy.57, f32[1,64,1024]{1,2,0:T(8,128)S(1)} %convert_bitcast_fusion.1, f32[1,64,1024]{1,2,0:T(8,128)S(1)} %fusion.14, f32[2,30,1024]{1,2,0:T(8,128)} %copy.56), kind=kLoop, calls=%fused_computation.58 | loop fusion | flops 761856 | bytes 2031616 | tf_op jit(solution)/shard_map/concatenate | solution.py:25
  36.4 1.4 %collective-permute-start.2 = (f32[2,124,30]{1,2,0:T(8,128)S(1)}, f32[2,124,30]{1,2,0:T(8,128)S(1)}, u32[]{:S(2)}, u32[]{:S(2)}) collective-permute-start(f32[2,124,30]{1,2,0:T(8,128)S(1)} %get-tuple-element.94), channel_id=1, source_target_pairs={{0,1},{2,3},{4,5},{6,7},{8,9},{10,11},{12,13},{14,15},{16,17},{18,... | collective-permute-start | bytes 89288 | tf_op jit(solution)/shard_map/ppermute | solution.py:21
  37.8 1.5 %collective-permute-start.3 = (f32[2,124,30]{1,2,0:T(8,128)S(1)}, f32[2,124,30]{1,2,0:T(8,128)S(1)}, u32[]{:S(2)}, u32[]{:S(2)}) collective-permute-start(f32[2,124,30]{1,2,0:T(8,128)S(1)} %get-tuple-element.93), channel_id=1, source_target_pairs={{1,0},{3,2},{5,4},{7,6},{9,8},{11,10},{13,12},{15,14},{17,16},{19,... | collective-permute-start | bytes 89288 | tf_op jit(solution)/shard_map/ppermute | solution.py:24
  39.3 1.6 %collective-permute-done.3 = f32[2,124,30]{1,2,0:T(8,128)S(1)} collective-permute-done((f32[2,124,30]{1,2,0:T(8,128)S(1)}, f32[2,124,30]{1,2,0:T(8,128)S(1)}, u32[]{:S(2)}, u32[]{:S(2)}) %collective-permute-start.3) | collective-permute-done | bytes 29792 | tf_op jit(solution)/shard_map/ppermute | solution.py:24
  40.9 1.5 %concatenate.10 = f32[2,124,1084]{1,2,0:T(8,128)S(1)} concatenate(f32[2,124,30]{1,2,0:T(8,128)S(1)} %collective-permute-done.2, f32[2,124,1024]{1,2,0:T(8,128)S(1)} %pad_maximum_fusion.1, f32[2,124,30]{1,2,0:T(8,128)S(1)} %collective-permute-done.3), dimensions={2} | concatenate | bytes 2150656 | tf_op jit(solution)/shard_map/concatenate | solution.py:25
  46.2 44.1 %while.10 = (s32[]{:T(128)}, bf16[4,16,4,1024]{3,2,1,0:T(4,128)(2,1)S(1)}, f32[4,16,1024]{2,1,0:T(8,128)S(1)}, f32[4,16,1024]{2,1,0:T(8,128)}, bf16[96,128]{1,0:...) while((s32[]{:T(128)}, ...), condition=%wide.region_4.5_spmd, body=%wide.region_2.4_spmd.sunk | while | flops 412516352 | bytes 38035576 | solution.py:143
  48.8 2.8 %copy.106 = bf16[16,8,16,1024]{3,1,2,0:T(8,128)(2,1)S(1)} copy(bf16[16,8,16,1024]{3,2,1,0:T(8,128)(2,1)S(1)} %fusion.94) | data formatting | bytes 8388608 | tf_op jit(solution)/shard_map/while
  53.5 2.4 %multiply_reduce_fusion.2 = f32[4,3,16,1024]{3,2,1,0:T(8,128)S(1)} fusion(f32[4,3,8,16,1024]{4,2,3,1,0:T(8,128)S(1)} %bitcast.209, f32[8,16,1024]{2,0,1:T(8,128)S(1)} %select_add_fusion.2), kind=kLoop, calls=%fused_computation.1.clone.1 | loop fusion | flops 2949120 | bytes 7602176 | tf_op jit(solution)/shard_map/while/body/eval_jaxpr/reduce_sum | solution.py:130
  59.8 2.8 %copy.106 = bf16[16,8,16,1024]{3,1,2,0:T(8,128)(2,1)S(1)} copy(bf16[16,8,16,1024]{3,2,1,0:T(8,128)(2,1)S(1)} %fusion.94) | data formatting | bytes 8388608 | tf_op jit(solution)/shard_map/while
  64.5 2.4 %multiply_reduce_fusion.2 = f32[4,3,16,1024]{3,2,1,0:T(8,128)S(1)} fusion(f32[4,3,8,16,1024]{4,2,3,1,0:T(8,128)S(1)} %bitcast.209, f32[8,16,1024]{2,0,1:T(8,128)S(1)} %select_add_fusion.2), kind=kLoop, calls=%fused_computation.1.clone.1 | loop fusion | flops 2949120 | bytes 7602176 | tf_op jit(solution)/shard_map/while/body/eval_jaxpr/reduce_sum | solution.py:130
  70.7 2.8 %copy.106 = bf16[16,8,16,1024]{3,1,2,0:T(8,128)(2,1)S(1)} copy(bf16[16,8,16,1024]{3,2,1,0:T(8,128)(2,1)S(1)} %fusion.94) | data formatting | bytes 8388608 | tf_op jit(solution)/shard_map/while
  75.5 2.4 %multiply_reduce_fusion.2 = f32[4,3,16,1024]{3,2,1,0:T(8,128)S(1)} fusion(f32[4,3,8,16,1024]{4,2,3,1,0:T(8,128)S(1)} %bitcast.209, f32[8,16,1024]{2,0,1:T(8,128)S(1)} %select_add_fusion.2), kind=kLoop, calls=%fused_computation.1.clone.1 | loop fusion | flops 2949120 | bytes 7602176 | tf_op jit(solution)/shard_map/while/body/eval_jaxpr/reduce_sum | solution.py:130
  81.7 2.8 %copy.106 = bf16[16,8,16,1024]{3,1,2,0:T(8,128)(2,1)S(1)} copy(bf16[16,8,16,1024]{3,2,1,0:T(8,128)(2,1)S(1)} %fusion.94) | data formatting | bytes 8388608 | tf_op jit(solution)/shard_map/while
  86.5 2.4 %multiply_reduce_fusion.2 = f32[4,3,16,1024]{3,2,1,0:T(8,128)S(1)} fusion(f32[4,3,8,16,1024]{4,2,3,1,0:T(8,128)S(1)} %bitcast.209, f32[8,16,1024]{2,0,1:T(8,128)S(1)} %select_add_fusion.2), kind=kLoop, calls=%fused_computation.1.clone.1 | loop fusion | flops 2949120 | bytes 7602176 | tf_op jit(solution)/shard_map/while/body/eval_jaxpr/reduce_sum | solution.py:130
  92.4 4.2 %collective-permute-start.11 = (bf16[2,65536]{1,0:T(2,128)(2,1)S(1)}, bf16[2,65536]{1,0:T(2,128)(2,1)S(1)}, u32[]{:S(2)}, u32[]{:S(2)}) collective-permute-start(bf16[2,65536]{1,0:T(2,128)(2,1)S(1)} %convolution_convert_fusion), channel_id=1, source_target_pairs={{0,4},{2,6},{4,8},{6,10},{8,12},{10,14},{1,5},{3,7},{5,9},{7,11},{... | collective-permute-start | bytes 786440 | tf_op jit(solution)/shard_map/ppermute | solution.py:32
  96.6 3.2 %collective-permute-start.9 = (bf16[2,65536]{1,0:T(2,128)(2,1)S(1)}, bf16[2,65536]{1,0:T(2,128)(2,1)S(1)}, u32[]{:S(2)}, u32[]{:S(2)}) collective-permute-start(bf16[2,65536]{1,0:T(2,128)(2,1)S(1)} %convolution_convert_fusion.1), channel_id=1, source_target_pairs={{0,2},{2,4},{4,6},{6,8},{8,10},{10,12},{12,14},{1,3},{3,5},{5,7},{... | collective-permute-start | bytes 786440 | tf_op jit(solution)/shard_map/ppermute | solution.py:32
  103.7 6.6 %collective-permute-done.9 = bf16[2,65536]{1,0:T(2,128)(2,1)S(1)} collective-permute-done((bf16[2,65536]{1,0:T(2,128)(2,1)S(1)}, bf16[2,65536]{1,0:T(2,128)(2,1)S(1)}, u32[]{:S(2)}, u32[]{:S(2)}) %collective-permute-start.9) | collective-permute-done | bytes 262176 | tf_op jit(solution)/shard_map/ppermute | solution.py:32
  111.2 5.6 %collective-permute-done.5 = bf16[2,65536]{1,0:T(2,128)(2,1)S(1)} collective-permute-done((bf16[2,65536]{1,0:T(2,128)(2,1)S(1)}, bf16[2,65536]{1,0:T(2,128)(2,1)S(1)}, u32[]{:S(2)}, u32[]{:S(2)}) %collective-permute-start.5) | collective-permute-done | bytes 262176 | tf_op jit(solution)/shard_map/ppermute | solution.py:32
  (143 shorter events, 48.4 us)
Async XLA Ops:
  2.9 9.8 %copy-start.5 = (s32[4,2]{0,1:T(2,128)S(1)}, s32[4,2]{0,1:T(2,128)}, u32[]{:S(2)}) copy-start(s32[4,2]{0,1:T(2,128)} %param.22) | copy-start | bytes 100
  2.9 10.6 %copy-start.6 = (s32[4,2]{0,1:T(2,128)S(1)}, s32[4,2]{0,1:T(2,128)}, u32[]{:S(2)}) copy-start(s32[4,2]{0,1:T(2,128)} %param.23) | copy-start | bytes 100
  2.9 20.4 %copy-start.4 = (f32[61]{0:T(128)S(1)}, f32[61]{0:T(128)}, u32[]{:S(2)}) copy-start(f32[61]{0:T(128)} %param.18) | copy-start | bytes 736
  3.1 21.2 %copy-start.1 = (bf16[4,8,16,8]{2,3,1,0:T(8,128)(2,1)S(1)}, bf16[4,8,16,8]{2,3,1,0:T(8,128)(2,1)}, u32[]{:S(2)}) copy-start(bf16[4,8,16,8]{2,3,1,0:T(8,128)(2,1)} %param.21) | copy-start | bytes 24580
  3.1 21.2 %copy-start.2 = (bf16[4,8,16,8]{2,3,1,0:T(8,128)(2,1)S(1)}, bf16[4,8,16,8]{2,3,1,0:T(8,128)(2,1)}, u32[]{:S(2)}) copy-start(bf16[4,8,16,8]{2,3,1,0:T(8,128)(2,1)} %param.20) | copy-start | bytes 24580
  3.1 21.2 %copy-start.3 = (bf16[4,8,16,8]{2,3,1,0:T(8,128)(2,1)S(1)}, bf16[4,8,16,8]{2,3,1,0:T(8,128)(2,1)}, u32[]{:S(2)}) copy-start(bf16[4,8,16,8]{2,3,1,0:T(8,128)(2,1)} %param.19) | copy-start | bytes 24580
  4.9 27.0 %collective-permute-start.1 = (f32[2,30,1024]{2,0,1:T(2,128)}, f32[2,30,1024]{2,0,1:T(2,128)}, u32[]{:S(2)}, u32[]{:S(2)}) collective-permute-start(f32[2,30,1024]{2,0,1:T(2,128)} %copy.55), channel_id=1, source_target_pairs={{2,0},{4,2},{6,4},{8,6},{10,8},{12,10},{14,12},{3,1},{5,3},{7,5},{... | collective-permute-start | bytes 737288 | tf_op jit(solution)/shard_map/ppermute | solution.py:24
  7.2 26.0 %collective-permute-start = (f32[2,30,1024]{2,0,1:T(2,128)}, f32[2,30,1024]{2,0,1:T(2,128)S(1)}, u32[]{:S(2)}, u32[]{:S(2)}) collective-permute-start(f32[2,30,1024]{2,0,1:T(2,128)} %copy.54), channel_id=1, source_target_pairs={{0,2},{2,4},{4,6},{6,8},{8,10},{10,12},{12,14},{1,3},{3,5},{5,7},{... | collective-permute-start | bytes 737288 | tf_op jit(solution)/shard_map/ppermute | solution.py:21
  13.6 11.6 %collective-permute-start.10 = (s32[2]{0:T(128)S(1)}, s32[2]{0:T(128)S(1)}, u32[]{:S(2)}, u32[]{:S(2)}) collective-permute-start(s32[2]{0:T(128)S(1)} %get-tuple-element.67), channel_id=1, source_target_pairs={{0,4},{2,6},{4,8},{6,10},{8,12},{10,14},{1,5},{3,7},{5,9},{7,11},{... | collective-permute-start | bytes 32 | tf_op jit(solution)/shard_map/ppermute | solution.py:32
  17.6 9.0 %collective-permute-start.8 = (s32[2]{0:T(128)S(1)}, s32[2]{0:T(128)S(1)}, u32[]{:S(2)}, u32[]{:S(2)}) collective-permute-start(s32[2]{0:T(128)S(1)} %get-tuple-element.66), channel_id=1, source_target_pairs={{0,2},{2,4},{4,6},{6,8},{8,10},{10,12},{12,14},{1,3},{3,5},{5,7},{... | collective-permute-start | bytes 32 | tf_op jit(solution)/shard_map/ppermute | solution.py:32
  21.9 5.4 %collective-permute-start.6 = (s32[2]{0:T(128)S(1)}, s32[2]{0:T(128)S(1)}, u32[]{:S(2)}, u32[]{:S(2)}) collective-permute-start(s32[2]{0:T(128)S(1)} %get-tuple-element.65), channel_id=1, source_target_pairs={{2,0},{4,2},{6,4},{8,6},{10,8},{12,10},{14,12},{3,1},{5,3},{7,5},{... | collective-permute-start | bytes 32 | tf_op jit(solution)/shard_map/ppermute | solution.py:32
  25.2 6.1 %collective-permute-start.4 = (s32[2]{0:T(128)S(1)}, s32[2]{0:T(128)S(1)}, u32[]{:S(2)}, u32[]{:S(2)}) collective-permute-start(s32[2]{0:T(128)S(1)} %get-tuple-element.64), channel_id=1, source_target_pairs={{4,0},{6,2},{8,4},{10,6},{12,8},{14,10},{5,1},{7,3},{9,5},{11,7},{... | collective-permute-start | bytes 32 | tf_op jit(solution)/shard_map/ppermute | solution.py:32
  36.4 9.8 %copy-start = (bf16[4,16,4,1024]{3,2,1,0:T(4,128)(2,1)S(1)}, bf16[4,16,4,1024]{3,2,1,0:T(4,128)(2,1)}, u32[]{:S(2)}) copy-start(bf16[4,16,4,1024]{3,2,1,0:T(4,128)(2,1)} %custom-call.1) | copy-start | bytes 1572868
  36.4 2.9 %collective-permute-start.2 = (f32[2,124,30]{1,2,0:T(8,128)S(1)}, f32[2,124,30]{1,2,0:T(8,128)S(1)}, u32[]{:S(2)}, u32[]{:S(2)}) collective-permute-start(f32[2,124,30]{1,2,0:T(8,128)S(1)} %get-tuple-element.94), channel_id=1, source_target_pairs={{0,1},{2,3},{4,5},{6,7},{8,9},{10,11},{12,13},{14,15},{16,17},{18,... | collective-permute-start | bytes 89288 | tf_op jit(solution)/shard_map/ppermute | solution.py:21
  37.8 3.1 %collective-permute-start.3 = (f32[2,124,30]{1,2,0:T(8,128)S(1)}, f32[2,124,30]{1,2,0:T(8,128)S(1)}, u32[]{:S(2)}, u32[]{:S(2)}) collective-permute-start(f32[2,124,30]{1,2,0:T(8,128)S(1)} %get-tuple-element.93), channel_id=1, source_target_pairs={{1,0},{3,2},{5,4},{7,6},{9,8},{11,10},{13,12},{15,14},{17,16},{19,... | collective-permute-start | bytes 89288 | tf_op jit(solution)/shard_map/ppermute | solution.py:24
  92.4 10.8 %collective-permute-start.11 = (bf16[2,65536]{1,0:T(2,128)(2,1)S(1)}, bf16[2,65536]{1,0:T(2,128)(2,1)S(1)}, u32[]{:S(2)}, u32[]{:S(2)}) collective-permute-start(bf16[2,65536]{1,0:T(2,128)(2,1)S(1)} %convolution_convert_fusion), channel_id=1, source_target_pairs={{0,4},{2,6},{4,8},{6,10},{8,12},{10,14},{1,5},{3,7},{5,9},{7,11},{... | collective-permute-start | bytes 786440 | tf_op jit(solution)/shard_map/ppermute | solution.py:32
  96.6 13.7 %collective-permute-start.9 = (bf16[2,65536]{1,0:T(2,128)(2,1)S(1)}, bf16[2,65536]{1,0:T(2,128)(2,1)S(1)}, u32[]{:S(2)}, u32[]{:S(2)}) collective-permute-start(bf16[2,65536]{1,0:T(2,128)(2,1)S(1)} %convolution_convert_fusion.1), channel_id=1, source_target_pairs={{0,2},{2,4},{4,6},{6,8},{8,10},{10,12},{12,14},{1,3},{3,5},{5,7},{... | collective-permute-start | bytes 786440 | tf_op jit(solution)/shard_map/ppermute | solution.py:32
  99.8 10.9 %collective-permute-start.7 = (bf16[2,65536]{1,0:T(2,128)(2,1)S(1)}, bf16[2,65536]{1,0:T(2,128)(2,1)S(1)}, u32[]{:S(2)}, u32[]{:S(2)}) collective-permute-start(bf16[2,65536]{1,0:T(2,128)(2,1)S(1)} %convolution_convert_fusion.2), channel_id=1, source_target_pairs={{2,0},{4,2},{6,4},{8,6},{10,8},{12,10},{14,12},{3,1},{5,3},{7,5},{... | collective-permute-start | bytes 786440 | tf_op jit(solution)/shard_map/ppermute | solution.py:32
  102.0 14.8 %collective-permute-start.5 = (bf16[2,65536]{1,0:T(2,128)(2,1)S(1)}, bf16[2,65536]{1,0:T(2,128)(2,1)S(1)}, u32[]{:S(2)}, u32[]{:S(2)}) collective-permute-start(bf16[2,65536]{1,0:T(2,128)(2,1)S(1)} %convolution_convert_fusion.3), channel_id=1, source_target_pairs={{4,0},{6,2},{8,4},{10,6},{12,8},{14,10},{5,1},{7,3},{9,5},{11,7},{... | collective-permute-start | bytes 786440 | tf_op jit(solution)/shard_map/ppermute | solution.py:32
where the time goes:
time: 119 us; the launch traced here: 118 us
  starting transfers between devices  30.5 us (26%)
  local copies, waits for them, and re-layouts  28.7 us (24%)
  other arithmetic  28.3 us (24%)
  waiting for transfers between devices  18.4 us (15%)
  matrix products  11.3 us (9%)
    ppermute x8, starting transfers between devices, from_behind(): lax.ppermute(value, axis, [(source, source + steps) for source in range(i...  20.8 us
    ppermute x8, waiting for transfers between devices, from_behind(): lax.ppermute(value, axis, [(source, source + steps) for source in range(i...  16.8 us
    while x4, local copies, waits for them, and re-layouts  11 us
    reduce_sum x4, other arithmetic, correct_block(): coefficient = jnp.sum(node_values * weight_e[None, None], axis=2)  9.71 us
    ppermute x2, starting transfers between devices, with_halo(): lax.ppermute(lax.slice_in_dim(block, block.shape[dim] - width, None, axis...  6.93 us
    while x4, other arithmetic  4.29 us
    dot_general x4, matrix products, correct_block(): jnp.dot(lut_table, joint_weight, preferred_element_type=jnp.float32)  3.92 us
    dynamic_slice x4, local copies, waits for them, and re-layouts, body(): lax.map(correct_block, inputs).reshape(row_count, band_count, col_count)  3.83 us
  transfers between devices with their start and end apart: 12, of which 5 were waited for; matrix products, arithmetic and copies ran while one was open for 7% of the time, Pallas kernels for 0%

commit v1 on v0

v1 whole, which is shorter than its diff:
```python
import functools

import jax
import jax.numpy as jnp
from jax import lax
from jax.experimental import pallas as pl
from jax.experimental.pallas import tpu as pltpu
from jax.sharding import PartitionSpec as P

SEG = 16
CAP = 2
LANES = 128

F32 = jnp.float32
BF16 = jnp.bfloat16
VMEM = pl.BlockSpec(memory_space=pltpu.VMEM)
SMEM = pl.BlockSpec(memory_space=pltpu.SMEM)


def params(mib=32):
    return pltpu.CompilerParams(vmem_limit_bytes=mib * 1024 * 1024)


def swap_pairs(count, step, offset):
    pairs = []
    for i in range(count - step):
        if (i // step) % 2 == offset:
            pairs += [(i, i + step), (i + step, i)]
    return pairs


def split_bf16(x):
    high = x.astype(BF16)
    return high, (x - high.astype(F32)).astype(BF16)


def prep_kernel(meta_ref, toa_ref, dark_ref, near_ref, far_ref):
    half = toa_ref.shape[0] // 2
    even = meta_ref[0] == 0
    for field, band in ((0, 0), (1, 2)):
        lines = toa_ref[:, band, :].astype(F32) * dark_ref[...].astype(F32)
        lines = lines.astype(BF16)
        upper, lower = lines[:half], lines[half:]
        near_ref[field] = jnp.where(even, lower, upper)
        far_ref[field] = jnp.where(even, upper, lower)


def bands_kernel(taps_ref, rows_ref, cols_ref):
    taps = taps_ref[...]
    for out_ref, first in ((rows_ref, rows_ref.shape[1] // 2 - 30), (cols_ref, LANES - 30)):
        depth, width = out_ref.shape[1], out_ref.shape[2]
        base = taps
        if width > LANES:
            base = jnp.concatenate([taps, jnp.zeros((1, width - LANES), F32)], axis=1)
        base = jnp.broadcast_to(base, (8, width))
        base = pltpu.roll(base, 0, 1, stride=1, stride_axis=0)
        for at in range(0, depth, 16):
            pair = [pltpu.roll(base, first + at + 8 * k, 1) for k in range(2)]
            high, low = split_bf16(jnp.concatenate(pair, axis=0))
            out_ref[0, at : at + 16] = high
            out_ref[1, at : at + 16] = low


def vertical_kernel(meta_ref, bands_ref, near_ref, far_ref, near_in_ref, far_in_ref, out_ref, edge_ref):
    even = meta_ref[0] == 0
    left = meta_ref[1] == 0
    size = bands_ref.shape[1]
    matrix = jnp.concatenate([bands_ref[0], bands_ref[1]], axis=0)

    def field(index):
        near, far = near_ref[index], far_ref[index]
        near_in, far_in = near_in_ref[index], far_in_ref[index]
        return jnp.concatenate(
            [
                jnp.where(even, far_in, near_in),
                jnp.where(even, far, near),
                jnp.where(even, near, far),
                jnp.where(even, near_in, far_in),
            ],
            axis=0,
        )

    def along_rows(block):
        both = jnp.dot(matrix, block, preferred_element_type=F32)
        return both[:size] + both[size:]

    blue, red = field(0), field(1)
    dark = jnp.where(blue.astype(F32) > 0.0, 1.0, 0.0).astype(BF16)
    weighted = 8.0 * (along_rows(blue) - 0.5 * along_rows(red))
    darkness = along_rows(dark)
    for index, value in ((0, weighted), (1, darkness)):
        out_ref[index] = value
        edge_ref[index] = jnp.where(left, value[:, -LANES:], value[:, :LANES])


def correct_kernel(
    meta_ref,
    bands_ref,
    lut_ref,
    vert_ref,
    edge_ref,
    toa_ref,
    vapour_ref,
    class_ref,
    frac_ref,
    corr_ref,
    side0_ref,
    side1_ref,
    side2_ref,
    side3_ref,
    ext_ref,
    pos_ref,
    hat_ref,
    even_ref,
):
    rows, cols = vapour_ref.shape
    left = meta_ref[1] == 0
    levels_w = hat_ref.shape[0]
    levels_a = lut_ref.shape[1] // levels_w
    block = bands_ref.shape[1]
    window = bands_ref.shape[2]
    for index in range(2):
        edge = edge_ref[index]
        zero = jnp.zeros_like(edge)
        pieces = jnp.concatenate([jnp.where(left, zero, edge), vert_ref[index], jnp.where(left, edge, zero)], axis=1)
        high, low = split_bf16(pieces)
        ext_ref[index * rows : (index + 1) * rows, :] = high
        ext_ref[(2 + index) * rows : (3 + index) * rows, :] = low
    contract = (((1,), (1,)), ((), ()))
    for number in range(cols // block):
        at = slice(number * block, (number + 1) * block)
        part = ext_ref[:, number * block : number * block + window]
        full = lax.dot_general(part, bands_ref[0], contract, preferred_element_type=F32)
        rest = lax.dot_general(part[: 2 * rows], bands_ref[1], contract, preferred_element_type=F32)
        weighted = full[:rows] + full[2 * rows : 3 * rows] + rest[:rows]
        darkness = full[rows : 2 * rows] + full[3 * rows :] + rest[rows:]
        aerosol = weighted / jnp.maximum(darkness, 1.0)
        pos_ref[:, at] = (levels_a - 1.0) / (1.0 + jnp.exp(-aerosol))
    vapour = vapour_ref[...]
    for w in range(levels_w):
        hat_ref[w] = jnp.maximum(0.0, 1.0 - jnp.abs(vapour - float(w)))
    frac = frac_ref[...]
    even_ref[...] = jnp.where(class_ref[...] % 2 == 0, 1.0 - frac, frac)

    step = 256
    node_a = lax.broadcasted_iota(jnp.int32, (levels_a, step), 0).astype(F32)
    sublane = lax.broadcasted_iota(jnp.int32, (8, step), 0)
    upper = sublane >= 4
    shift = jnp.where(upper, 1, 0)
    lut = lut_ref[...]

    def row_step(row, carry):
        for number in range(cols // step):
            at = slice(number * step, (number + 1) * step)
            one = pl.ds(row, 1)
            pos = pos_ref[one, at]
            hat_a = jnp.maximum(0.0, 1.0 - jnp.abs(pos - node_a))
            joint = jnp.concatenate(
                [(hat_a * hat_ref[w, one, at]).astype(BF16) for w in range(levels_w)], axis=0
            )
            nodes = jnp.dot(lut, joint, preferred_element_type=F32)
            node = [nodes[8 * k : 8 * k + 8] for k in range(12)]
            level = jnp.broadcast_to(class_ref[one, at], (8, step))
            w_even = jnp.broadcast_to(even_ref[one, at], (8, step))
            w_odd = 1.0 - w_even
            even = jnp.where(level < 3, jnp.where(level < 1, node[0], node[2]), jnp.where(level < 5, node[4], node[6]))
            odd = jnp.where(level < 4, jnp.where(level < 2, node[1], node[3]), jnp.where(level < 6, node[5], node[7]))
            linear = w_even * even + w_odd * odd
            low = level - shift
            mixed = jnp.where(low < 3, jnp.where(low < 1, node[8], node[9]), jnp.where(low < 5, node[10], node[11]))
            mixed = mixed * jnp.where(upper, w_odd, w_even)
            albedo = mixed[:4] + mixed[4:]
            scaled = linear[:4] * toa_ref[row, :, at].astype(F32) - linear[4:]
            surface = scaled / (1.0 + albedo * scaled)
            corr_ref[row, :, at] = surface.astype(BF16)
        return carry

    lax.fori_loop(0, rows, row_step, 0)

    segments = rows // SEG
    band = lax.broadcasted_iota(jnp.int32, corr_ref.shape[1:], 0)
    for side, out_ref in enumerate((side0_ref, side1_ref, side2_ref, side3_ref)):
        target = meta_ref[2 + side]
        tags = jnp.zeros(corr_ref.shape[1:], F32)
        count = jnp.int32(0)
        for segment in range(segments):
            hit = meta_ref[6 + segment] == target
            slot = count

            @pl.when(hit)
            def _():
                out_ref[pl.ds(slot * SEG, SEG)] = corr_ref[segment * SEG : (segment + 1) * SEG]

            tag = jnp.where(hit, meta_ref[6 + 2 * segments + segment] + 1, 0).astype(F32)
            tags = tags + jnp.where(band == slot, tag, 0.0)
            count = count + hit.astype(jnp.int32)
        out_ref[CAP * SEG] = tags.astype(BF16)


def own_kernel(meta_ref, corr_ref, acc_ref):
    rows = corr_ref.shape[0]
    segments = rows // SEG
    acc_ref[...] = jnp.zeros(acc_ref.shape, F32)
    for segment in range(segments):
        start = meta_ref[6 + segments + segment]
        at = pl.ds(start, SEG)
        acc_ref[at] = acc_ref[at] + corr_ref[segment * SEG : (segment + 1) * SEG].astype(F32)


def combine_kernel(meta_ref, acc_in_ref, side0_ref, side1_ref, side2_ref, side3_ref, out_ref, acc_ref, inv_ref):
    rows = acc_ref.shape[0]
    segments = rows // SEG
    line = lax.broadcasted_iota(jnp.int32, (rows, LANES), 0)

    def covers(start):
        return jnp.where((line >= start) & (line < start + SEG), 1.0, 0.0)

    count = jnp.zeros((rows, LANES), F32)
    for segment in range(segments):
        count = count + covers(meta_ref[6 + segments + segment])
    acc_ref[...] = acc_in_ref[...]
    for side_ref in (side0_ref, side1_ref, side2_ref, side3_ref):
        tags = side_ref[CAP * SEG, :, :LANES].astype(F32)
        band = lax.broadcasted_iota(jnp.int32, tags.shape, 0)
        for slot in range(CAP):
            tag = jnp.max(jnp.where(band == slot, tags, 0.0)).astype(jnp.int32)
            start = jnp.maximum(tag - 1, 0)
            count = count + jnp.where(tag > 0, covers(start), 0.0)

            @pl.when(tag > 0)
            def _():
                at = pl.ds(start, SEG)
                acc_ref[at] = acc_ref[at] + side_ref[slot * SEG : (slot + 1) * SEG].astype(F32)

    inv_ref[...] = 1.0 / jnp.maximum(count, 1.0)
    repeat = out_ref.shape[2] // LANES
    for row in range(rows):
        inverse = jnp.broadcast_to(inv_ref[row : row + 1, :], (out_ref.shape[1], LANES))
        inverse = jnp.concatenate([inverse] * repeat, axis=1)
        out_ref[row] = (acc_ref[row] * inverse).astype(BF16)


def body(
    toa_bands,
    dark_mask,
    vapour,
    elev_class,
    elev_frac,
    kernel,
    lut_gain,
    lut_path,
    lut_albedo,
    routes,
    starts,
):
    rows, bands, cols = toa_bands.shape
    levels_e, levels_a, levels_w = lut_gain.shape[1:]
    nodes = levels_a * levels_w
    count = lax.axis_size("along")
    me = lax.axis_index("along")
    core = lax.axis_index("across")
    near = 1 - 2 * (me % 2)
    far_z = 2 - 4 * ((me // 2) % 2)
    distance = routes[:, 1] - me
    meta = jnp.concatenate(
        [jnp.stack([me % 2, core, near, -near, far_z, -far_z]), distance, starts[:, 0], starts[:, 1]]
    ).astype(jnp.int32)
    half = rows // 2
    fields = jax.ShapeDtypeStruct((2, half, cols), BF16)
    near_out, far_out = pl.pallas_call(
        prep_kernel,
        out_shape=(fields, fields),
        in_specs=[SMEM, VMEM, VMEM],
        out_specs=(VMEM, VMEM),
        compiler_params=params(),
        name="prep",
    )(meta, toa_bands, dark_mask)
    near_in = lax.ppermute(near_out, "along", swap_pairs(count, 1, 0))
    far_in = lax.ppermute(far_out, "along", swap_pairs(count, 1, 1))
    taps = jnp.pad(kernel, (0, LANES - kernel.shape[0]))[None, :]
    block = 256
    row_bands, col_bands = pl.pallas_call(
        bands_kernel,
        out_shape=(
            jax.ShapeDtypeStruct((2, rows, 2 * rows), BF16),
            jax.ShapeDtypeStruct((2, block, block + 2 * LANES), BF16),
        ),
        in_specs=[VMEM],
        out_specs=(VMEM, VMEM),
        compiler_params=params(),
        name="bands",
    )(taps)
    lut_first = jnp.concatenate([lut_gain, lut_path], axis=0).transpose(1, 0, 3, 2)
    lut_last = lut_albedo.transpose(1, 0, 3, 2)
    lut = jnp.concatenate(
        [lut_first.reshape(2 * bands * levels_e, nodes), lut_last.reshape(bands * levels_e, nodes)], axis=0
    )
    vert, edge = pl.pallas_call(
        vertical_kernel,
        out_shape=(
            jax.ShapeDtypeStruct((2, rows, cols), F32),
            jax.ShapeDtypeStruct((2, rows, LANES), F32),
        ),
        in_specs=[SMEM] + [VMEM] * 5,
        out_specs=(VMEM, VMEM),
        compiler_params=params(),
        name="vertical",
    )(meta, row_bands, near_out, far_out, near_in, far_in)
    edge_in = lax.ppermute(edge, "across", swap_pairs(lax.axis_size("across"), 1, 0))
    slots = jax.ShapeDtypeStruct((CAP * SEG + 1, bands, cols), BF16)
    corr, *sides = pl.pallas_call(
        correct_kernel,
        out_shape=(jax.ShapeDtypeStruct((rows, bands, cols), BF16),) + (slots,) * 4,
        in_specs=[SMEM] + [VMEM] * 8,
        out_specs=(VMEM,) * 5,
        scratch_shapes=[
            pltpu.VMEM((4 * rows, cols + 2 * LANES), BF16),
            pltpu.VMEM((rows, cols), F32),
            pltpu.VMEM((levels_w, rows, cols), F32),
            pltpu.VMEM((rows, cols), F32),
        ],
        compiler_params=params(),
        name="correct",
    )(meta, col_bands, lut, vert, edge_in, toa_bands, vapour, elev_class, elev_frac)
    moves = ((1, 0), (1, 1), (2, 0), (2, 1))
    got = [
        lax.ppermute(side, "along", swap_pairs(count, step, offset)) for side, (step, offset) in zip(sides, moves)
    ]
    total = jax.ShapeDtypeStruct((rows, bands, cols), F32)
    acc = pl.pallas_call(
        own_kernel,
        out_shape=total,
        in_specs=[SMEM, VMEM],
        out_specs=VMEM,
        compiler_params=params(),
        name="own",
    )(meta, corr)
    out = pl.pallas_call(
        combine_kernel,
        out_shape=jax.ShapeDtypeStruct((rows, bands, cols), BF16),
        in_specs=[SMEM] + [VMEM] * 5,
        out_specs=VMEM,
        scratch_shapes=[pltpu.VMEM((rows, bands, cols), F32), pltpu.VMEM((rows, LANES), F32)],
        compiler_params=params(),
        name="combine",
    )(meta, acc, *got)
    return out[None]


def solution(mesh):
    in_specs = (
        P(("groups", "along"), None, "across"),
        P(("groups", "along"), "across"),
        P(("groups", "along"), "across"),
        P(("groups", "along"), "across"),
        P(("groups", "along"), "across"),
        P(),
        P(),
        P(),
        P(),
        P(("groups", "along"), None),
        P(("groups", "along"), None),
    )
    out_specs = P(("groups", "along"), None, None, "across")
    return jax.shard_map(body, mesh=mesh, in_specs=in_specs, out_specs=out_specs, check_vma=False)
```

time: 119 us -> 52.4 us (0.44)
  other arithmetic: 28.3 us -> 0.04 us
  local copies, waits for them, and re-layouts: 28.7 us -> 3.44 us
  Pallas kernels: 0 us -> 21.6 us
  starting transfers between devices: 30.5 us -> 13.1 us
  matrix products: 11.3 us -> 0 us
  waiting for transfers between devices: 18.4 us -> 13.8 us
    pallas_call x0 -> x6, Pallas kernels: none -> 21.6 us  [the longest x1 16.3 us: body(): pl.pallas_call(correct_kernel, out_shape=(jax.ShapeDtypeStruct((rows, ban...]
    ppermute x12 -> x7, starting transfers between devices: 30.5 us -> 13.1 us  [the longest x4 9.17 us: body(): lax.ppermute(side, 'along', swap_pairs(count, step, offset))]
    reduce_sum x12 -> x0, other arithmetic: 11.4 us -> none  [the longest x4 9.71 us: correct_block(): coefficient = jnp.sum(node_values * weight_e[None, None], axis=2)]
    dot_general x22 -> x0, matrix products: 11.3 us -> none  [the longest x4 3.92 us: correct_block(): jnp.dot(lut_table, joint_weight, preferred_element_type=jnp.float32)]
    while x4 -> x0, local copies, waits for them, and re-layouts: 11 us -> none
    ppermute x12 -> x7, waiting for transfers between devices: 18.4 us -> 13.8 us  [the longest x4 10.9 us: body(): lax.ppermute(side, 'along', swap_pairs(count, step, offset))]
    while x4 -> x0, other arithmetic: 4.29 us -> none
    broadcast_in_dim x9 -> x0, other arithmetic: 4.01 us -> none  [the longest x4 3.56 us: correct_block(): jnp.where(elev_ids == class_block[None], 1.0 - frac_block[None], 0.0)]
  transfers between devices with their start and end apart: 12 -> 7, of which waited for: 5 -> 4; matrix products, arithmetic and copies ran while one was open for 7% -> 1% of each run, Pallas kernels for 0% -> 2%
where the time goes in v1:
time: 52.4 us; the launch traced here: 52.2 us
  Pallas kernels  21.6 us (41%)
  waiting for transfers between devices  13.8 us (26%)
  starting transfers between devices  13.1 us (25%)
  local copies, waits for them, and re-layouts  3.44 us (7%)
    pallas_call x1, Pallas kernels, body(): pl.pallas_call(correct_kernel, out_shape=(jax.ShapeDtypeStruct((rows, ban...  16.3 us
    ppermute x4, waiting for transfers between devices, body(): lax.ppermute(side, 'along', swap_pairs(count, step, offset))  10.9 us
    ppermute x4, starting transfers between devices, body(): lax.ppermute(side, 'along', swap_pairs(count, step, offset))  9.17 us
    unnamed x24, local copies, waits for them, and re-layouts  3.08 us
    ppermute x1, starting transfers between devices, body(): near_in = lax.ppermute(near_out, 'along', swap_pairs(count, 1, 0))  3.03 us
    pallas_call x1, Pallas kernels, body(): pl.pallas_call(combine_kernel, out_shape=jax.ShapeDtypeStruct((rows, band...  2.69 us
    ppermute x1, waiting for transfers between devices, body(): near_in = lax.ppermute(near_out, 'along', swap_pairs(count, 1, 0))  1.72 us
    ppermute x1, waiting for transfers between devices, body(): lax.ppermute(edge, 'across', swap_pairs(lax.axis_size('across'), 1, 0))  1.23 us
  transfers between devices with their start and end apart: 7, of which 4 were waited for; matrix products, arithmetic and copies ran while one was open for 1% of the time, Pallas kernels for 2%

profile of v1, /device:TPU:0, one launch (start us, length us, event | category | flops | bytes accessed | tf_op | source)
XLA Modules:
  0.0 52.2 jit_solution(5063877249559116671)
XLA Ops:
  0.0 0.7 %copy-done.10 = s32[4,2]{0,1:T(2,128)S(1)} copy-done((s32[4,2]{0,1:T(2,128)S(1)}, s32[4,2]{0,1:T(2,128)}, u32[]{:S(2)}) %copy-start.10) | copy-done | bytes 56
  0.7 0.1 concatenate.9.meta_ref
  0.8 1.0 %copy-done = bf16[64,4,1024]{2,1,0:T(4,128)(2,1)S(1)} copy-done((bf16[64,4,1024]{2,1,0:T(4,128)(2,1)S(1)}, bf16[64,4,1024]{2,1,0:T(4,128)(2,1)}, u32[]{:S(2)}) %copy-start) | copy-done | bytes 524312
  1.8 0.9 %copy-done.2 = s32[64,1024]{1,0:T(8,128)S(1)} copy-done((s32[64,1024]{1,0:T(8,128)S(1)}, s32[64,1024]{1,0:T(8,128)}, u32[]{:S(2)}) %copy-start.2) | copy-done | bytes 262168
  2.8 0.9 %prep.1 = (bf16[2,32,1024]{2,1,0:T(8,128)(2,1)S(1)}, bf16[2,32,1024]{2,1,0:T(8,128)(2,1)S(1)}) custom-call(s32[18]{0:T(128)S(1)} %concatenate.9.meta_ref, bf16[64,4,1024]{2,1,0:T(4,128)(2,1)S(1)} %copy-done, s32[64,1024]{1,0:T(8,128)S(1)} %copy-done.2), custom_call_target="tpu_custom_call" | custom-call | tf_op jit(solution)/shard_map/prep/pallas_call | solution.py:270
  3.7 3.0 %collective-permute-start = (bf16[2,32,1024]{2,1,0:T(8,128)(2,1)S(1)}, bf16[2,32,1024]{2,1,0:T(8,128)(2,1)S(1)}, u32[]{:S(2)}, u32[]{:S(2)}) collective-permute-start(bf16[2,32,1024]{2,1,0:T(8,128)(2,1)S(1)} %get-tuple-element.18.near_ref), channel_id=1, source_target_pairs={{0,2},{2,0},{4,6},{6,4},{8,10},{10,8},{12,14},{14,12},{1,3},{3,1},... | collective-permute-start | bytes 393224 | tf_op jit(solution)/shard_map/ppermute | solution.py:278
  6.7 0.8 %collective-permute-start.1 = (bf16[2,32,1024]{2,1,0:T(8,128)(2,1)S(1)}, bf16[2,32,1024]{2,1,0:T(8,128)(2,1)S(1)}, u32[]{:S(2)}, u32[]{:S(2)}) collective-permute-start(bf16[2,32,1024]{2,1,0:T(8,128)(2,1)S(1)} %get-tuple-element.19.far_ref), channel_id=1, source_target_pairs={{2,4},{4,2},{6,8},{8,6},{10,12},{12,10},{3,5},{5,3},{7,9},{9,7},{1... | collective-permute-start | bytes 393224 | tf_op jit(solution)/shard_map/ppermute | solution.py:279
  7.6 0.1 reshape.9
  7.8 0.1 reshape.8
  7.9 0.3 copy-done.11
  8.2 0.2 bands.1
  8.5 1.7 %collective-permute-done.near_in_ref = bf16[2,32,1024]{2,1,0:T(8,128)(2,1)S(1)} collective-permute-done((bf16[2,32,1024]{2,1,0:T(8,128)(2,1)S(1)}, bf16[2,32,1024]{2,1,0:T(8,128)(2,1)S(1)}, u32[]{:S(2)}, u32[]{:S(2)}) %collective-permute-start) | collective-permute-done | bytes 131104 | tf_op jit(solution)/shard_map/ppermute | solution.py:278
  10.2 0.9 %vertical.1 = (f32[2,64,1024]{2,1,0:T(8,128)S(1)}, f32[2,64,128]{2,1,0:T(8,128)S(1)}) custom-call(s32[18]{0:T(128)S(1)} %concatenate.9.meta_ref, bf16[2,64,128]{2,1,0:T(8,128)(2,1)S(1)} %get-tuple-element.17.bands_ref, bf16[2,32,1024]{2,1,0:T(8,128)(2,1)S(1)} %get-tuple-element.18.near_ref, bf16[2,32,1024]{2,1,0:T(8,128)(2,1)S(1)} %get-tuple-element.19.far_ref, ...), custom_call_target="tpu_custom_call" | custom-call | tf_op jit(solution)/shard_map/vertical/pallas_call | solution.py:298
  11.1 0.1 collective-permute-start.2
  11.2 1.2 %collective-permute-done.2.edge_ref = f32[2,64,128]{2,1,0:T(8,128)S(1)} collective-permute-done((f32[2,64,128]{2,1,0:T(8,128)S(1)}, f32[2,64,128]{2,1,0:T(8,128)S(1)}, u32[]{:S(2)}, u32[]{:S(2)}) %collective-permute-start.2) | collective-permute-done | bytes 65568 | tf_op jit(solution)/shard_map/ppermute | solution.py:309
  12.4 16.3 %correct.1 = (bf16[64,4,1024]{2,1,0:T(4,128)(2,1)S(1)}, bf16[33,4,1024]{2,1,0:T(4,128)(2,1)S(1)}, bf16[33,4,1024]{2,1,0:T(4,128)(2,1)S(1)}, bf16[33,4,1024]{2,1,0:T(4,128)(2,1)S(1)}, bf16[33,4,1024]{2,1,0:T(4,128)(2,1)S(1)}) custom-call(s32[18]{0:T(128)S(1)} %concatenate.9.meta_ref, bf16[2,256,512]{2,1,0:T(8,128)(2,1)S(1)} %get-tuple-element.16.bands_ref, ...), custom_call_target="tpu_custom_call" | custom-call | tf_op jit(solution)/shard_map/correct/pallas_call | solution.py:311
  28.7 4.8 %collective-permute-start.3 = (bf16[33,4,1024]{2,1,0:T(4,128)(2,1)S(1)}, bf16[33,4,1024]{2,1,0:T(4,128)(2,1)S(1)}, u32[]{:S(2)}, u32[]{:S(2)}) collective-permute-start(bf16[33,4,1024]{2,1,0:T(4,128)(2,1)S(1)} %get-tuple-element.23), channel_id=1, source_target_pairs={{0,2},{2,0},{4,6},{6,4},{8,10},{10,8},{12,14},{14,12},{1,3},{3,1},... | collective-permute-start | bytes 811016 | tf_op jit(solution)/shard_map/ppermute | solution.py:327
  33.6 0.7 %collective-permute-start.4 = (bf16[33,4,1024]{2,1,0:T(4,128)(2,1)S(1)}, bf16[33,4,1024]{2,1,0:T(4,128)(2,1)S(1)}, u32[]{:S(2)}, u32[]{:S(2)}) collective-permute-start(bf16[33,4,1024]{2,1,0:T(4,128)(2,1)S(1)} %get-tuple-element.24), channel_id=1, source_target_pairs={{2,4},{4,2},{6,8},{8,6},{10,12},{12,10},{3,5},{5,3},{7,9},{9,7},{1... | collective-permute-start | bytes 811016 | tf_op jit(solution)/shard_map/ppermute | solution.py:327
  34.2 3.0 %collective-permute-start.5 = (bf16[33,4,1024]{2,1,0:T(4,128)(2,1)S(1)}, bf16[33,4,1024]{2,1,0:T(4,128)(2,1)S(1)}, u32[]{:S(2)}, u32[]{:S(2)}) collective-permute-start(bf16[33,4,1024]{2,1,0:T(4,128)(2,1)S(1)} %get-tuple-element.25), channel_id=1, source_target_pairs={{0,4},{4,0},{2,6},{6,2},{8,12},{12,8},{10,14},{14,10},{1,5},{5,1},... | collective-permute-start | bytes 811016 | tf_op jit(solution)/shard_map/ppermute | solution.py:327
  37.2 0.7 %collective-permute-start.6 = (bf16[33,4,1024]{2,1,0:T(4,128)(2,1)S(1)}, bf16[33,4,1024]{2,1,0:T(4,128)(2,1)S(1)}, u32[]{:S(2)}, u32[]{:S(2)}) collective-permute-start(bf16[33,4,1024]{2,1,0:T(4,128)(2,1)S(1)} %get-tuple-element.26), channel_id=1, source_target_pairs={{4,8},{8,4},{6,10},{10,6},{5,9},{9,5},{7,11},{11,7},{20,24},{24,20... | collective-permute-start | bytes 811016 | tf_op jit(solution)/shard_map/ppermute | solution.py:327
  37.9 0.7 %own.1.acc_in_ref = f32[64,4,1024]{2,1,0:T(4,128)S(1)} custom-call(s32[18]{0:T(128)S(1)} %concatenate.9.meta_ref, bf16[64,4,1024]{2,1,0:T(4,128)(2,1)S(1)} %get-tuple-element.22.corr_ref), custom_call_target="tpu_custom_call" | custom-call | tf_op jit(solution)/shard_map/own/pallas_call | solution.py:330
  38.6 6.8 %collective-permute-done.3.side0_ref = bf16[33,4,1024]{2,1,0:T(4,128)(2,1)S(1)} collective-permute-done((bf16[33,4,1024]{2,1,0:T(4,128)(2,1)S(1)}, bf16[33,4,1024]{2,1,0:T(4,128)(2,1)S(1)}, u32[]{:S(2)}, u32[]{:S(2)}) %collective-permute-start.3) | collective-permute-done | bytes 270368 | tf_op jit(solution)/shard_map/ppermute | solution.py:327
  45.4 4.1 %collective-permute-done.5.side2_ref = bf16[33,4,1024]{2,1,0:T(4,128)(2,1)S(1)} collective-permute-done((bf16[33,4,1024]{2,1,0:T(4,128)(2,1)S(1)}, bf16[33,4,1024]{2,1,0:T(4,128)(2,1)S(1)}, u32[]{:S(2)}, u32[]{:S(2)}) %collective-permute-start.5) | collective-permute-done | bytes 270368 | tf_op jit(solution)/shard_map/ppermute | solution.py:327
  49.5 2.7 %combine.1 = bf16[64,4,1024]{2,1,0:T(4,128)(2,1)} custom-call(s32[18]{0:T(128)S(1)} %concatenate.9.meta_ref, f32[64,4,1024]{2,1,0:T(4,128)S(1)} %own.1.acc_in_ref, bf16[33,4,1024]{2,1,0:T(4,128)(2,1)S(1)} %collective-permute-done.3.side0_ref, bf16[33,4,1024]{2,1,0:T(4,128)(2,1)S(1)} %collective-permute-done.4.side1_ref, ...), custom_call_target="tpu_custom_call" | custom-call | tf_op jit(solution)/shard_map/combine/pallas_call | solution.py:338
  (29 shorter events, 0.1 us)
Async XLA Ops:
  0.0 0.7 %copy-start.10 = (s32[4,2]{0,1:T(2,128)S(1)}, s32[4,2]{0,1:T(2,128)}, u32[]{:S(2)}) copy-start(s32[4,2]{0,1:T(2,128)} %param.20) | copy-start | bytes 100
  0.0 0.7 %copy-start.9 = (s32[4,2]{0,1:T(2,128)S(1)}, s32[4,2]{0,1:T(2,128)}, u32[]{:S(2)}) copy-start(s32[4,2]{0,1:T(2,128)} %param.21) | copy-start | bytes 100
  0.8 1.1 %copy-start = (bf16[64,4,1024]{2,1,0:T(4,128)(2,1)S(1)}, bf16[64,4,1024]{2,1,0:T(4,128)(2,1)}, u32[]{:S(2)}) copy-start(bf16[64,4,1024]{2,1,0:T(4,128)(2,1)} %toa_ref.3) | copy-start | bytes 1572868
  1.8 0.9 %copy-start.2 = (s32[64,1024]{1,0:T(8,128)S(1)}, s32[64,1024]{1,0:T(8,128)}, u32[]{:S(2)}) copy-start(s32[64,1024]{1,0:T(8,128)} %dark_ref.1) | copy-start | bytes 786436
  2.8 4.7 %copy-start.7 = (bf16[4,8,16,8]{2,3,1,0:T(8,128)(2,1)S(1)}, bf16[4,8,16,8]{2,3,1,0:T(8,128)(2,1)}, u32[]{:S(2)}) copy-start(bf16[4,8,16,8]{2,3,1,0:T(8,128)(2,1)} %param.18) | copy-start | bytes 24580
  2.8 4.7 %copy-start.8 = (bf16[4,8,16,8]{2,3,1,0:T(8,128)(2,1)S(1)}, bf16[4,8,16,8]{2,3,1,0:T(8,128)(2,1)}, u32[]{:S(2)}) copy-start(bf16[4,8,16,8]{2,3,1,0:T(8,128)(2,1)} %param.17) | copy-start | bytes 24580
  3.7 6.5 %collective-permute-start = (bf16[2,32,1024]{2,1,0:T(8,128)(2,1)S(1)}, bf16[2,32,1024]{2,1,0:T(8,128)(2,1)S(1)}, u32[]{:S(2)}, u32[]{:S(2)}) collective-permute-start(bf16[2,32,1024]{2,1,0:T(8,128)(2,1)S(1)} %get-tuple-element.18.near_ref), channel_id=1, source_target_pairs={{0,2},{2,0},{4,6},{6,4},{8,10},{10,8},{12,14},{14,12},{1,3},{3,1},... | collective-permute-start | bytes 393224 | tf_op jit(solution)/shard_map/ppermute | solution.py:278
  6.7 0.9 %copy-start.6 = (bf16[4,8,16,8]{2,3,1,0:T(8,128)(2,1)S(1)}, bf16[4,8,16,8]{2,3,1,0:T(8,128)(2,1)}, u32[]{:S(2)}) copy-start(bf16[4,8,16,8]{2,3,1,0:T(8,128)(2,1)} %param.19) | copy-start | bytes 24580
  6.7 3.5 %collective-permute-start.1 = (bf16[2,32,1024]{2,1,0:T(8,128)(2,1)S(1)}, bf16[2,32,1024]{2,1,0:T(8,128)(2,1)S(1)}, u32[]{:S(2)}, u32[]{:S(2)}) collective-permute-start(bf16[2,32,1024]{2,1,0:T(8,128)(2,1)S(1)} %get-tuple-element.19.far_ref), channel_id=1, source_target_pairs={{2,4},{4,2},{6,8},{8,6},{10,12},{12,10},{3,5},{5,3},{7,9},{9,7},{1... | collective-permute-start | bytes 393224 | tf_op jit(solution)/shard_map/ppermute | solution.py:279
  7.5 4.9 %copy-start.5 = (f32[64,1024]{1,0:T(8,128)S(1)}, f32[64,1024]{1,0:T(8,128)}, u32[]{:S(2)}) copy-start(f32[64,1024]{1,0:T(8,128)} %frac_ref.1) | copy-start | bytes 786436
  7.6 0.7 %copy-start.11 = (f32[61]{0:T(128)S(1)}, f32[61]{0:T(128)}, u32[]{:S(2)}) copy-start(f32[61]{0:T(128)} %param.16) | copy-start | bytes 736
  7.6 4.8 %copy-start.4 = (s32[64,1024]{1,0:T(8,128)S(1)}, s32[64,1024]{1,0:T(8,128)}, u32[]{:S(2)}) copy-start(s32[64,1024]{1,0:T(8,128)} %class_ref.1) | copy-start | bytes 786436
  7.7 4.7 %copy-start.1 = (bf16[64,4,1024]{2,1,0:T(4,128)(2,1)S(1)}, bf16[64,4,1024]{2,1,0:T(4,128)(2,1)}, u32[]{:S(2)}) copy-start(bf16[64,4,1024]{2,1,0:T(4,128)(2,1)} %toa_ref.3) | copy-start | bytes 1572868
  10.2 2.2 %copy-start.3 = (f32[64,1024]{1,0:T(8,128)S(1)}, f32[64,1024]{1,0:T(8,128)}, u32[]{:S(2)}) copy-start(f32[64,1024]{1,0:T(8,128)} %vapour_ref.1) | copy-start | bytes 786436
  11.1 1.3 %collective-permute-start.2 = (f32[2,64,128]{2,1,0:T(8,128)S(1)}, f32[2,64,128]{2,1,0:T(8,128)S(1)}, u32[]{:S(2)}, u32[]{:S(2)}) collective-permute-start(f32[2,64,128]{2,1,0:T(8,128)S(1)} %get-tuple-element.21), channel_id=1, source_target_pairs={{0,1},{1,0},{2,3},{3,2},{4,5},{5,4},{6,7},{7,6},{8,9},{9,8},{10,11... | collective-permute-start | bytes 196616 | tf_op jit(solution)/shard_map/ppermute | solution.py:309
  28.7 16.7 %collective-permute-start.3 = (bf16[33,4,1024]{2,1,0:T(4,128)(2,1)S(1)}, bf16[33,4,1024]{2,1,0:T(4,128)(2,1)S(1)}, u32[]{:S(2)}, u32[]{:S(2)}) collective-permute-start(bf16[33,4,1024]{2,1,0:T(4,128)(2,1)S(1)} %get-tuple-element.23), channel_id=1, source_target_pairs={{0,2},{2,0},{4,6},{6,4},{8,10},{10,8},{12,14},{14,12},{1,3},{3,1},... | collective-permute-start | bytes 811016 | tf_op jit(solution)/shard_map/ppermute | solution.py:327
  33.6 11.9 %collective-permute-start.4 = (bf16[33,4,1024]{2,1,0:T(4,128)(2,1)S(1)}, bf16[33,4,1024]{2,1,0:T(4,128)(2,1)S(1)}, u32[]{:S(2)}, u32[]{:S(2)}) collective-permute-start(bf16[33,4,1024]{2,1,0:T(4,128)(2,1)S(1)} %get-tuple-element.24), channel_id=1, source_target_pairs={{2,4},{4,2},{6,8},{8,6},{10,12},{12,10},{3,5},{5,3},{7,9},{9,7},{1... | collective-permute-start | bytes 811016 | tf_op jit(solution)/shard_map/ppermute | solution.py:327
  34.2 15.3 %collective-permute-start.5 = (bf16[33,4,1024]{2,1,0:T(4,128)(2,1)S(1)}, bf16[33,4,1024]{2,1,0:T(4,128)(2,1)S(1)}, u32[]{:S(2)}, u32[]{:S(2)}) collective-permute-start(bf16[33,4,1024]{2,1,0:T(4,128)(2,1)S(1)} %get-tuple-element.25), channel_id=1, source_target_pairs={{0,4},{4,0},{2,6},{6,2},{8,12},{12,8},{10,14},{14,10},{1,5},{5,1},... | collective-permute-start | bytes 811016 | tf_op jit(solution)/shard_map/ppermute | solution.py:327
  37.2 12.3 %collective-permute-start.6 = (bf16[33,4,1024]{2,1,0:T(4,128)(2,1)S(1)}, bf16[33,4,1024]{2,1,0:T(4,128)(2,1)S(1)}, u32[]{:S(2)}, u32[]{:S(2)}) collective-permute-start(bf16[33,4,1024]{2,1,0:T(4,128)(2,1)S(1)} %get-tuple-element.26), channel_id=1, source_target_pairs={{4,8},{8,4},{6,10},{10,6},{5,9},{9,5},{7,11},{11,7},{20,24},{24,20... | collective-permute-start | bytes 811016 | tf_op jit(solution)/shard_map/ppermute | solution.py:327

commit v2 on v1

v2 whole, which is shorter than its diff:
```python
import functools

import jax
import jax.numpy as jnp
from jax import lax
from jax.experimental import pallas as pl
from jax.experimental.pallas import tpu as pltpu
from jax.sharding import PartitionSpec as P

SEG = 16
CAP = 2
LANES = 128

F32 = jnp.float32
BF16 = jnp.bfloat16
VMEM = pl.BlockSpec(memory_space=pltpu.VMEM)
HBM = pl.BlockSpec(memory_space=pltpu.HBM)
SMEM = pl.BlockSpec(memory_space=pltpu.SMEM)


def params(mib=32):
    return pltpu.CompilerParams(vmem_limit_bytes=mib * 1024 * 1024)


def swap_pairs(count, step, offset):
    pairs = []
    for i in range(count - step):
        if (i // step) % 2 == offset:
            pairs += [(i, i + step), (i + step, i)]
    return pairs


def split_bf16(x):
    high = x.astype(BF16)
    return high, (x - high.astype(F32)).astype(BF16)


def prep_kernel(toa_ref, dark_ref, near_ref, far_ref, toa_in, dark_in, sems):
    rows = toa_in.shape[0]
    parts = 4
    size = rows // parts
    even = lax.axis_index("along") % 2 == 0
    copies = []
    for part in range(parts):
        at = pl.ds(part * size, size)
        copies.append(
            (
                pltpu.make_async_copy(toa_ref.at[at], toa_in.at[at], sems.at[0, part]),
                pltpu.make_async_copy(dark_ref.at[at], dark_in.at[at], sems.at[1, part]),
            )
        )
        for copy in copies[-1]:
            copy.start()
    for part in range(parts):
        for copy in copies[part]:
            copy.wait()
        at = slice(part * size, (part + 1) * size)
        to = slice(part % 2 * size, (part % 2 + 1) * size)
        into_near = even if part >= 2 else jnp.logical_not(even)
        dark = dark_in[at].astype(F32)
        lines = [(toa_in[at, band, :].astype(F32) * dark).astype(BF16) for band in (0, 2)]
        for flag, out_ref in ((into_near, near_ref), (jnp.logical_not(into_near), far_ref)):

            @pl.when(flag)
            def _():
                for field in range(2):
                    out_ref[field, to] = lines[field]


def bands_kernel(taps_ref, rows_ref, cols_ref):
    taps = taps_ref[...]
    for out_ref, first in ((rows_ref, rows_ref.shape[1] - 30), (cols_ref, LANES - 30)):
        depth, width = out_ref.shape[1], out_ref.shape[2]
        base = taps
        if width > LANES:
            base = jnp.concatenate([taps, jnp.zeros((1, width - LANES), F32)], axis=1)
        base = jnp.broadcast_to(base, (8, base.shape[1]))
        base = pltpu.roll(base, 0, 1, stride=1, stride_axis=0)
        for at in range(0, depth, 16):
            pair = [pltpu.roll(base, first + at + 8 * k, 1)[:, :width] for k in range(2)]
            high, low = split_bf16(jnp.concatenate(pair, axis=0))
            out_ref[0, at : at + 16] = high
            out_ref[1, at : at + 16] = low


def is_half(flip):
    return lax.axis_index("along") % 2 == flip


def vertical_kernel(flip, bands_ref, here_ref, beside_ref, in_ref, *rest):
    ext_ref, edge_ref = rest[-2:]
    lower = is_half(flip)
    left = lax.axis_index("across") == 0
    size = bands_ref.shape[1]
    matrix = jnp.concatenate([bands_ref[0], bands_ref[1]], axis=0)

    def field(index):
        beside, incoming = beside_ref[index], in_ref[index]
        return jnp.concatenate(
            [jnp.where(lower, beside, incoming), here_ref[index], jnp.where(lower, incoming, beside)], axis=0
        )

    def smooth(block):
        both = jnp.dot(matrix, block, preferred_element_type=F32)
        return both[:size] + both[size:]

    blue, red = field(0), field(1)
    dark = jnp.where(blue.astype(F32) > 0.0, 1.0, 0.0).astype(BF16)
    for index, value in enumerate((8.0 * (smooth(blue) - 0.5 * smooth(red)), smooth(dark))):
        edge_ref[index] = jnp.where(left, value[:, -LANES:], value[:, :LANES])
        high, low = split_bf16(value)
        ext_ref[0, index] = high
        ext_ref[1, index] = low


def hats_kernel(vapour_ref, class_ref, frac_ref, *halves):
    for flip in range(2):
        hat_ref, even_ref = halves[2 * flip : 2 * flip + 2]
        rows = even_ref.shape[0]
        here = pl.ds(pl.multiple_of(jnp.where(is_half(flip), rows, 0), rows), rows)
        vapour = vapour_ref[here]
        for w in range(hat_ref.shape[0]):
            hat_ref[w] = jnp.maximum(0.0, 1.0 - jnp.abs(vapour - float(w)))
        frac = frac_ref[here]
        even_ref[...] = jnp.where(class_ref[here] % 2 == 0, 1.0 - frac, frac)


def correct_rows(
    flip,
    bands_ref,
    lut_ref,
    edge_ref,
    ext_ref,
    hat_ref,
    even_ref,
    toa_ref,
    class_ref,
    corr_ref,
    pos_ref,
):
    rows, cols = pos_ref.shape
    base = pl.multiple_of(jnp.where(is_half(flip), rows, 0), rows)
    left = lax.axis_index("across") == 0
    levels_w = hat_ref.shape[0]
    levels_a = lut_ref.shape[1] // (2 * levels_w)
    block = bands_ref.shape[1]
    window = bands_ref.shape[2]
    lines = []
    for index in range(2):
        terms = split_bf16(edge_ref[index])
        for k in range(2):
            none = jnp.zeros_like(terms[k])
            lines.append((jnp.where(left, none, terms[k]), ext_ref[k, index], jnp.where(left, terms[k], none)))
    lines = [jnp.concatenate(line, axis=1) for line in (lines[0], lines[2], lines[1], lines[3])]
    windows = [slice(number * block, number * block + window) for number in range(cols // block)]
    contract = (((1,), (1,)), ((), ()))
    every = jnp.concatenate([line[:, at] for line in lines for at in windows], axis=0)
    full = lax.dot_general(every, bands_ref[0], contract, preferred_element_type=F32)
    rest = lax.dot_general(every[: every.shape[0] // 2], bands_ref[1], contract, preferred_element_type=F32)
    pieces = len(windows)
    for number in range(pieces):
        at = slice(number * block, (number + 1) * block)

        def part(array, line):
            return array[(line * pieces + number) * rows : (line * pieces + number + 1) * rows]

        weighted = part(full, 0) + (part(full, 2) + part(rest, 0))
        darkness = part(full, 1) + (part(full, 3) + part(rest, 1))
        aerosol = weighted / jnp.maximum(darkness, 1.0)
        pos_ref[:, at] = (levels_a - 1.0) / (1.0 + jnp.exp(-aerosol))

    step = 256
    node_a = lax.broadcasted_iota(jnp.int32, (levels_a, step), 0).astype(F32)
    second = lax.broadcasted_iota(jnp.int32, (8, step), 0) >= 4
    lut = lut_ref[...]

    def pair(row, number):
        at = slice(number * step, (number + 1) * step)
        pieces = []
        for k in range(2):
            one = pl.ds(row + k, 1)
            hat_a = jnp.maximum(0.0, 1.0 - jnp.abs(pos_ref[one, at] - node_a)).astype(BF16)
            pieces += [
                hat_a * jnp.broadcast_to(hat_ref[w, one, at], (levels_a, step)).astype(BF16) for w in range(levels_w)
            ]
        nodes = jnp.dot(lut, jnp.concatenate(pieces, axis=0), preferred_element_type=F32)

        def both(ref, first):
            one, two = (jnp.broadcast_to(ref[pl.ds(first + k, 1), at], (8, step)) for k in range(2))
            return jnp.where(second, two, one)

        level = both(class_ref, base + row)
        w_even = both(even_ref, row)
        w_odd = 1.0 - w_even
        below = [level < k for k in range(7)]

        def coefficient(table):
            node = [nodes[64 * table + 8 * k : 64 * table + 8 * k + 8] for k in range(8)]
            even = jnp.where(
                below[3], jnp.where(below[1], node[0], node[2]), jnp.where(below[5], node[4], node[6])
            )
            odd = jnp.where(
                below[4], jnp.where(below[2], node[1], node[3]), jnp.where(below[6], node[5], node[7])
            )
            return w_even * even + w_odd * odd

        toa = jnp.concatenate([toa_ref[base + row + k, :, at].astype(F32) for k in range(2)], axis=0)
        scaled = coefficient(0) * toa - coefficient(1)
        surface = scaled / (1.0 + coefficient(2) * scaled)
        corr_ref[row, :, at] = surface[:4].astype(BF16)
        corr_ref[row + 1, :, at] = surface[4:].astype(BF16)

    group = 16

    def group_step(number, carry):
        for k in range(0, group, 2):
            for piece in range(cols // step):
                pair(number * group + k, piece)
        return carry

    lax.fori_loop(0, rows // group, group_step, 0)


def correct_near_kernel(*refs):
    correct_rows(0, *refs)


def segment_list(near_ref, far_ref):
    each = far_ref.shape[0] // SEG
    shift = jnp.where(is_half(0), each, 0)
    return [(shift + k, near_ref, k) for k in range(each)] + [(each - shift + k, far_ref, k) for k in range(each)]


def correct_far_kernel(meta_ref, *refs):
    near_ref, corr_ref, sides = refs[8], refs[9], refs[10:14]
    correct_rows(1, *refs[:8], corr_ref, *refs[14:])
    listed = segment_list(near_ref, corr_ref)
    segments = len(listed)
    band = lax.broadcasted_iota(jnp.int32, corr_ref.shape[1:], 0)
    for side, out_ref in enumerate(sides):
        target = meta_ref[side]
        tags = jnp.zeros(corr_ref.shape[1:], F32)
        count = jnp.int32(0)
        for segment, from_ref, place in listed:
            hit = meta_ref[4 + segment] == target
            slot = count

            @pl.when(hit)
            def _():
                out_ref[pl.ds(slot * SEG, SEG)] = from_ref[place * SEG : (place + 1) * SEG]

            tag = jnp.where(hit, meta_ref[4 + 2 * segments + segment] + 1, 0).astype(F32)
            tags = tags + jnp.where(band == slot, tag, 0.0)
            count = count + hit.astype(jnp.int32)
        out_ref[CAP * SEG] = tags.astype(BF16)


def add_rows(acc_ref, start, from_ref, place):
    for row in range(SEG):
        acc_ref[start + row] = acc_ref[start + row] + from_ref[place * SEG + row].astype(F32)


def covers(rows, start):
    line = lax.broadcasted_iota(jnp.int32, (rows, LANES), 0)
    return jnp.where((line >= start) & (line < start + SEG), 1.0, 0.0)


def read_tags(side_refs):
    found = []
    for side_ref in side_refs:
        tags = side_ref[CAP * SEG, :, :LANES].astype(F32)
        band = lax.broadcasted_iota(jnp.int32, tags.shape, 0)
        for slot in range(CAP):
            found.append((jnp.max(jnp.where(band == slot, tags, 0.0)).astype(jnp.int32), side_ref, slot))
    return found


def add_sides(acc_ref, count, side_refs):
    found = read_tags(side_refs)
    for tag, side_ref, slot in found:
        start = jnp.maximum(tag - 1, 0)
        count = count + jnp.where(tag > 0, covers(count.shape[0], start), 0.0)

        @pl.when(tag > 0)
        def _():
            add_rows(acc_ref, start, side_ref, slot)

    return count


def own_kernel(meta_ref, near_ref, far_ref, acc_ref, count_ref):
    acc_ref[...] = jnp.zeros(acc_ref.shape, F32)
    count = jnp.zeros(count_ref.shape, F32)
    listed = segment_list(near_ref, far_ref)
    for segment, from_ref, place in listed:
        start = meta_ref[4 + len(listed) + segment]
        count = count + covers(count.shape[0], start)
        add_rows(acc_ref, start, from_ref, place)
    count_ref[...] = count


def add_kernel(acc_in_ref, count_in_ref, side0_ref, side1_ref, acc_ref, count_ref):
    count_ref[...] = add_sides(acc_ref, count_in_ref[...], (side0_ref, side1_ref))


def last_kernel(acc_in_ref, count_in_ref, side0_ref, side1_ref, acc_ref, out_ref, inv_ref):
    count = add_sides(acc_ref, count_in_ref[...], (side0_ref, side1_ref))
    inv_ref[...] = 1.0 / jnp.maximum(count, 1.0)
    repeat = out_ref.shape[2] // LANES
    for row in range(out_ref.shape[0]):
        inverse = jnp.broadcast_to(inv_ref[row : row + 1, :], (out_ref.shape[1], LANES))
        inverse = jnp.concatenate([inverse] * repeat, axis=1)
        out_ref[row] = (acc_ref[row] * inverse).astype(BF16)


def body(
    toa_bands,
    dark_mask,
    vapour,
    elev_class,
    elev_frac,
    kernel,
    lut_gain,
    lut_path,
    lut_albedo,
    routes,
    starts,
):
    rows, bands, cols = toa_bands.shape
    levels_e, levels_a, levels_w = lut_gain.shape[1:]
    nodes = levels_a * levels_w
    count = lax.axis_size("along")
    me = lax.axis_index("along")
    near = 1 - 2 * (me % 2)
    far_z = 2 - 4 * ((me // 2) % 2)
    distance = routes[:, 1] - me
    meta = jnp.concatenate(
        [jnp.stack([near, -near, far_z, -far_z]), distance, starts[:, 0], starts[:, 1]]
    ).astype(jnp.int32)
    half = rows // 2
    fields = jax.ShapeDtypeStruct((2, half, cols), BF16)
    near_out, far_out = pl.pallas_call(
        prep_kernel,
        out_shape=(fields, fields),
        in_specs=[HBM, HBM],
        out_specs=(VMEM, VMEM),
        scratch_shapes=[
            pltpu.VMEM((rows, bands, cols), BF16),
            pltpu.VMEM((rows, cols), jnp.int32),
            pltpu.SemaphoreType.DMA((2, 4)),
        ],
        compiler_params=params(62),
        name="prep",
    )(toa_bands, dark_mask)
    near_in = lax.ppermute(near_out, "along", swap_pairs(count, 1, 0))
    far_in = lax.ppermute(far_out, "along", swap_pairs(count, 1, 1))
    taps = jnp.pad(kernel, (0, LANES - kernel.shape[0]))[None, :]
    block = 256
    row_bands, col_bands = pl.pallas_call(
        bands_kernel,
        out_shape=(
            jax.ShapeDtypeStruct((2, half, 3 * half), BF16),
            jax.ShapeDtypeStruct((2, block, block + 2 * LANES), BF16),
        ),
        in_specs=[VMEM],
        out_specs=(VMEM, VMEM),
        compiler_params=params(),
        name="bands",
    )(taps)
    tables = jnp.stack([lut_gain, lut_path, lut_albedo]).transpose(0, 2, 1, 4, 3)
    tables = tables.reshape(3, levels_e, bands, nodes)
    blank = jnp.zeros_like(tables)
    lut = jnp.stack(
        [jnp.concatenate([tables, blank], axis=3), jnp.concatenate([blank, tables], axis=3)], axis=2
    ).reshape(6 * levels_e * bands, 2 * nodes)

    def smooth_rows(flip, here, beside, incoming, *after):
        ext, edge = pl.pallas_call(
            functools.partial(vertical_kernel, flip),
            out_shape=(
                jax.ShapeDtypeStruct((2, 2, half, cols), BF16),
                jax.ShapeDtypeStruct((2, half, LANES), F32),
            ),
            in_specs=[VMEM] * (4 + len(after)),
            out_specs=(VMEM, VMEM),
            compiler_params=params(),
            name="vertical",
        )(row_bands, here, beside, incoming, *after)
        return lax.ppermute(edge, "across", swap_pairs(lax.axis_size("across"), 1, 0)), ext

    weights = (
        jax.ShapeDtypeStruct((levels_w, half, cols), F32),
        jax.ShapeDtypeStruct((half, cols), F32),
    )
    near_hats, near_even, far_hats, far_even = pl.pallas_call(
        hats_kernel,
        out_shape=weights * 2,
        in_specs=[VMEM] * 3,
        out_specs=(VMEM,) * 4,
        compiler_params=params(),
        name="hats",
    )(vapour, elev_class, elev_frac)
    corrected = jax.ShapeDtypeStruct((half, bands, cols), BF16)
    scratch = [pltpu.VMEM((half, cols), F32)]
    near_corr = pl.pallas_call(
        correct_near_kernel,
        out_shape=corrected,
        in_specs=[VMEM] * 8,
        out_specs=VMEM,
        scratch_shapes=scratch,
        compiler_params=params(),
        name="correct_near",
    )(col_bands, lut, *smooth_rows(0, near_out, far_out, near_in), near_hats, near_even, toa_bands, elev_class)
    far_edge, far_ext = smooth_rows(1, far_out, near_out, far_in, near_corr)
    slots = jax.ShapeDtypeStruct((CAP * SEG + 1, bands, cols), BF16)
    far_corr, *sides = pl.pallas_call(
        correct_far_kernel,
        out_shape=(corrected,) + (slots,) * 4,
        in_specs=[SMEM] + [VMEM] * 9,
        out_specs=(VMEM,) * 5,
        scratch_shapes=scratch,
        compiler_params=params(),
        name="correct_far",
    )(meta, col_bands, lut, far_edge, far_ext, far_hats, far_even, toa_bands, elev_class, near_corr)
    moves = ((1, 0), (1, 1), (2, 0), (2, 1))
    got = [
        lax.ppermute(side, "along", swap_pairs(count, step, offset)) for side, (step, offset) in zip(sides, moves)
    ]
    total = jax.ShapeDtypeStruct((rows, bands, cols), F32)
    counts = jax.ShapeDtypeStruct((rows, LANES), F32)
    acc, number = pl.pallas_call(
        own_kernel,
        out_shape=(total, counts),
        in_specs=[SMEM, VMEM, VMEM],
        out_specs=(VMEM, VMEM),
        compiler_params=params(),
        name="own",
    )(meta, near_corr, far_corr)
    acc, number = pl.pallas_call(
        add_kernel,
        out_shape=(total, counts),
        in_specs=[VMEM] * 4,
        out_specs=(VMEM, VMEM),
        input_output_aliases={0: 0, 1: 1},
        compiler_params=params(),
        name="add",
    )(acc, number, got[0], got[1])
    _, out = pl.pallas_call(
        last_kernel,
        out_shape=(total, jax.ShapeDtypeStruct((rows, bands, cols), BF16)),
        in_specs=[VMEM] * 4,
        out_specs=(VMEM, VMEM),
        scratch_shapes=[pltpu.VMEM((rows, LANES), F32)],
        input_output_aliases={0: 0},
        compiler_params=params(),
        name="last",
    )(acc, number, got[2], got[3])
    return out[None]


def solution(mesh):
    in_specs = (
        P(("groups", "along"), None, "across"),
        P(("groups", "along"), "across"),
        P(("groups", "along"), "across"),
        P(("groups", "along"), "across"),
        P(("groups", "along"), "across"),
        P(),
        P(),
        P(),
        P(),
        P(("groups", "along"), None),
        P(("groups", "along"), None),
    )
    out_specs = P(("groups", "along"), None, None, "across")
    return jax.shard_map(body, mesh=mesh, in_specs=in_specs, out_specs=out_specs, check_vma=False)
```

time: 52.4 us -> 40.2 us (0.77)
  Pallas kernels: 21.6 us -> 12.7 us
  waiting for transfers between devices: 13.8 us -> 11.4 us
  starting transfers between devices: 13.1 us -> 11.9 us
    pallas_call x6 -> x10, Pallas kernels: 21.6 us -> 12.7 us  [the longest x1 3.35 us: body(): pl.pallas_call(correct_far_kernel, out_shape=(corrected,) + (slots,) * 4,...]
    ppermute x4, starting transfers between devices: 9.17 us -> 7.33 us  [body(): lax.ppermute(side, 'along', swap_pairs(count, step, offset))]
    ppermute x1 -> x2, waiting for transfers between devices: 1.23 us -> 0.03 us  [smooth_rows(): lax.ppermute(edge, 'across', swap_pairs(lax.axis_size('across'), 1, 0))]
    ppermute x1, waiting for transfers between devices: 1.72 us -> 0.66 us  [body(): near_in = lax.ppermute(near_out, 'along', swap_pairs(count, 1, 0))]
    squeeze x0 -> x1, local copies, waits for them, and re-layouts: none -> 0.57 us  [body(): starts[:, 1]]
    unnamed x24 -> x32, local copies, waits for them, and re-layouts: 3.08 us -> 2.59 us
  transfers between devices with their start and end apart: 7 -> 8, of which waited for: 4 -> 3; matrix products, arithmetic and copies ran while one was open for 1% -> 3% of each run, Pallas kernels for 2% -> 13%
where the time goes in v2:
time: 40.2 us; the launch traced here: 39.9 us
  Pallas kernels  12.7 us (32%)
  starting transfers between devices  11.9 us (30%)
  waiting for transfers between devices  11.4 us (28%)
  local copies, waits for them, and re-layouts  3.47 us (9%)
    ppermute x4, waiting for transfers between devices, body(): lax.ppermute(side, 'along', swap_pairs(count, step, offset))  10.7 us
    ppermute x4, starting transfers between devices, body(): lax.ppermute(side, 'along', swap_pairs(count, step, offset))  7.33 us
    pallas_call x1, Pallas kernels, body(): pl.pallas_call(correct_far_kernel, out_shape=(corrected,) + (slots,) * 4,...  3.35 us
    ppermute x1, starting transfers between devices, body(): near_in = lax.ppermute(near_out, 'along', swap_pairs(count, 1, 0))  3.04 us
    pallas_call x1, Pallas kernels, body(): pl.pallas_call(correct_near_kernel, out_shape=corrected, in_specs=[VMEM]...  2.6 us
    unnamed x32, local copies, waits for them, and re-layouts  2.59 us
    pallas_call x2, Pallas kernels, smooth_rows(): pl.pallas_call(functools.partial(vertical_kernel, flip), out_shape=(jax.S...  2.1 us
    pallas_call x1, Pallas kernels, body(): pl.pallas_call(prep_kernel, out_shape=(fields, fields), in_specs=[HBM, HB...  2.05 us
  transfers between devices with their start and end apart: 8, of which 3 were waited for; matrix products, arithmetic and copies ran while one was open for 3% of the time, Pallas kernels for 13%

profile of v2, /device:TPU:0, one launch (start us, length us, event | category | flops | bytes accessed | tf_op | source)
XLA Modules:
  0.0 39.9 jit_solution(7635752214753746815)
XLA Ops:
  0.0 2.0 %prep.1 = (bf16[2,32,1024]{2,1,0:T(8,128)(2,1)}, bf16[2,32,1024]{2,1,0:T(8,128)(2,1)}) custom-call(bf16[64,4,1024]{2,1,0:T(4,128)(2,1)} %refs_6_.3, s32[64,1024]{1,0:T(8,128)} %dark_ref.1), custom_call_target="tpu_custom_call" | custom-call | tf_op jit(solution)/shard_map/prep/pallas_call | solution.py:342
  2.1 3.0 %collective-permute-start = (bf16[2,32,1024]{2,1,0:T(8,128)(2,1)}, bf16[2,32,1024]{2,1,0:T(8,128)(2,1)S(1)}, u32[]{:S(2)}, u32[]{:S(2)}) collective-permute-start(bf16[2,32,1024]{2,1,0:T(8,128)(2,1)} %get-tuple-element.29.here_ref.beside_ref), channel_id=1, source_target_pairs={{0,2},{2,0},{4,6},{6,4},{8,10},{10,8},{12,14},{14,12},{1,3},{3,1},... | collective-permute-start | bytes 393224 | tf_op jit(solution)/shard_map/ppermute | solution.py:355
  5.1 1.3 %collective-permute-start.2 = (bf16[2,32,1024]{2,1,0:T(8,128)(2,1)}, bf16[2,32,1024]{2,1,0:T(8,128)(2,1)}, u32[]{:S(2)}, u32[]{:S(2)}) collective-permute-start(bf16[2,32,1024]{2,1,0:T(8,128)(2,1)} %get-tuple-element.30.beside_ref.here_ref), channel_id=1, source_target_pairs={{2,4},{4,2},{6,8},{8,6},{10,12},{12,10},{3,5},{5,3},{7,9},{9,7},{1... | collective-permute-start | bytes 393224 | tf_op jit(solution)/shard_map/ppermute | solution.py:356
  6.4 0.6 %slice_bitcast_fusion = (s32[4]{0:T(128)}, s32[4]{0:T(128)}) fusion(s32[4,2]{0,1:T(2,128)S(1)} %copy-done.13), kind=kLoop, calls=%fused_computation.5 | loop fusion | bytes 64 | tf_op jit(solution)/shard_map/squeeze | solution.py:338
  7.3 0.6 %copy-done.15 = f32[61]{0:T(128)S(1)} copy-done((f32[61]{0:T(128)S(1)}, f32[61]{0:T(128)}, u32[]{:S(2)}) %copy-start.15) | copy-done | bytes 268
  7.9 0.2 bands.1
  8.2 0.7 %collective-permute-done.in_ref = bf16[2,32,1024]{2,1,0:T(8,128)(2,1)S(1)} collective-permute-done((bf16[2,32,1024]{2,1,0:T(8,128)(2,1)}, bf16[2,32,1024]{2,1,0:T(8,128)(2,1)S(1)}, u32[]{:S(2)}, u32[]{:S(2)}) %collective-permute-start) | collective-permute-done | bytes 131104 | tf_op jit(solution)/shard_map/ppermute | solution.py:355
  8.8 0.9 %vertical.2 = (bf16[2,2,32,1024]{3,2,1,0:T(8,128)(2,1)S(1)}, f32[2,32,128]{2,1,0:T(8,128)}) custom-call(bf16[2,32,96]{2,1,0:T(8,128)(2,1)S(1)} %get-tuple-element.28.bands_ref, bf16[2,32,1024]{2,1,0:T(8,128)(2,1)S(1)} %copy-done.2, bf16[2,32,1024]{2,1,0:T(8,128)(2,1)S(1)} %copy-done.3, bf16[2,32,1024]{2,1,0:T(8,128)(2,1)S(1)} %collective-permute-done.in_ref), custom_call_target="tpu_custom_call" | custom-call | tf_op jit(solution)/shard_map/vertical/pallas_call | solution.py:378
  9.9 0.8 %copy-done.1 = s32[64,1024]{1,0:T(8,128)S(1)} copy-done((s32[64,1024]{1,0:T(8,128)S(1)}, s32[64,1024]{1,0:T(8,128)}, u32[]{:S(2)}) %copy-start.1) | copy-done | bytes 262168
  10.7 0.4 %hats.1 = (f32[8,32,1024]{2,1,0:T(8,128)S(1)}, f32[32,1024]{1,0:T(8,128)S(1)}, f32[8,32,1024]{2,1,0:T(8,128)S(1)}, f32[32,1024]{1,0:T(8,128)S(1)}) custom-call(f32[64,1024]{1,0:T(8,128)S(1)} %copy-done.4, s32[64,1024]{1,0:T(8,128)S(1)} %copy-done.1, f32[64,1024]{1,0:T(8,128)S(1)} %copy-done.5), custom_call_target="tpu_custom_call" | custom-call | tf_op jit(solution)/shard_map/hats/pallas_call | solution.py:395
  11.2 2.6 %correct_near.1.rest_0_.refs_8_.near_ref = bf16[32,4,1024]{2,1,0:T(4,128)(2,1)S(1)} custom-call(bf16[2,256,512]{2,1,0:T(8,128)(2,1)S(1)} %get-tuple-element.27.refs_0_, bf16[192,256]{1,0:T(8,128)(2,1)S(1)} %reshape.9.refs_1_, f32[2,32,128]{2,1,0:T(8,128)S(1)} %collective-permute-done.1.refs_2_, bf16[2,2,32,1024]{3,2,1,0:T(8,128)(2,1)S(1)} %get-tuple-element.32.refs_3_, ...), custom_call_target="tpu_custom_call" | custom-call | tf_op jit(solution)/shard_map/correct_near/pallas_call | solution.py:405
  13.8 1.2 %vertical.3 = (bf16[2,2,32,1024]{3,2,1,0:T(8,128)(2,1)S(1)}, f32[2,32,128]{2,1,0:T(8,128)S(1)}) custom-call(bf16[2,32,96]{2,1,0:T(8,128)(2,1)S(1)} %get-tuple-element.28.bands_ref, bf16[2,32,1024]{2,1,0:T(8,128)(2,1)S(1)} %copy-done.3, bf16[2,32,1024]{2,1,0:T(8,128)(2,1)S(1)} %copy-done.2, bf16[2,32,1024]{2,1,0:T(8,128)(2,1)} %collective-permute-done.2.in_ref, ...), custom_call_target="tpu_custom_call" | custom-call | tf_op jit(solution)/shard_map/vertical/pallas_call | solution.py:378
  15.0 0.3 collective-permute-start.3
  15.3 0.4 copy-done.14
  15.7 0.7 %copy-done.11 = s32[4]{0:T(128)S(1)} copy-done((s32[4]{0:T(128)S(1)}, s32[4]{0:T(128)}, u32[]{:S(2)}) %copy-start.11) | copy-done | bytes 40
  16.4 3.3 %correct_far.1 = (bf16[32,4,1024]{2,1,0:T(4,128)(2,1)S(1)}, bf16[33,4,1024]{2,1,0:T(4,128)(2,1)S(1)}, bf16[33,4,1024]{2,1,0:T(4,128)(2,1)S(1)}, bf16[33,4,1024]{2,1,0:T(4,128)(2,1)S(1)}, bf16[33,4,1024]{2,1,0:T(4,128)(2,1)S(1)}) custom-call(s32[16]{0:T(128)S(1)} %concatenate.9.meta_ref, bf16[2,256,512]{2,1,0:T(8,128)(2,1)S(1)} %get-tuple-element.27.refs_0_, ...), custom_call_target="tpu_custom_call" | custom-call | tf_op jit(solution)/shard_map/correct_far/pallas_call | solution.py:416
  19.8 3.1 %collective-permute-start.4 = (bf16[33,4,1024]{2,1,0:T(4,128)(2,1)S(1)}, bf16[33,4,1024]{2,1,0:T(4,128)(2,1)S(1)}, u32[]{:S(2)}, u32[]{:S(2)}) collective-permute-start(bf16[33,4,1024]{2,1,0:T(4,128)(2,1)S(1)} %get-tuple-element.42), channel_id=1, source_target_pairs={{0,2},{2,0},{4,6},{6,4},{8,10},{10,8},{12,14},{14,12},{1,3},{3,1},... | collective-permute-start | bytes 811016 | tf_op jit(solution)/shard_map/ppermute | solution.py:427
  22.9 0.7 %collective-permute-start.5 = (bf16[33,4,1024]{2,1,0:T(4,128)(2,1)S(1)}, bf16[33,4,1024]{2,1,0:T(4,128)(2,1)S(1)}, u32[]{:S(2)}, u32[]{:S(2)}) collective-permute-start(bf16[33,4,1024]{2,1,0:T(4,128)(2,1)S(1)} %get-tuple-element.43), channel_id=1, source_target_pairs={{2,4},{4,2},{6,8},{8,6},{10,12},{12,10},{3,5},{5,3},{7,9},{9,7},{1... | collective-permute-start | bytes 811016 | tf_op jit(solution)/shard_map/ppermute | solution.py:427
  23.6 2.9 %collective-permute-start.6 = (bf16[33,4,1024]{2,1,0:T(4,128)(2,1)S(1)}, bf16[33,4,1024]{2,1,0:T(4,128)(2,1)S(1)}, u32[]{:S(2)}, u32[]{:S(2)}) collective-permute-start(bf16[33,4,1024]{2,1,0:T(4,128)(2,1)S(1)} %get-tuple-element.46), channel_id=1, source_target_pairs={{0,4},{4,0},{2,6},{6,2},{8,12},{12,8},{10,14},{14,10},{1,5},{5,1},... | collective-permute-start | bytes 811016 | tf_op jit(solution)/shard_map/ppermute | solution.py:427
  26.5 0.7 %collective-permute-start.7 = (bf16[33,4,1024]{2,1,0:T(4,128)(2,1)S(1)}, bf16[33,4,1024]{2,1,0:T(4,128)(2,1)S(1)}, u32[]{:S(2)}, u32[]{:S(2)}) collective-permute-start(bf16[33,4,1024]{2,1,0:T(4,128)(2,1)S(1)} %get-tuple-element.47), channel_id=1, source_target_pairs={{4,8},{8,4},{6,10},{10,6},{5,9},{9,5},{7,11},{11,7},{20,24},{24,20... | collective-permute-start | bytes 811016 | tf_op jit(solution)/shard_map/ppermute | solution.py:427
  27.1 0.7 %own.1 = (f32[64,4,1024]{2,1,0:T(4,128)S(1)}, f32[64,128]{1,0:T(8,128)S(1)}) custom-call(s32[16]{0:T(128)S(1)} %concatenate.9.meta_ref, bf16[32,4,1024]{2,1,0:T(4,128)(2,1)S(1)} %correct_near.1.rest_0_.refs_8_.near_ref, bf16[32,4,1024]{2,1,0:T(4,128)(2,1)S(1)} %get-tuple-element.39.far_ref), custom_call_target="tpu_custom_call" | custom-call | tf_op jit(solution)/shard_map/own/pallas_call | solution.py:431
  27.9 6.9 %collective-permute-done.4.side0_ref = bf16[33,4,1024]{2,1,0:T(4,128)(2,1)S(1)} collective-permute-done((bf16[33,4,1024]{2,1,0:T(4,128)(2,1)S(1)}, bf16[33,4,1024]{2,1,0:T(4,128)(2,1)S(1)}, u32[]{:S(2)}, u32[]{:S(2)}) %collective-permute-start.4) | collective-permute-done | bytes 270368 | tf_op jit(solution)/shard_map/ppermute | solution.py:427
  35.0 3.8 %collective-permute-done.6.side0_ref = bf16[33,4,1024]{2,1,0:T(4,128)(2,1)S(1)} collective-permute-done((bf16[33,4,1024]{2,1,0:T(4,128)(2,1)S(1)}, bf16[33,4,1024]{2,1,0:T(4,128)(2,1)S(1)}, u32[]{:S(2)}, u32[]{:S(2)}) %collective-permute-start.6) | collective-permute-done | bytes 270368 | tf_op jit(solution)/shard_map/ppermute | solution.py:427
  38.8 1.1 %last.1 = (f32[64,4,1024]{2,1,0:T(4,128)S(1)}, bf16[64,4,1024]{2,1,0:T(4,128)(2,1)}) custom-call(f32[64,4,1024]{2,1,0:T(4,128)S(1)} %get-tuple-element.44.acc_in_ref, f32[64,128]{1,0:T(8,128)S(1)} %get-tuple-element.45.count_in_ref, bf16[33,4,1024]{2,1,0:T(4,128)(2,1)S(1)} %collective-permute-done.6.side0_ref, ...), custom_call_target="tpu_custom_call", output_to_operand_aliasing={{0}: (0, {})} | custom-call | tf_op jit(solution)/shard_map/last/pallas_call | solution.py:448
  (44 shorter events, 0.7 us)
Async XLA Ops:
  0.0 7.0 %copy-start.8 = (bf16[4,8,16,8]{2,3,1,0:T(8,128)(2,1)S(1)}, bf16[4,8,16,8]{2,3,1,0:T(8,128)(2,1)}, u32[]{:S(2)}) copy-start(bf16[4,8,16,8]{2,3,1,0:T(8,128)(2,1)} %param.19) | copy-start | bytes 24580
  0.0 7.0 %copy-start.10 = (bf16[4,8,16,8]{2,3,1,0:T(8,128)(2,1)S(1)}, bf16[4,8,16,8]{2,3,1,0:T(8,128)(2,1)}, u32[]{:S(2)}) copy-start(bf16[4,8,16,8]{2,3,1,0:T(8,128)(2,1)} %param.17) | copy-start | bytes 24580
  0.0 7.0 %copy-start.9 = (bf16[4,8,16,8]{2,3,1,0:T(8,128)(2,1)S(1)}, bf16[4,8,16,8]{2,3,1,0:T(8,128)(2,1)}, u32[]{:S(2)}) copy-start(bf16[4,8,16,8]{2,3,1,0:T(8,128)(2,1)} %param.18) | copy-start | bytes 24580
  2.1 4.4 %copy-start.13 = (s32[4,2]{0,1:T(2,128)S(1)}, s32[4,2]{0,1:T(2,128)}, u32[]{:S(2)}) copy-start(s32[4,2]{0,1:T(2,128)} %param.21) | copy-start | bytes 100
  2.1 6.7 %collective-permute-start = (bf16[2,32,1024]{2,1,0:T(8,128)(2,1)}, bf16[2,32,1024]{2,1,0:T(8,128)(2,1)S(1)}, u32[]{:S(2)}, u32[]{:S(2)}) collective-permute-start(bf16[2,32,1024]{2,1,0:T(8,128)(2,1)} %get-tuple-element.29.here_ref.beside_ref), channel_id=1, source_target_pairs={{0,2},{2,0},{4,6},{6,4},{8,10},{10,8},{12,14},{14,12},{1,3},{3,1},... | collective-permute-start | bytes 393224 | tf_op jit(solution)/shard_map/ppermute | solution.py:355
  5.1 8.7 %collective-permute-start.2 = (bf16[2,32,1024]{2,1,0:T(8,128)(2,1)}, bf16[2,32,1024]{2,1,0:T(8,128)(2,1)}, u32[]{:S(2)}, u32[]{:S(2)}) collective-permute-start(bf16[2,32,1024]{2,1,0:T(8,128)(2,1)} %get-tuple-element.30.beside_ref.here_ref), channel_id=1, source_target_pairs={{2,4},{4,2},{6,8},{8,6},{10,12},{12,10},{3,5},{5,3},{7,9},{9,7},{1... | collective-permute-start | bytes 393224 | tf_op jit(solution)/shard_map/ppermute | solution.py:356
  7.1 1.8 %copy-start.3 = (bf16[2,32,1024]{2,1,0:T(8,128)(2,1)S(1)}, bf16[2,32,1024]{2,1,0:T(8,128)(2,1)}, u32[]{:S(2)}) copy-start(bf16[2,32,1024]{2,1,0:T(8,128)(2,1)} %get-tuple-element.30.beside_ref.here_ref) | copy-start | bytes 393220
  7.2 1.6 %copy-start.2 = (bf16[2,32,1024]{2,1,0:T(8,128)(2,1)S(1)}, bf16[2,32,1024]{2,1,0:T(8,128)(2,1)}, u32[]{:S(2)}) copy-start(bf16[2,32,1024]{2,1,0:T(8,128)(2,1)} %get-tuple-element.29.here_ref.beside_ref) | copy-start | bytes 393220
  7.3 0.7 %copy-start.15 = (f32[61]{0:T(128)S(1)}, f32[61]{0:T(128)}, u32[]{:S(2)}) copy-start(f32[61]{0:T(128)} %param.16) | copy-start | bytes 736
  8.8 1.0 %copy-start.4 = (f32[64,1024]{1,0:T(8,128)S(1)}, f32[64,1024]{1,0:T(8,128)}, u32[]{:S(2)}) copy-start(f32[64,1024]{1,0:T(8,128)} %vapour_ref.1) | copy-start | bytes 786436
  8.8 1.0 %copy-start.5 = (f32[64,1024]{1,0:T(8,128)S(1)}, f32[64,1024]{1,0:T(8,128)}, u32[]{:S(2)}) copy-start(f32[64,1024]{1,0:T(8,128)} %frac_ref.1) | copy-start | bytes 786436
  9.7 1.0 %copy-start.1 = (s32[64,1024]{1,0:T(8,128)S(1)}, s32[64,1024]{1,0:T(8,128)}, u32[]{:S(2)}) copy-start(s32[64,1024]{1,0:T(8,128)} %refs_7_.3) | copy-start | bytes 786436
  9.7 1.4 %collective-permute-start.1 = (f32[2,32,128]{2,1,0:T(8,128)}, f32[2,32,128]{2,1,0:T(8,128)S(1)}, u32[]{:S(2)}, u32[]{:S(2)}) collective-permute-start(f32[2,32,128]{2,1,0:T(8,128)} %get-tuple-element.31), channel_id=1, source_target_pairs={{0,1},{1,0},{2,3},{3,2},{4,5},{5,4},{6,7},{7,6},{8,9},{9,8},{10,11... | collective-permute-start | bytes 98312 | tf_op jit(solution)/shard_map/ppermute | solution.py:389
  9.8 1.3 %copy-start = (bf16[64,4,1024]{2,1,0:T(4,128)(2,1)S(1)}, bf16[64,4,1024]{2,1,0:T(4,128)(2,1)}, u32[]{:S(2)}) copy-start(bf16[64,4,1024]{2,1,0:T(4,128)(2,1)} %refs_6_.3) | copy-start | bytes 1572868
  11.1 2.6 %copy-start.6 = (f32[32,1024]{1,0:T(8,128)}, f32[32,1024]{1,0:T(8,128)S(1)}, u32[]{:S(2)}) copy-start(f32[32,1024]{1,0:T(8,128)S(1)} %get-tuple-element.38.refs_5_) | copy-start | bytes 393220
  13.8 2.7 %copy-start.7 = (f32[32,1024]{1,0:T(8,128)S(1)}, f32[32,1024]{1,0:T(8,128)}, u32[]{:S(2)}) copy-start(f32[32,1024]{1,0:T(8,128)} %copy-done.6) | copy-start | bytes 393220
  15.0 0.7 %copy-start.14 = (s32[4,2]{0,1:T(2,128)S(1)}, s32[4,2]{0,1:T(2,128)}, u32[]{:S(2)}) copy-start(s32[4,2]{0,1:T(2,128)} %param.20) | copy-start | bytes 100
  15.0 1.4 %collective-permute-start.3 = (f32[2,32,128]{2,1,0:T(8,128)S(1)}, f32[2,32,128]{2,1,0:T(8,128)S(1)}, u32[]{:S(2)}, u32[]{:S(2)}) collective-permute-start(f32[2,32,128]{2,1,0:T(8,128)S(1)} %get-tuple-element.35), channel_id=1, source_target_pairs={{0,1},{1,0},{2,3},{3,2},{4,5},{5,4},{6,7},{7,6},{8,9},{9,8},{10,11... | collective-permute-start | bytes 98312 | tf_op jit(solution)/shard_map/ppermute | solution.py:389
  15.7 0.7 %copy-start.11 = (s32[4]{0:T(128)S(1)}, s32[4]{0:T(128)}, u32[]{:S(2)}) copy-start(s32[4]{0:T(128)} %get-tuple-element.51) | copy-start | bytes 52
  15.7 0.7 %copy-start.12 = (s32[4]{0:T(128)S(1)}, s32[4]{0:T(128)}, u32[]{:S(2)}) copy-start(s32[4]{0:T(128)} %get-tuple-element.52) | copy-start | bytes 52
  19.8 15.0 %collective-permute-start.4 = (bf16[33,4,1024]{2,1,0:T(4,128)(2,1)S(1)}, bf16[33,4,1024]{2,1,0:T(4,128)(2,1)S(1)}, u32[]{:S(2)}, u32[]{:S(2)}) collective-permute-start(bf16[33,4,1024]{2,1,0:T(4,128)(2,1)S(1)} %get-tuple-element.42), channel_id=1, source_target_pairs={{0,2},{2,0},{4,6},{6,4},{8,10},{10,8},{12,14},{14,12},{1,3},{3,1},... | collective-permute-start | bytes 811016 | tf_op jit(solution)/shard_map/ppermute | solution.py:427
  22.9 11.9 %collective-permute-start.5 = (bf16[33,4,1024]{2,1,0:T(4,128)(2,1)S(1)}, bf16[33,4,1024]{2,1,0:T(4,128)(2,1)S(1)}, u32[]{:S(2)}, u32[]{:S(2)}) collective-permute-start(bf16[33,4,1024]{2,1,0:T(4,128)(2,1)S(1)} %get-tuple-element.43), channel_id=1, source_target_pairs={{2,4},{4,2},{6,8},{8,6},{10,12},{12,10},{3,5},{5,3},{7,9},{9,7},{1... | collective-permute-start | bytes 811016 | tf_op jit(solution)/shard_map/ppermute | solution.py:427
  23.6 15.2 %collective-permute-start.6 = (bf16[33,4,1024]{2,1,0:T(4,128)(2,1)S(1)}, bf16[33,4,1024]{2,1,0:T(4,128)(2,1)S(1)}, u32[]{:S(2)}, u32[]{:S(2)}) collective-permute-start(bf16[33,4,1024]{2,1,0:T(4,128)(2,1)S(1)} %get-tuple-element.46), channel_id=1, source_target_pairs={{0,4},{4,0},{2,6},{6,2},{8,12},{12,8},{10,14},{14,10},{1,5},{5,1},... | collective-permute-start | bytes 811016 | tf_op jit(solution)/shard_map/ppermute | solution.py:427
  26.5 12.3 %collective-permute-start.7 = (bf16[33,4,1024]{2,1,0:T(4,128)(2,1)S(1)}, bf16[33,4,1024]{2,1,0:T(4,128)(2,1)S(1)}, u32[]{:S(2)}, u32[]{:S(2)}) collective-permute-start(bf16[33,4,1024]{2,1,0:T(4,128)(2,1)S(1)} %get-tuple-element.47), channel_id=1, source_target_pairs={{4,8},{8,4},{6,10},{10,6},{5,9},{9,5},{7,11},{11,7},{20,24},{24,20... | collective-permute-start | bytes 811016 | tf_op jit(solution)/shard_map/ppermute | solution.py:427

commit v3 on v2

--- a/solution.py
+++ b/solution.py
@@ -18,7 +18,7 @@
 SMEM = pl.BlockSpec(memory_space=pltpu.SMEM)
 
 
-def params(mib=32):
+def params(mib=24):
     return pltpu.CompilerParams(vmem_limit_bytes=mib * 1024 * 1024)
 
 
@@ -28,6 +28,10 @@
         if (i // step) % 2 == offset:
             pairs += [(i, i + step), (i + step, i)]
     return pairs
+
+
+def in_hbm(*arrays):
+    return [pltpu.with_memory_space_constraint(array, pltpu.HBM) for array in arrays]
 
 
 def split_bf16(x):
@@ -67,20 +71,18 @@
                     out_ref[field, to] = lines[field]
 
 
-def bands_kernel(taps_ref, rows_ref, cols_ref):
-    taps = taps_ref[...]
-    for out_ref, first in ((rows_ref, rows_ref.shape[1] - 30), (cols_ref, LANES - 30)):
-        depth, width = out_ref.shape[1], out_ref.shape[2]
-        base = taps
-        if width > LANES:
-            base = jnp.concatenate([taps, jnp.zeros((1, width - LANES), F32)], axis=1)
-        base = jnp.broadcast_to(base, (8, base.shape[1]))
-        base = pltpu.roll(base, 0, 1, stride=1, stride_axis=0)
-        for at in range(0, depth, 16):
-            pair = [pltpu.roll(base, first + at + 8 * k, 1)[:, :width] for k in range(2)]
-            high, low = split_bf16(jnp.concatenate(pair, axis=0))
-            out_ref[0, at : at + 16] = high
-            out_ref[1, at : at + 16] = low
+def store_bands(taps, out_ref, first):
+    depth, width = out_ref.shape[1], out_ref.shape[2]
+    base = taps
+    if width > LANES:
+        base = jnp.concatenate([taps, jnp.zeros((1, width - LANES), F32)], axis=1)
+    base = jnp.broadcast_to(base, (8, base.shape[1]))
+    base = pltpu.roll(base, 0, 1, stride=1, stride_axis=0)
+    for at in range(0, depth, 16):
+        pair = [pltpu.roll(base, first + at + 8 * k, 1)[:, :width] for k in range(2)]
+        high, low = split_bf16(jnp.concatenate(pair, axis=0))
+        out_ref[0, at : at + 16] = high
+        out_ref[1, at : at + 16] = low
 
 
 def is_half(flip):
@@ -113,16 +115,72 @@
         ext_ref[1, index] = low
 
 
-def hats_kernel(vapour_ref, class_ref, frac_ref, *halves):
-    for flip in range(2):
-        hat_ref, even_ref = halves[2 * flip : 2 * flip + 2]
-        rows = even_ref.shape[0]
-        here = pl.ds(pl.multiple_of(jnp.where(is_half(flip), rows, 0), rows), rows)
-        vapour = vapour_ref[here]
-        for w in range(hat_ref.shape[0]):
-            hat_ref[w] = jnp.maximum(0.0, 1.0 - jnp.abs(vapour - float(w)))
-        frac = frac_ref[here]
-        even_ref[...] = jnp.where(class_ref[here] % 2 == 0, 1.0 - frac, frac)
+def store_table(array, out_ref, table, shape):
+    bands, levels_e, levels_w, levels_a = shape
+    nodes = levels_w * levels_a
+
+    def iota(size, dim):
+        return lax.broadcasted_iota(jnp.int32, size, dim)
+
+    repeat = iota((levels_a, nodes), 1) % levels_a == iota((levels_a, nodes), 0)
+    spread = jnp.dot(array, jnp.where(repeat, 1.0, 0.0).astype(BF16), preferred_element_type=F32)
+    own = iota(spread.shape, 1) // levels_a == iota(spread.shape, 0) % levels_w
+    spread = jnp.where(own, spread, 0.0).astype(BF16)
+    size = (2 * bands * levels_e, spread.shape[0])
+    row, source = iota(size, 0), iota(size, 1) // levels_w
+    wanted = row % bands * levels_e + row // (2 * bands)
+    for k in range(2):
+        pick = (source == wanted) & (row // bands % 2 == k)
+        part = jnp.dot(jnp.where(pick, 1.0, 0.0).astype(BF16), spread, preferred_element_type=F32)
+        out_ref[table * size[0] : (table + 1) * size[0], k * nodes : (k + 1) * nodes] = part.astype(BF16)
+
+
+def early_kernel(
+    shape,
+    gain_ref,
+    path_ref,
+    albedo_ref,
+    taps_ref,
+    vapour_ref,
+    class_ref,
+    frac_ref,
+    lut_ref,
+    rows_ref,
+    cols_ref,
+    vapour_out_ref,
+    class_out_ref,
+    frac_out_ref,
+    tables_in,
+    taps_in,
+    sems,
+):
+    tables = [(source, tables_in.at[k]) for k, source in enumerate((gain_ref, path_ref, albedo_ref))]
+    others = [(vapour_ref, vapour_out_ref), (class_ref, class_out_ref), (frac_ref, frac_out_ref)]
+    pairs = [(taps_ref, taps_in)] + tables + others
+    copies = [pltpu.make_async_copy(source, into, sems.at[k]) for k, (source, into) in enumerate(pairs)]
+    for copy in copies:
+        copy.start()
+    copies[0].wait()
+    taps = taps_in[...]
+    taps = jnp.concatenate([taps, jnp.zeros((1, LANES - taps.shape[1]), F32)], axis=1)
+    store_bands(taps, rows_ref, rows_ref.shape[1] - 30)
+    store_bands(taps, cols_ref, LANES - 30)
+    for table in range(3):
+        copies[1 + table].wait()
+        store_table(tables_in[table], lut_ref, table, shape)
+    for copy in copies[4:]:
+        copy.wait()
+
+
+def hats_kernel(flip, vapour_ref, class_ref, frac_ref, *rest):
+    hat_ref, even_ref = rest[-2:]
+    rows = even_ref.shape[0]
+    here = pl.ds(pl.multiple_of(jnp.where(is_half(flip), rows, 0), rows), rows)
+    vapour = vapour_ref[here]
+    for w in range(hat_ref.shape[0]):
+        hat_ref[w] = jnp.maximum(0.0, 1.0 - jnp.abs(vapour - float(w)))
+    frac = frac_ref[here]
+    even_ref[...] = jnp.where(class_ref[here] % 2 == 0, 1.0 - frac, frac)
 
 
 def correct_rows(
@@ -231,28 +289,41 @@
     return [(shift + k, near_ref, k) for k in range(each)] + [(each - shift + k, far_ref, k) for k in range(each)]
 
 
-def correct_far_kernel(meta_ref, *refs):
+def correct_far_kernel(routes_in_ref, starts_in_ref, *refs):
     near_ref, corr_ref, sides = refs[8], refs[9], refs[10:14]
-    correct_rows(1, *refs[:8], corr_ref, *refs[14:])
+    pos_ref, routes_ref, starts_ref, sems = refs[14:]
+    copies = [
+        pltpu.make_async_copy(routes_in_ref, routes_ref, sems.at[0]),
+        pltpu.make_async_copy(starts_in_ref, starts_ref, sems.at[1]),
+    ]
+    for copy in copies:
+        copy.start()
+    correct_rows(1, *refs[:8], corr_ref, pos_ref)
+    for copy in copies:
+        copy.wait()
+    me = lax.axis_index("along")
+    beside = 1 - 2 * (me % 2)
+    beyond = 2 - 4 * ((me // 2) % 2)
     listed = segment_list(near_ref, corr_ref)
-    segments = len(listed)
     band = lax.broadcasted_iota(jnp.int32, corr_ref.shape[1:], 0)
-    for side, out_ref in enumerate(sides):
-        target = meta_ref[side]
-        tags = jnp.zeros(corr_ref.shape[1:], F32)
+    for target, out_ref in zip((me + beside, me - beside, me + beyond, me - beyond), sides):
         count = jnp.int32(0)
+        tags = [jnp.int32(0) for _ in range(CAP)]
         for segment, from_ref, place in listed:
-            hit = meta_ref[4 + segment] == target
+            hit = routes_ref[1, segment] == target
             slot = count
 
             @pl.when(hit)
             def _():
                 out_ref[pl.ds(slot * SEG, SEG)] = from_ref[place * SEG : (place + 1) * SEG]
 
-            tag = jnp.where(hit, meta_ref[4 + 2 * segments + segment] + 1, 0).astype(F32)
-            tags = tags + jnp.where(band == slot, tag, 0.0)
+            tag = jnp.where(hit, starts_ref[1, segment] + 1, 0)
+            tags = [jnp.where(slot == k, tags[k] + tag, tags[k]) for k in range(CAP)]
             count = count + hit.astype(jnp.int32)
-        out_ref[CAP * SEG] = tags.astype(BF16)
+        line = jnp.zeros(band.shape, jnp.int32)
+        for k in range(CAP):
+            line = jnp.where(band == k, tags[k], line)
+        out_ref[CAP * SEG] = line.astype(F32).astype(BF16)
 
 
 def add_rows(acc_ref, start, from_ref, place):
@@ -288,12 +359,12 @@
     return count
 
 
-def own_kernel(meta_ref, near_ref, far_ref, acc_ref, count_ref):
+def own_kernel(starts_ref, near_ref, far_ref, acc_ref, count_ref):
     acc_ref[...] = jnp.zeros(acc_ref.shape, F32)
     count = jnp.zeros(count_ref.shape, F32)
     listed = segment_list(near_ref, far_ref)
     for segment, from_ref, place in listed:
-        start = meta_ref[4 + len(listed) + segment]
+        start = starts_ref[0, segment]
         count = count + covers(count.shape[0], start)
         add_rows(acc_ref, start, from_ref, place)
     count_ref[...] = count
@@ -303,14 +374,22 @@
     count_ref[...] = add_sides(acc_ref, count_in_ref[...], (side0_ref, side1_ref))
 
 
-def last_kernel(acc_in_ref, count_in_ref, side0_ref, side1_ref, acc_ref, out_ref, inv_ref):
+def last_kernel(acc_in_ref, count_in_ref, side0_ref, side1_ref, acc_ref, out_ref, inv_ref, line_ref, sems):
     count = add_sides(acc_ref, count_in_ref[...], (side0_ref, side1_ref))
     inv_ref[...] = 1.0 / jnp.maximum(count, 1.0)
-    repeat = out_ref.shape[2] // LANES
-    for row in range(out_ref.shape[0]):
-        inverse = jnp.broadcast_to(inv_ref[row : row + 1, :], (out_ref.shape[1], LANES))
-        inverse = jnp.concatenate([inverse] * repeat, axis=1)
-        out_ref[row] = (acc_ref[row] * inverse).astype(BF16)
+    rows, bands, cols = line_ref.shape
+    size = rows // 4
+    copies = []
+    for part in range(4):
+        for row in range(part * size, (part + 1) * size):
+            inverse = jnp.broadcast_to(inv_ref[row : row + 1, :], (bands, LANES))
+            inverse = jnp.concatenate([inverse] * (cols // LANES), axis=1)
+            line_ref[row] = (acc_ref[row] * inverse).astype(BF16)
+        at = pl.ds(part * size, size)
+        copies.append(pltpu.make_async_copy(line_ref.at[at], out_ref.at[at], sems.at[part]))
+        copies[-1].start()
+    for copy in copies:
+        copy.wait()
 
 
 def body(
@@ -330,13 +409,6 @@
     levels_e, levels_a, levels_w = lut_gain.shape[1:]
     nodes = levels_a * levels_w
     count = lax.axis_size("along")
-    me = lax.axis_index("along")
-    near = 1 - 2 * (me % 2)
-    far_z = 2 - 4 * ((me // 2) % 2)
-    distance = routes[:, 1] - me
-    meta = jnp.concatenate(
-        [jnp.stack([near, -near, far_z, -far_z]), distance, starts[:, 0], starts[:, 1]]
-    ).astype(jnp.int32)
     half = rows // 2
     fields = jax.ShapeDtypeStruct((2, half, cols), BF16)
     near_out, far_out = pl.pallas_call(
@@ -349,30 +421,38 @@
             pltpu.VMEM((rows, cols), jnp.int32),
             pltpu.SemaphoreType.DMA((2, 4)),
         ],
-        compiler_params=params(62),
+        compiler_params=params(),
         name="prep",
-    )(toa_bands, dark_mask)
+    )(*in_hbm(toa_bands, dark_mask))
     near_in = lax.ppermute(near_out, "along", swap_pairs(count, 1, 0))
     far_in = lax.ppermute(far_out, "along", swap_pairs(count, 1, 1))
-    taps = jnp.pad(kernel, (0, LANES - kernel.shape[0]))[None, :]
     block = 256
-    row_bands, col_bands = pl.pallas_call(
-        bands_kernel,
+    weights = (
+        jax.ShapeDtypeStruct((levels_w, half, cols), F32),
+        jax.ShapeDtypeStruct((half, cols), F32),
+    )
+    tables = [table.transpose(0, 1, 3, 2).reshape(-1, levels_a) for table in (lut_gain, lut_path, lut_albedo)]
+    whole = jax.ShapeDtypeStruct((rows, cols), F32)
+    lut, row_bands, col_bands, vapours, classes, fracs = pl.pallas_call(
+        functools.partial(early_kernel, (bands, levels_e, levels_w, levels_a)),
         out_shape=(
+            jax.ShapeDtypeStruct((6 * levels_e * bands, 2 * nodes), BF16),
             jax.ShapeDtypeStruct((2, half, 3 * half), BF16),
             jax.ShapeDtypeStruct((2, block, block + 2 * LANES), BF16),
+            whole,
+            jax.ShapeDtypeStruct((rows, cols), jnp.int32),
+            whole,
         ),
-        in_specs=[VMEM],
-        out_specs=(VMEM, VMEM),
-        compiler_params=params(),
-        name="bands",
-    )(taps)
-    tables = jnp.stack([lut_gain, lut_path, lut_albedo]).transpose(0, 2, 1, 4, 3)
-    tables = tables.reshape(3, levels_e, bands, nodes)
-    blank = jnp.zeros_like(tables)
-    lut = jnp.stack(
-        [jnp.concatenate([tables, blank], axis=3), jnp.concatenate([blank, tables], axis=3)], axis=2
-    ).reshape(6 * levels_e * bands, 2 * nodes)
+        in_specs=[HBM] * 7,
+        out_specs=(VMEM,) * 6,
+        scratch_shapes=[
+            pltpu.VMEM((3, bands * levels_e * levels_w, levels_a), BF16),
+            pltpu.VMEM((1, kernel.shape[0]), F32),
+            pltpu.SemaphoreType.DMA((7,)),
+        ],
+        compiler_params=params(),
+        name="early",
+    )(*in_hbm(*tables, kernel[None, :], vapour, elev_class, elev_frac))
 
     def smooth_rows(flip, here, beside, incoming, *after):
         ext, edge = pl.pallas_call(
@@ -386,20 +466,17 @@
             compiler_params=params(),
             name="vertical",
         )(row_bands, here, beside, incoming, *after)
-        return lax.ppermute(edge, "across", swap_pairs(lax.axis_size("across"), 1, 0)), ext
-
-    weights = (
-        jax.ShapeDtypeStruct((levels_w, half, cols), F32),
-        jax.ShapeDtypeStruct((half, cols), F32),
-    )
-    near_hats, near_even, far_hats, far_even = pl.pallas_call(
-        hats_kernel,
-        out_shape=weights * 2,
-        in_specs=[VMEM] * 3,
-        out_specs=(VMEM,) * 4,
-        compiler_params=params(),
-        name="hats",
-    )(vapour, elev_class, elev_frac)
+        hats = pl.pallas_call(
+            functools.partial(hats_kernel, flip),
+            out_shape=weights,
+            in_specs=[VMEM] * 4,
+            out_specs=(VMEM, VMEM),
+            compiler_params=params(),
+            name="hats",
+        )(vapours, classes, fracs, edge)
+        return lax.ppermute(edge, "across", swap_pairs(lax.axis_size("across"), 1, 0)), ext, *hats
+
+
     corrected = jax.ShapeDtypeStruct((half, bands, cols), BF16)
     scratch = [pltpu.VMEM((half, cols), F32)]
     near_corr = pl.pallas_call(
@@ -410,18 +487,21 @@
         scratch_shapes=scratch,
         compiler_params=params(),
         name="correct_near",
-    )(col_bands, lut, *smooth_rows(0, near_out, far_out, near_in), near_hats, near_even, toa_bands, elev_class)
-    far_edge, far_ext = smooth_rows(1, far_out, near_out, far_in, near_corr)
+    )(col_bands, lut, *smooth_rows(0, near_out, far_out, near_in), toa_bands, classes)
+    far = smooth_rows(1, far_out, near_out, far_in, near_corr)
+    segments = rows // SEG
     slots = jax.ShapeDtypeStruct((CAP * SEG + 1, bands, cols), BF16)
     far_corr, *sides = pl.pallas_call(
         correct_far_kernel,
         out_shape=(corrected,) + (slots,) * 4,
-        in_specs=[SMEM] + [VMEM] * 9,
+        in_specs=[HBM, HBM] + [VMEM] * 9,
         out_specs=(VMEM,) * 5,
-        scratch_shapes=scratch,
+        scratch_shapes=scratch
+        + [pltpu.SMEM((2, segments), jnp.int32)] * 2
+        + [pltpu.SemaphoreType.DMA((2,))],
         compiler_params=params(),
         name="correct_far",
-    )(meta, col_bands, lut, far_edge, far_ext, far_hats, far_even, toa_bands, elev_class, near_corr)
+    )(*in_hbm(routes.T, starts.T), col_bands, lut, *far, toa_bands, classes, near_corr)
     moves = ((1, 0), (1, 1), (2, 0), (2, 1))
     got = [
         lax.ppermute(side, "along", swap_pairs(count, step, offset)) for side, (step, offset) in zip(sides, moves)
@@ -435,7 +515,7 @@
         out_specs=(VMEM, VMEM),
         compiler_params=params(),
         name="own",
-    )(meta, near_corr, far_corr)
+    )(starts.T, near_corr, far_corr)
     acc, number = pl.pallas_call(
         add_kernel,
         out_shape=(total, counts),
@@ -449,8 +529,12 @@
         last_kernel,
         out_shape=(total, jax.ShapeDtypeStruct((rows, bands, cols), BF16)),
         in_specs=[VMEM] * 4,
-        out_specs=(VMEM, VMEM),
-        scratch_shapes=[pltpu.VMEM((rows, LANES), F32)],
+        out_specs=(VMEM, HBM),
+        scratch_shapes=[
+            pltpu.VMEM((rows, LANES), F32),
+            pltpu.VMEM((rows, bands, cols), BF16),
+            pltpu.SemaphoreType.DMA((4,)),
+        ],
         input_output_aliases={0: 0},
         compiler_params=params(),
         name="last",

time: 40.2 us -> 37 us (0.920)
  local copies, waits for them, and re-layouts: 3.47 us -> 0.01 us
  waiting for transfers between devices: 11.4 us -> 13.3 us
  Pallas kernels: 12.7 us -> 11.6 us
    unnamed x32 -> x4, local copies, waits for them, and re-layouts: 2.59 us -> 0.01 us
    ppermute x2, waiting for transfers between devices: 0.03 us -> 1.82 us  [smooth_rows(): lax.ppermute(edge, 'across', swap_pairs(lax.axis_size('across'), 1, 0))]
    pallas_call x2 -> x3, Pallas kernels: 0.6 us -> 2.26 us  [the longest x1 1.84 us: body(): pl.pallas_call(functools.partial(early_kernel, (bands, levels_e, levels_w...]
    pallas_call x2, Pallas kernels: 2.1 us -> 0.56 us  [smooth_rows(): pl.pallas_call(functools.partial(vertical_kernel, flip), out_shape=(jax.S...]
    pallas_call x1, Pallas kernels: 2.05 us -> 1.32 us  [body(): pl.pallas_call(prep_kernel, out_shape=(fields, fields), in_specs=[HBM, HB...]
    ppermute x1, starting transfers between devices: 1.3 us -> 0.66 us  [body(): far_in = lax.ppermute(far_out, 'along', swap_pairs(count, 1, 1))]
    squeeze x1 -> x0, local copies, waits for them, and re-layouts: 0.57 us -> none  [body(): starts[:, 1]]
    pallas_call x1, Pallas kernels: 3.35 us -> 2.87 us  [body(): pl.pallas_call(correct_far_kernel, out_shape=(corrected,) + (slots,) * 4,...]
  transfers between devices with their start and end apart: 8 -> 8, of which waited for: 3 -> 5; matrix products, arithmetic and copies ran while one was open for 3% -> 0% of each run, Pallas kernels for 13% -> 17%
where the time goes in v3:
time: 37 us; the launch traced here: 36.8 us
  waiting for transfers between devices  13.3 us (36%)
  starting transfers between devices  11.7 us (32%)
  Pallas kernels  11.6 us (31%)
    ppermute x4, waiting for transfers between devices, body(): lax.ppermute(side, 'along', swap_pairs(count, step, offset))  10.5 us
    ppermute x4, starting transfers between devices, body(): lax.ppermute(side, 'along', swap_pairs(count, step, offset))  7.73 us
    ppermute x1, starting transfers between devices, body(): near_in = lax.ppermute(near_out, 'along', swap_pairs(count, 1, 0))  3.03 us
    pallas_call x1, Pallas kernels, body(): pl.pallas_call(correct_far_kernel, out_shape=(corrected,) + (slots,) * 4,...  2.87 us
    pallas_call x1, Pallas kernels, body(): pl.pallas_call(correct_near_kernel, out_shape=corrected, in_specs=[VMEM]...  2.61 us
    pallas_call x1, Pallas kernels, body(): pl.pallas_call(functools.partial(early_kernel, (bands, levels_e, levels_w...  1.84 us
    ppermute x2, waiting for transfers between devices, smooth_rows(): lax.ppermute(edge, 'across', swap_pairs(lax.axis_size('across'), 1, 0))  1.82 us
    pallas_call x1, Pallas kernels, body(): pl.pallas_call(prep_kernel, out_shape=(fields, fields), in_specs=[HBM, HB...  1.32 us
  transfers between devices with their start and end apart: 8, of which 5 were waited for; matrix products, arithmetic and copies ran while one was open for 0% of the time, Pallas kernels for 17%

profile of v3, /device:TPU:0, one launch (start us, length us, event | category | flops | bytes accessed | tf_op | source)
XLA Modules:
  0.0 36.8 jit_solution(3318216534728647076)
XLA Ops:
  0.0 1.3 %prep.1 = (bf16[2,32,1024]{2,1,0:T(8,128)(2,1)S(1)}, bf16[2,32,1024]{2,1,0:T(8,128)(2,1)S(1)}) custom-call(bf16[64,4,1024]{2,1,0:T(4,128)(2,1)} %refs_6_.3, s32[64,1024]{1,0:T(8,128)} %dark_ref.1), custom_call_target="tpu_custom_call" | custom-call | tf_op jit(solution)/shard_map/prep/pallas_call | solution.py:414
  1.3 3.0 %collective-permute-start = (bf16[2,32,1024]{2,1,0:T(8,128)(2,1)S(1)}, bf16[2,32,1024]{2,1,0:T(8,128)(2,1)S(1)}, u32[]{:S(2)}, u32[]{:S(2)}) collective-permute-start(bf16[2,32,1024]{2,1,0:T(8,128)(2,1)S(1)} %get-tuple-element.34.here_ref.beside_ref), channel_id=1, source_target_pairs={{0,2},{2,0},{4,6},{6,4},{8,10},{10,8},{12,14},{14,12},{1,3},{3,1},... | collective-permute-start | bytes 393224 | tf_op jit(solution)/shard_map/ppermute | solution.py:427
  4.4 0.7 %collective-permute-start.2 = (bf16[2,32,1024]{2,1,0:T(8,128)(2,1)S(1)}, bf16[2,32,1024]{2,1,0:T(8,128)(2,1)S(1)}, u32[]{:S(2)}, u32[]{:S(2)}) collective-permute-start(bf16[2,32,1024]{2,1,0:T(8,128)(2,1)S(1)} %get-tuple-element.35.beside_ref.here_ref), channel_id=1, source_target_pairs={{2,4},{4,2},{6,8},{8,6},{10,12},{12,10},{3,5},{5,3},{7,9},{9,7},{1... | collective-permute-start | bytes 393224 | tf_op jit(solution)/shard_map/ppermute | solution.py:428
  5.0 1.8 %early.1 = (bf16[192,256]{1,0:T(8,128)(2,1)S(1)}, bf16[2,32,96]{2,1,0:T(8,128)(2,1)S(1)}, bf16[2,256,512]{2,1,0:T(8,128)(2,1)S(1)}, f32[64,1024]{1,0:T(8,128)S(1...) custom-call(bf16[256,16]{1,0:T(8,128)(2,1)} %bitcast.15, bf16[256,16]{1,0:T(8,128)(2,1)} %bitcast.16, ...), custom_call_target="tpu_custom_call" | custom-call | tf_op jit(solution)/shard_map/early/pallas_call | solution.py:436
  6.9 1.0 %collective-permute-done.in_ref = bf16[2,32,1024]{2,1,0:T(8,128)(2,1)S(1)} collective-permute-done((bf16[2,32,1024]{2,1,0:T(8,128)(2,1)S(1)}, bf16[2,32,1024]{2,1,0:T(8,128)(2,1)S(1)}, u32[]{:S(2)}, u32[]{:S(2)}) %collective-permute-start) | collective-permute-done | bytes 131104 | tf_op jit(solution)/shard_map/ppermute | solution.py:427
  7.9 0.3 vertical.2
  8.1 0.1 collective-permute-start.1
  8.2 0.2 hats.2
  8.5 1.0 %collective-permute-done.1.refs_2_ = f32[2,32,128]{2,1,0:T(8,128)S(1)} collective-permute-done((f32[2,32,128]{2,1,0:T(8,128)S(1)}, f32[2,32,128]{2,1,0:T(8,128)S(1)}, u32[]{:S(2)}, u32[]{:S(2)}) %collective-permute-start.1) | collective-permute-done | bytes 32800 | tf_op jit(solution)/shard_map/ppermute | solution.py:477
  9.4 2.6 %correct_near.1.rest_0_.refs_8_.near_ref = bf16[32,4,1024]{2,1,0:T(4,128)(2,1)S(1)} custom-call(bf16[2,256,512]{2,1,0:T(8,128)(2,1)S(1)} %get-tuple-element.31.refs_0_, bf16[192,256]{1,0:T(8,128)(2,1)S(1)} %get-tuple-element.32.refs_1_, f32[2,32,128]{2,1,0:T(8,128)S(1)} %collective-permute-done.1.refs_2_, ...), custom_call_target="tpu_custom_call" | custom-call | tf_op jit(solution)/shard_map/correct_near/pallas_call | solution.py:482
  12.0 0.3 vertical.3
  12.3 0.2 collective-permute-start.3
  12.6 0.2 hats.3
  12.8 0.9 %collective-permute-done.3.refs_2_ = f32[2,32,128]{2,1,0:T(8,128)S(1)} collective-permute-done((f32[2,32,128]{2,1,0:T(8,128)S(1)}, f32[2,32,128]{2,1,0:T(8,128)S(1)}, u32[]{:S(2)}, u32[]{:S(2)}) %collective-permute-start.3) | collective-permute-done | bytes 32800 | tf_op jit(solution)/shard_map/ppermute | solution.py:477
  13.6 2.9 %correct_far.1 = (bf16[32,4,1024]{2,1,0:T(4,128)(2,1)S(1)}, bf16[33,4,1024]{2,1,0:T(4,128)(2,1)S(1)}, bf16[33,4,1024]{2,1,0:T(4,128)(2,1)S(1)}, bf16[33,4,1024]{2,1,0:T(4,128)(2,1)S(1)}, bf16[33,4,1024]{2,1,0:T(4,128)(2,1)S(1)}) custom-call(s32[2,4]{1,0:T(2,128)} %bitcast.18, s32[2,4]{1,0:T(2,128)} %bitcast.13, ...), custom_call_target="tpu_custom_call" | custom-call | tf_op jit(solution)/shard_map/correct_far/pallas_call | solution.py:494
  16.5 3.4 %collective-permute-start.4 = (bf16[33,4,1024]{2,1,0:T(4,128)(2,1)S(1)}, bf16[33,4,1024]{2,1,0:T(4,128)(2,1)S(1)}, u32[]{:S(2)}, u32[]{:S(2)}) collective-permute-start(bf16[33,4,1024]{2,1,0:T(4,128)(2,1)S(1)} %get-tuple-element.50), channel_id=1, source_target_pairs={{0,2},{2,0},{4,6},{6,4},{8,10},{10,8},{12,14},{14,12},{1,3},{3,1},... | collective-permute-start | bytes 811016 | tf_op jit(solution)/shard_map/ppermute | solution.py:507
  19.9 0.7 %collective-permute-start.5 = (bf16[33,4,1024]{2,1,0:T(4,128)(2,1)S(1)}, bf16[33,4,1024]{2,1,0:T(4,128)(2,1)S(1)}, u32[]{:S(2)}, u32[]{:S(2)}) collective-permute-start(bf16[33,4,1024]{2,1,0:T(4,128)(2,1)S(1)} %get-tuple-element.51), channel_id=1, source_target_pairs={{2,4},{4,2},{6,8},{8,6},{10,12},{12,10},{3,5},{5,3},{7,9},{9,7},{1... | collective-permute-start | bytes 811016 | tf_op jit(solution)/shard_map/ppermute | solution.py:507
  20.6 2.9 %collective-permute-start.6 = (bf16[33,4,1024]{2,1,0:T(4,128)(2,1)S(1)}, bf16[33,4,1024]{2,1,0:T(4,128)(2,1)S(1)}, u32[]{:S(2)}, u32[]{:S(2)}) collective-permute-start(bf16[33,4,1024]{2,1,0:T(4,128)(2,1)S(1)} %get-tuple-element.54), channel_id=1, source_target_pairs={{0,4},{4,0},{2,6},{6,2},{8,12},{12,8},{10,14},{14,10},{1,5},{5,1},... | collective-permute-start | bytes 811016 | tf_op jit(solution)/shard_map/ppermute | solution.py:507
  23.4 0.8 %collective-permute-start.7 = (bf16[33,4,1024]{2,1,0:T(4,128)(2,1)S(1)}, bf16[33,4,1024]{2,1,0:T(4,128)(2,1)S(1)}, u32[]{:S(2)}, u32[]{:S(2)}) collective-permute-start(bf16[33,4,1024]{2,1,0:T(4,128)(2,1)S(1)} %get-tuple-element.55), channel_id=1, source_target_pairs={{4,8},{8,4},{6,10},{10,6},{5,9},{9,5},{7,11},{11,7},{20,24},{24,20... | collective-permute-start | bytes 811016 | tf_op jit(solution)/shard_map/ppermute | solution.py:507
  24.3 0.7 %own.1 = (f32[64,4,1024]{2,1,0:T(4,128)S(1)}, f32[64,128]{1,0:T(8,128)S(1)}) custom-call(s32[2,4]{1,0:T(2,128)S(1)} %bitcast.14, bf16[32,4,1024]{2,1,0:T(4,128)(2,1)S(1)} %correct_near.1.rest_0_.refs_8_.near_ref, bf16[32,4,1024]{2,1,0:T(4,128)(2,1)S(1)} %get-tuple-element.47.far_ref), custom_call_target="tpu_custom_call" | custom-call | tf_op jit(solution)/shard_map/own/pallas_call | solution.py:511
  25.0 6.8 %collective-permute-done.4.side0_ref = bf16[33,4,1024]{2,1,0:T(4,128)(2,1)S(1)} collective-permute-done((bf16[33,4,1024]{2,1,0:T(4,128)(2,1)S(1)}, bf16[33,4,1024]{2,1,0:T(4,128)(2,1)S(1)}, u32[]{:S(2)}, u32[]{:S(2)}) %collective-permute-start.4) | collective-permute-done | bytes 270368 | tf_op jit(solution)/shard_map/ppermute | solution.py:507
  31.8 0.2 add.1
  32.0 3.8 %collective-permute-done.6.side0_ref = bf16[33,4,1024]{2,1,0:T(4,128)(2,1)S(1)} collective-permute-done((bf16[33,4,1024]{2,1,0:T(4,128)(2,1)S(1)}, bf16[33,4,1024]{2,1,0:T(4,128)(2,1)S(1)}, u32[]{:S(2)}, u32[]{:S(2)}) %collective-permute-start.6) | collective-permute-done | bytes 270368 | tf_op jit(solution)/shard_map/ppermute | solution.py:507
  35.7 1.0 %last.1 = (f32[64,4,1024]{2,1,0:T(4,128)S(1)}, bf16[64,4,1024]{2,1,0:T(4,128)(2,1)}) custom-call(f32[64,4,1024]{2,1,0:T(4,128)S(1)} %get-tuple-element.52.acc_in_ref, f32[64,128]{1,0:T(8,128)S(1)} %get-tuple-element.53.count_in_ref, bf16[33,4,1024]{2,1,0:T(4,128)(2,1)S(1)} %collective-permute-done.6.side0_ref, ...), custom_call_target="tpu_custom_call", output_to_operand_aliasing={{0}: (0, {})} | custom-call | tf_op jit(solution)/shard_map/last/pallas_call | solution.py:528
  (7 shorter events, 0.0 us)
Async XLA Ops:
  1.3 6.5 %collective-permute-start = (bf16[2,32,1024]{2,1,0:T(8,128)(2,1)S(1)}, bf16[2,32,1024]{2,1,0:T(8,128)(2,1)S(1)}, u32[]{:S(2)}, u32[]{:S(2)}) collective-permute-start(bf16[2,32,1024]{2,1,0:T(8,128)(2,1)S(1)} %get-tuple-element.34.here_ref.beside_ref), channel_id=1, source_target_pairs={{0,2},{2,0},{4,6},{6,4},{8,10},{10,8},{12,14},{14,12},{1,3},{3,1},... | collective-permute-start | bytes 393224 | tf_op jit(solution)/shard_map/ppermute | solution.py:427
  4.4 7.7 %collective-permute-start.2 = (bf16[2,32,1024]{2,1,0:T(8,128)(2,1)S(1)}, bf16[2,32,1024]{2,1,0:T(8,128)(2,1)S(1)}, u32[]{:S(2)}, u32[]{:S(2)}) collective-permute-start(bf16[2,32,1024]{2,1,0:T(8,128)(2,1)S(1)} %get-tuple-element.35.beside_ref.here_ref), channel_id=1, source_target_pairs={{2,4},{4,2},{6,8},{8,6},{10,12},{12,10},{3,5},{5,3},{7,9},{9,7},{1... | collective-permute-start | bytes 393224 | tf_op jit(solution)/shard_map/ppermute | solution.py:428
  7.9 1.6 %copy-start = (bf16[64,4,1024]{2,1,0:T(4,128)(2,1)S(1)}, bf16[64,4,1024]{2,1,0:T(4,128)(2,1)}, u32[]{:S(2)}) copy-start(bf16[64,4,1024]{2,1,0:T(4,128)(2,1)} %refs_6_.3) | copy-start | bytes 1572868
  8.1 1.3 %collective-permute-start.1 = (f32[2,32,128]{2,1,0:T(8,128)S(1)}, f32[2,32,128]{2,1,0:T(8,128)S(1)}, u32[]{:S(2)}, u32[]{:S(2)}) collective-permute-start(f32[2,32,128]{2,1,0:T(8,128)S(1)} %get-tuple-element.36.rest_0_), channel_id=1, source_target_pairs={{0,1},{1,0},{2,3},{3,2},{4,5},{5,4},{6,7},{7,6},{8,9},{9,8},{10,11... | collective-permute-start | bytes 98312 | tf_op jit(solution)/shard_map/ppermute | solution.py:477
  12.3 1.3 %collective-permute-start.3 = (f32[2,32,128]{2,1,0:T(8,128)S(1)}, f32[2,32,128]{2,1,0:T(8,128)S(1)}, u32[]{:S(2)}, u32[]{:S(2)}) collective-permute-start(f32[2,32,128]{2,1,0:T(8,128)S(1)} %get-tuple-element.43.rest_0_), channel_id=1, source_target_pairs={{0,1},{1,0},{2,3},{3,2},{4,5},{5,4},{6,7},{7,6},{8,9},{9,8},{10,11... | collective-permute-start | bytes 98312 | tf_op jit(solution)/shard_map/ppermute | solution.py:477
  16.5 15.3 %collective-permute-start.4 = (bf16[33,4,1024]{2,1,0:T(4,128)(2,1)S(1)}, bf16[33,4,1024]{2,1,0:T(4,128)(2,1)S(1)}, u32[]{:S(2)}, u32[]{:S(2)}) collective-permute-start(bf16[33,4,1024]{2,1,0:T(4,128)(2,1)S(1)} %get-tuple-element.50), channel_id=1, source_target_pairs={{0,2},{2,0},{4,6},{6,4},{8,10},{10,8},{12,14},{14,12},{1,3},{3,1},... | collective-permute-start | bytes 811016 | tf_op jit(solution)/shard_map/ppermute | solution.py:507
  19.9 11.9 %collective-permute-start.5 = (bf16[33,4,1024]{2,1,0:T(4,128)(2,1)S(1)}, bf16[33,4,1024]{2,1,0:T(4,128)(2,1)S(1)}, u32[]{:S(2)}, u32[]{:S(2)}) collective-permute-start(bf16[33,4,1024]{2,1,0:T(4,128)(2,1)S(1)} %get-tuple-element.51), channel_id=1, source_target_pairs={{2,4},{4,2},{6,8},{8,6},{10,12},{12,10},{3,5},{5,3},{7,9},{9,7},{1... | collective-permute-start | bytes 811016 | tf_op jit(solution)/shard_map/ppermute | solution.py:507
  20.6 15.2 %collective-permute-start.6 = (bf16[33,4,1024]{2,1,0:T(4,128)(2,1)S(1)}, bf16[33,4,1024]{2,1,0:T(4,128)(2,1)S(1)}, u32[]{:S(2)}, u32[]{:S(2)}) collective-permute-start(bf16[33,4,1024]{2,1,0:T(4,128)(2,1)S(1)} %get-tuple-element.54), channel_id=1, source_target_pairs={{0,4},{4,0},{2,6},{6,2},{8,12},{12,8},{10,14},{14,10},{1,5},{5,1},... | collective-permute-start | bytes 811016 | tf_op jit(solution)/shard_map/ppermute | solution.py:507
  23.4 0.8 %copy-start.1 = (s32[4,2]{0,1:T(2,128)S(1)}, s32[4,2]{0,1:T(2,128)}, u32[]{:S(2)}) copy-start(s32[4,2]{0,1:T(2,128)} %param.21) | copy-start | bytes 100
  23.4 12.3 %collective-permute-start.7 = (bf16[33,4,1024]{2,1,0:T(4,128)(2,1)S(1)}, bf16[33,4,1024]{2,1,0:T(4,128)(2,1)S(1)}, u32[]{:S(2)}, u32[]{:S(2)}) collective-permute-start(bf16[33,4,1024]{2,1,0:T(4,128)(2,1)S(1)} %get-tuple-element.55), channel_id=1, source_target_pairs={{4,8},{8,4},{6,10},{10,6},{5,9},{9,5},{7,11},{11,7},{20,24},{24,20... | collective-permute-start | bytes 811016 | tf_op jit(solution)/shard_map/ppermute | solution.py:507

commit v4 on v3

--- a/solution.py
+++ b/solution.py
@@ -73,6 +73,7 @@
 
 def store_bands(taps, out_ref, first):
     depth, width = out_ref.shape[1], out_ref.shape[2]
+    taps = jnp.concatenate([taps, jnp.zeros((1, LANES - taps.shape[1]), F32)], axis=1)
     base = taps
     if width > LANES:
         base = jnp.concatenate([taps, jnp.zeros((1, width - LANES), F32)], axis=1)
@@ -135,41 +136,24 @@
         out_ref[table * size[0] : (table + 1) * size[0], k * nodes : (k + 1) * nodes] = part.astype(BF16)
 
 
-def early_kernel(
-    shape,
-    gain_ref,
-    path_ref,
-    albedo_ref,
-    taps_ref,
-    vapour_ref,
-    class_ref,
-    frac_ref,
-    lut_ref,
-    rows_ref,
-    cols_ref,
-    vapour_out_ref,
-    class_out_ref,
-    frac_out_ref,
-    tables_in,
-    taps_in,
-    sems,
-):
-    tables = [(source, tables_in.at[k]) for k, source in enumerate((gain_ref, path_ref, albedo_ref))]
-    others = [(vapour_ref, vapour_out_ref), (class_ref, class_out_ref), (frac_ref, frac_out_ref)]
-    pairs = [(taps_ref, taps_in)] + tables + others
+def early_kernel(taps_ref, *refs):
+    count = (len(refs) - 3) // 2
+    sources, results, (rows_ref, taps_out_ref, sems) = refs[:count], refs[count : 2 * count], refs[2 * count :]
+    pairs = [(taps_ref, taps_out_ref)] + list(zip(sources, results))
     copies = [pltpu.make_async_copy(source, into, sems.at[k]) for k, (source, into) in enumerate(pairs)]
     for copy in copies:
         copy.start()
     copies[0].wait()
-    taps = taps_in[...]
-    taps = jnp.concatenate([taps, jnp.zeros((1, LANES - taps.shape[1]), F32)], axis=1)
-    store_bands(taps, rows_ref, rows_ref.shape[1] - 30)
-    store_bands(taps, cols_ref, LANES - 30)
-    for table in range(3):
-        copies[1 + table].wait()
-        store_table(tables_in[table], lut_ref, table, shape)
-    for copy in copies[4:]:
+    store_bands(taps_out_ref[...], rows_ref, rows_ref.shape[1] - 30)
+    for copy in copies[1:]:
         copy.wait()
+
+
+def tables_kernel(shape, taps_ref, gain_ref, path_ref, albedo_ref, *rest):
+    lut_ref, cols_ref = rest[-2:]
+    store_bands(taps_ref[...], cols_ref, LANES - 30)
+    for number, table_ref in enumerate((gain_ref, path_ref, albedo_ref)):
+        store_table(table_ref[...], lut_ref, number, shape)
 
 
 def hats_kernel(flip, vapour_ref, class_ref, frac_ref, *rest):
@@ -433,26 +417,21 @@
     )
     tables = [table.transpose(0, 1, 3, 2).reshape(-1, levels_a) for table in (lut_gain, lut_path, lut_albedo)]
     whole = jax.ShapeDtypeStruct((rows, cols), F32)
-    lut, row_bands, col_bands, vapours, classes, fracs = pl.pallas_call(
-        functools.partial(early_kernel, (bands, levels_e, levels_w, levels_a)),
+    whole_int = jax.ShapeDtypeStruct((rows, cols), jnp.int32)
+    brought = [jax.ShapeDtypeStruct(table.shape, BF16) for table in tables] + [whole, whole_int, whole]
+    *tables, vapours, classes, fracs, row_bands, taps = pl.pallas_call(
+        early_kernel,
         out_shape=(
-            jax.ShapeDtypeStruct((6 * levels_e * bands, 2 * nodes), BF16),
+            *brought,
             jax.ShapeDtypeStruct((2, half, 3 * half), BF16),
-            jax.ShapeDtypeStruct((2, block, block + 2 * LANES), BF16),
-            whole,
-            jax.ShapeDtypeStruct((rows, cols), jnp.int32),
-            whole,
+            jax.ShapeDtypeStruct((1, kernel.shape[0]), F32),
         ),
         in_specs=[HBM] * 7,
-        out_specs=(VMEM,) * 6,
-        scratch_shapes=[
-            pltpu.VMEM((3, bands * levels_e * levels_w, levels_a), BF16),
-            pltpu.VMEM((1, kernel.shape[0]), F32),
-            pltpu.SemaphoreType.DMA((7,)),
-        ],
+        out_specs=(VMEM,) * 8,
+        scratch_shapes=[pltpu.SemaphoreType.DMA((7,))],
         compiler_params=params(),
         name="early",
-    )(*in_hbm(*tables, kernel[None, :], vapour, elev_class, elev_frac))
+    )(*in_hbm(kernel[None, :], *tables, vapour, elev_class, elev_frac))
 
     def smooth_rows(flip, here, beside, incoming, *after):
         ext, edge = pl.pallas_call(
@@ -474,11 +453,23 @@
             compiler_params=params(),
             name="hats",
         )(vapours, classes, fracs, edge)
-        return lax.ppermute(edge, "across", swap_pairs(lax.axis_size("across"), 1, 0)), ext, *hats
+        return edge, lax.ppermute(edge, "across", swap_pairs(lax.axis_size("across"), 1, 0)), ext, *hats
 
 
     corrected = jax.ShapeDtypeStruct((half, bands, cols), BF16)
     scratch = [pltpu.VMEM((half, cols), F32)]
+    sent, *near = smooth_rows(0, near_out, far_out, near_in)
+    lut, col_bands = pl.pallas_call(
+        functools.partial(tables_kernel, (bands, levels_e, levels_w, levels_a)),
+        out_shape=(
+            jax.ShapeDtypeStruct((6 * levels_e * bands, 2 * nodes), BF16),
+            jax.ShapeDtypeStruct((2, block, block + 2 * LANES), BF16),
+        ),
+        in_specs=[VMEM] * 5,
+        out_specs=(VMEM, VMEM),
+        compiler_params=params(),
+        name="tables",
+    )(taps, *tables, sent)
     near_corr = pl.pallas_call(
         correct_near_kernel,
         out_shape=corrected,
@@ -487,8 +478,8 @@
         scratch_shapes=scratch,
         compiler_params=params(),
         name="correct_near",
-    )(col_bands, lut, *smooth_rows(0, near_out, far_out, near_in), toa_bands, classes)
-    far = smooth_rows(1, far_out, near_out, far_in, near_corr)
+    )(col_bands, lut, *near, toa_bands, classes)
+    _, *far = smooth_rows(1, far_out, near_out, far_in, near_corr)
     segments = rows // SEG
     slots = jax.ShapeDtypeStruct((CAP * SEG + 1, bands, cols), BF16)
     far_corr, *sides = pl.pallas_call(
@@ -503,9 +494,10 @@
         name="correct_far",
     )(*in_hbm(routes.T, starts.T), col_bands, lut, *far, toa_bands, classes, near_corr)
     moves = ((1, 0), (1, 1), (2, 0), (2, 1))
-    got = [
-        lax.ppermute(side, "along", swap_pairs(count, step, offset)) for side, (step, offset) in zip(sides, moves)
-    ]
+    got = [None] * 4
+    for k in [0, 2, 1, 3]:
+        step, offset = moves[k]
+        got[k] = lax.ppermute(sides[k], "along", swap_pairs(count, step, offset))
     total = jax.ShapeDtypeStruct((rows, bands, cols), F32)
     counts = jax.ShapeDtypeStruct((rows, LANES), F32)
     acc, number = pl.pallas_call(
@@ -524,7 +516,7 @@
         input_output_aliases={0: 0, 1: 1},
         compiler_params=params(),
         name="add",
-    )(acc, number, got[0], got[1])
+    )(acc, number, got[0], got[2])
     _, out = pl.pallas_call(
         last_kernel,
         out_shape=(total, jax.ShapeDtypeStruct((rows, bands, cols), BF16)),
@@ -538,7 +530,7 @@
         input_output_aliases={0: 0},
         compiler_params=params(),
         name="last",
-    )(acc, number, got[2], got[3])
+    )(acc, number, got[1], got[3])
     return out[None]
 
 

time: 37 us -> 35.6 us (0.962)
  the two profiles are of different devices: /device:TPU:0 before, /device:TPU:20 now
where the time goes in v4:
time: 35.6 us; the launch traced here: 35.3 us
  starting transfers between devices  13.4 us (38%)
  Pallas kernels  11.5 us (32%)
  waiting for transfers between devices  10.3 us (29%)
    ppermute x4, waiting for transfers between devices, body(): got[k] = lax.ppermute(sides[k], 'along', swap_pairs(count, step, offset))  9.01 us
    ppermute x4, starting transfers between devices, body(): got[k] = lax.ppermute(sides[k], 'along', swap_pairs(count, step, offset))  7.91 us
    ppermute x1, starting transfers between devices, body(): far_in = lax.ppermute(far_out, 'along', swap_pairs(count, 1, 1))  4.43 us
    pallas_call x1, Pallas kernels, body(): pl.pallas_call(correct_far_kernel, out_shape=(corrected,) + (slots,) * 4,...  2.86 us
    pallas_call x1, Pallas kernels, body(): pl.pallas_call(correct_near_kernel, out_shape=corrected, in_specs=[VMEM]...  2.62 us
    pallas_call x1, Pallas kernels, body(): pl.pallas_call(prep_kernel, out_shape=(fields, fields), in_specs=[HBM, HB...  1.32 us
    pallas_call x1, Pallas kernels, body(): pl.pallas_call(early_kernel, out_shape=(*brought, jax.ShapeDtypeStruct((2...  1.3 us
    ppermute x2, waiting for transfers between devices, smooth_rows(): lax.ppermute(edge, 'across', swap_pairs(lax.axis_size('across'), 1, 0))  1.24 us
  transfers between devices with their start and end apart: 8, of which 5 were waited for; matrix products, arithmetic and copies ran while one was open for 0% of the time, Pallas kernels for 17%

profile of v4, /device:TPU:20, one launch (start us, length us, event | category | flops | bytes accessed | tf_op | source)
XLA Modules:
  0.0 35.3 jit_solution(13792356204470006496)
XLA Ops:
  0.0 1.3 %prep.1 = (bf16[2,32,1024]{2,1,0:T(8,128)(2,1)S(1)}, bf16[2,32,1024]{2,1,0:T(8,128)(2,1)S(1)}) custom-call(bf16[64,4,1024]{2,1,0:T(4,128)(2,1)} %refs_6_.3, s32[64,1024]{1,0:T(8,128)} %dark_ref.1), custom_call_target="tpu_custom_call" | custom-call | tf_op jit(solution)/shard_map/prep/pallas_call | solution.py:398
  1.3 0.6 %collective-permute-start = (bf16[2,32,1024]{2,1,0:T(8,128)(2,1)S(1)}, bf16[2,32,1024]{2,1,0:T(8,128)(2,1)S(1)}, u32[]{:S(2)}, u32[]{:S(2)}) collective-permute-start(bf16[2,32,1024]{2,1,0:T(8,128)(2,1)S(1)} %get-tuple-element.40.here_ref.beside_ref), channel_id=1, source_target_pairs={{0,2},{2,0},{4,6},{6,4},{8,10},{10,8},{12,14},{14,12},{1,3},{3,1},... | collective-permute-start | bytes 393224 | tf_op jit(solution)/shard_map/ppermute | solution.py:411
  1.9 4.4 %collective-permute-start.2 = (bf16[2,32,1024]{2,1,0:T(8,128)(2,1)S(1)}, bf16[2,32,1024]{2,1,0:T(8,128)(2,1)S(1)}, u32[]{:S(2)}, u32[]{:S(2)}) collective-permute-start(bf16[2,32,1024]{2,1,0:T(8,128)(2,1)S(1)} %get-tuple-element.41.beside_ref.here_ref), channel_id=1, source_target_pairs={{2,4},{4,2},{6,8},{8,6},{10,12},{12,10},{3,5},{5,3},{7,9},{9,7},{1... | collective-permute-start | bytes 393224 | tf_op jit(solution)/shard_map/ppermute | solution.py:412
  6.3 1.3 %early.1 = (bf16[256,16]{1,0:T(8,128)(2,1)S(1)}, bf16[256,16]{1,0:T(8,128)(2,1)S(1)}, bf16[256,16]{1,0:T(8,128)(2,1)S(1)}, f32[64,1024]{1,0:T(8,128)S(1)}, s32[6...) custom-call(f32[1,61]{1,0:T(1,128)} %bitcast.19, ...), custom_call_target="tpu_custom_call" | custom-call | tf_op jit(solution)/shard_map/early/pallas_call | solution.py:422
  7.7 0.3 vertical.2
  7.9 0.1 collective-permute-start.1
  8.0 0.2 hats.2
  8.3 0.4 %tables.1 = (bf16[192,256]{1,0:T(8,128)(2,1)S(1)}, bf16[2,256,512]{2,1,0:T(8,128)(2,1)S(1)}) custom-call(f32[1,61]{1,0:T(1,128)S(1)} %get-tuple-element.35.taps_ref, bf16[256,16]{1,0:T(8,128)(2,1)S(1)} %get-tuple-element.36.gain_ref, bf16[256,16]{1,0:T(8,128)(2,1)S(1)} %get-tuple-element.37.path_ref, bf16[256,16]{1,0:T(8,128)(2,1)S(1)} %get-tuple-element.38.albedo_ref, ...), custom_call_target="tpu_custom_call" | custom-call | tf_op jit(solution)/shard_map/tables/pallas_call | solution.py:462
  8.6 0.6 %collective-permute-done.1.refs_2_ = f32[2,32,128]{2,1,0:T(8,128)S(1)} collective-permute-done((f32[2,32,128]{2,1,0:T(8,128)S(1)}, f32[2,32,128]{2,1,0:T(8,128)S(1)}, u32[]{:S(2)}, u32[]{:S(2)}) %collective-permute-start.1) | collective-permute-done | bytes 32800 | tf_op jit(solution)/shard_map/ppermute | solution.py:456
  9.2 2.6 %correct_near.1.rest_0_.refs_8_.near_ref = bf16[32,4,1024]{2,1,0:T(4,128)(2,1)S(1)} custom-call(bf16[2,256,512]{2,1,0:T(8,128)(2,1)S(1)} %get-tuple-element.43.refs_0_, bf16[192,256]{1,0:T(8,128)(2,1)S(1)} %get-tuple-element.44.refs_1_, f32[2,32,128]{2,1,0:T(8,128)S(1)} %collective-permute-done.1.refs_2_, ...), custom_call_target="tpu_custom_call" | custom-call | tf_op jit(solution)/shard_map/correct_near/pallas_call | solution.py:473
  11.9 0.3 vertical.3
  12.1 0.4 %collective-permute-start.3 = (f32[2,32,128]{2,1,0:T(8,128)S(1)}, f32[2,32,128]{2,1,0:T(8,128)S(1)}, u32[]{:S(2)}, u32[]{:S(2)}) collective-permute-start(f32[2,32,128]{2,1,0:T(8,128)S(1)} %get-tuple-element.51.rest_0_), channel_id=1, source_target_pairs={{0,1},{1,0},{2,3},{3,2},{4,5},{5,4},{6,7},{7,6},{8,9},{9,8},{10,11... | collective-permute-start | bytes 98312 | tf_op jit(solution)/shard_map/ppermute | solution.py:456
  12.5 0.2 hats.3
  12.7 0.7 %collective-permute-done.3.refs_2_ = f32[2,32,128]{2,1,0:T(8,128)S(1)} collective-permute-done((f32[2,32,128]{2,1,0:T(8,128)S(1)}, f32[2,32,128]{2,1,0:T(8,128)S(1)}, u32[]{:S(2)}, u32[]{:S(2)}) %collective-permute-start.3) | collective-permute-done | bytes 32800 | tf_op jit(solution)/shard_map/ppermute | solution.py:456
  13.4 2.9 %correct_far.1 = (bf16[32,4,1024]{2,1,0:T(4,128)(2,1)S(1)}, bf16[33,4,1024]{2,1,0:T(4,128)(2,1)S(1)}, bf16[33,4,1024]{2,1,0:T(4,128)(2,1)S(1)}, bf16[33,4,1024]{2,1,0:T(4,128)(2,1)S(1)}, bf16[33,4,1024]{2,1,0:T(4,128)(2,1)S(1)}) custom-call(s32[2,4]{1,0:T(2,128)} %bitcast.18, s32[2,4]{1,0:T(2,128)} %bitcast.13, ...), custom_call_target="tpu_custom_call" | custom-call | tf_op jit(solution)/shard_map/correct_far/pallas_call | solution.py:485
  16.4 1.1 %collective-permute-start.5 = (bf16[33,4,1024]{2,1,0:T(4,128)(2,1)S(1)}, bf16[33,4,1024]{2,1,0:T(4,128)(2,1)S(1)}, u32[]{:S(2)}, u32[]{:S(2)}) collective-permute-start(bf16[33,4,1024]{2,1,0:T(4,128)(2,1)S(1)} %get-tuple-element.59), channel_id=1, source_target_pairs={{0,4},{4,0},{2,6},{6,2},{8,12},{12,8},{10,14},{14,10},{1,5},{5,1},... | collective-permute-start | bytes 811016 | tf_op jit(solution)/shard_map/ppermute | solution.py:500
  17.4 4.3 %collective-permute-start.6 = (bf16[33,4,1024]{2,1,0:T(4,128)(2,1)S(1)}, bf16[33,4,1024]{2,1,0:T(4,128)(2,1)S(1)}, u32[]{:S(2)}, u32[]{:S(2)}) collective-permute-start(bf16[33,4,1024]{2,1,0:T(4,128)(2,1)S(1)} %get-tuple-element.62), channel_id=1, source_target_pairs={{2,4},{4,2},{6,8},{8,6},{10,12},{12,10},{3,5},{5,3},{7,9},{9,7},{1... | collective-permute-start | bytes 811016 | tf_op jit(solution)/shard_map/ppermute | solution.py:500
  21.7 2.5 %collective-permute-start.7 = (bf16[33,4,1024]{2,1,0:T(4,128)(2,1)S(1)}, bf16[33,4,1024]{2,1,0:T(4,128)(2,1)S(1)}, u32[]{:S(2)}, u32[]{:S(2)}) collective-permute-start(bf16[33,4,1024]{2,1,0:T(4,128)(2,1)S(1)} %get-tuple-element.63), channel_id=1, source_target_pairs={{4,8},{8,4},{6,10},{10,6},{5,9},{9,5},{7,11},{11,7},{20,24},{24,20... | collective-permute-start | bytes 811016 | tf_op jit(solution)/shard_map/ppermute | solution.py:500
  24.2 0.7 %own.1 = (f32[64,4,1024]{2,1,0:T(4,128)S(1)}, f32[64,128]{1,0:T(8,128)S(1)}) custom-call(s32[2,4]{1,0:T(2,128)S(1)} %bitcast.14, bf16[32,4,1024]{2,1,0:T(4,128)(2,1)S(1)} %correct_near.1.rest_0_.refs_8_.near_ref, bf16[32,4,1024]{2,1,0:T(4,128)(2,1)S(1)} %get-tuple-element.55.far_ref), custom_call_target="tpu_custom_call" | custom-call | tf_op jit(solution)/shard_map/own/pallas_call | solution.py:503
  25.0 3.6 %collective-permute-done.4.side0_ref = bf16[33,4,1024]{2,1,0:T(4,128)(2,1)S(1)} collective-permute-done((bf16[33,4,1024]{2,1,0:T(4,128)(2,1)S(1)}, bf16[33,4,1024]{2,1,0:T(4,128)(2,1)S(1)}, u32[]{:S(2)}, u32[]{:S(2)}) %collective-permute-start.4) | collective-permute-done | bytes 270368 | tf_op jit(solution)/shard_map/ppermute | solution.py:500
  28.6 0.3 add.1
  28.9 3.2 %collective-permute-done.6.side0_ref = bf16[33,4,1024]{2,1,0:T(4,128)(2,1)S(1)} collective-permute-done((bf16[33,4,1024]{2,1,0:T(4,128)(2,1)S(1)}, bf16[33,4,1024]{2,1,0:T(4,128)(2,1)S(1)}, u32[]{:S(2)}, u32[]{:S(2)}) %collective-permute-start.6) | collective-permute-done | bytes 270368 | tf_op jit(solution)/shard_map/ppermute | solution.py:500
  32.1 2.2 %collective-permute-done.7.side1_ref = bf16[33,4,1024]{2,1,0:T(4,128)(2,1)S(1)} collective-permute-done((bf16[33,4,1024]{2,1,0:T(4,128)(2,1)S(1)}, bf16[33,4,1024]{2,1,0:T(4,128)(2,1)S(1)}, u32[]{:S(2)}, u32[]{:S(2)}) %collective-permute-start.7) | collective-permute-done | bytes 270368 | tf_op jit(solution)/shard_map/ppermute | solution.py:500
  34.2 1.1 %last.1 = (f32[64,4,1024]{2,1,0:T(4,128)S(1)}, bf16[64,4,1024]{2,1,0:T(4,128)(2,1)}) custom-call(f32[64,4,1024]{2,1,0:T(4,128)S(1)} %get-tuple-element.60.acc_in_ref, f32[64,128]{1,0:T(8,128)S(1)} %get-tuple-element.61.count_in_ref, bf16[33,4,1024]{2,1,0:T(4,128)(2,1)S(1)} %collective-permute-done.6.side0_ref, ...), custom_call_target="tpu_custom_call", output_to_operand_aliasing={{0}: (0, {})} | custom-call | tf_op jit(solution)/shard_map/last/pallas_call | solution.py:520
  (8 shorter events, 0.1 us)
Async XLA Ops:
  1.3 6.3 %collective-permute-start = (bf16[2,32,1024]{2,1,0:T(8,128)(2,1)S(1)}, bf16[2,32,1024]{2,1,0:T(8,128)(2,1)S(1)}, u32[]{:S(2)}, u32[]{:S(2)}) collective-permute-start(bf16[2,32,1024]{2,1,0:T(8,128)(2,1)S(1)} %get-tuple-element.40.here_ref.beside_ref), channel_id=1, source_target_pairs={{0,2},{2,0},{4,6},{6,4},{8,10},{10,8},{12,14},{14,12},{1,3},{3,1},... | collective-permute-start | bytes 393224 | tf_op jit(solution)/shard_map/ppermute | solution.py:411
  1.9 9.9 %collective-permute-start.2 = (bf16[2,32,1024]{2,1,0:T(8,128)(2,1)S(1)}, bf16[2,32,1024]{2,1,0:T(8,128)(2,1)S(1)}, u32[]{:S(2)}, u32[]{:S(2)}) collective-permute-start(bf16[2,32,1024]{2,1,0:T(8,128)(2,1)S(1)} %get-tuple-element.41.beside_ref.here_ref), channel_id=1, source_target_pairs={{2,4},{4,2},{6,8},{8,6},{10,12},{12,10},{3,5},{5,3},{7,9},{9,7},{1... | collective-permute-start | bytes 393224 | tf_op jit(solution)/shard_map/ppermute | solution.py:412
  7.9 1.3 %collective-permute-start.1 = (f32[2,32,128]{2,1,0:T(8,128)S(1)}, f32[2,32,128]{2,1,0:T(8,128)S(1)}, u32[]{:S(2)}, u32[]{:S(2)}) collective-permute-start(f32[2,32,128]{2,1,0:T(8,128)S(1)} %get-tuple-element.42.rest_0_), channel_id=1, source_target_pairs={{0,1},{1,0},{2,3},{3,2},{4,5},{5,4},{6,7},{7,6},{8,9},{9,8},{10,11... | collective-permute-start | bytes 98312 | tf_op jit(solution)/shard_map/ppermute | solution.py:456
  8.0 1.2 %copy-start = (bf16[64,4,1024]{2,1,0:T(4,128)(2,1)S(1)}, bf16[64,4,1024]{2,1,0:T(4,128)(2,1)}, u32[]{:S(2)}) copy-start(bf16[64,4,1024]{2,1,0:T(4,128)(2,1)} %refs_6_.3) | copy-start | bytes 1572868
  12.1 1.3 %collective-permute-start.3 = (f32[2,32,128]{2,1,0:T(8,128)S(1)}, f32[2,32,128]{2,1,0:T(8,128)S(1)}, u32[]{:S(2)}, u32[]{:S(2)}) collective-permute-start(f32[2,32,128]{2,1,0:T(8,128)S(1)} %get-tuple-element.51.rest_0_), channel_id=1, source_target_pairs={{0,1},{1,0},{2,3},{3,2},{4,5},{5,4},{6,7},{7,6},{8,9},{9,8},{10,11... | collective-permute-start | bytes 98312 | tf_op jit(solution)/shard_map/ppermute | solution.py:456
  16.3 12.3 %collective-permute-start.4 = (bf16[33,4,1024]{2,1,0:T(4,128)(2,1)S(1)}, bf16[33,4,1024]{2,1,0:T(4,128)(2,1)S(1)}, u32[]{:S(2)}, u32[]{:S(2)}) collective-permute-start(bf16[33,4,1024]{2,1,0:T(4,128)(2,1)S(1)} %get-tuple-element.58), channel_id=1, source_target_pairs={{0,2},{2,0},{4,6},{6,4},{8,10},{10,8},{12,14},{14,12},{1,3},{3,1},... | collective-permute-start | bytes 811016 | tf_op jit(solution)/shard_map/ppermute | solution.py:500
  16.4 12.2 %collective-permute-start.5 = (bf16[33,4,1024]{2,1,0:T(4,128)(2,1)S(1)}, bf16[33,4,1024]{2,1,0:T(4,128)(2,1)S(1)}, u32[]{:S(2)}, u32[]{:S(2)}) collective-permute-start(bf16[33,4,1024]{2,1,0:T(4,128)(2,1)S(1)} %get-tuple-element.59), channel_id=1, source_target_pairs={{0,4},{4,0},{2,6},{6,2},{8,12},{12,8},{10,14},{14,10},{1,5},{5,1},... | collective-permute-start | bytes 811016 | tf_op jit(solution)/shard_map/ppermute | solution.py:500
  17.4 14.6 %collective-permute-start.6 = (bf16[33,4,1024]{2,1,0:T(4,128)(2,1)S(1)}, bf16[33,4,1024]{2,1,0:T(4,128)(2,1)S(1)}, u32[]{:S(2)}, u32[]{:S(2)}) collective-permute-start(bf16[33,4,1024]{2,1,0:T(4,128)(2,1)S(1)} %get-tuple-element.62), channel_id=1, source_target_pairs={{2,4},{4,2},{6,8},{8,6},{10,12},{12,10},{3,5},{5,3},{7,9},{9,7},{1... | collective-permute-start | bytes 811016 | tf_op jit(solution)/shard_map/ppermute | solution.py:500
  21.7 2.5 %copy-start.1 = (s32[4,2]{0,1:T(2,128)S(1)}, s32[4,2]{0,1:T(2,128)}, u32[]{:S(2)}) copy-start(s32[4,2]{0,1:T(2,128)} %param.21) | copy-start | bytes 100
  21.7 12.5 %collective-permute-start.7 = (bf16[33,4,1024]{2,1,0:T(4,128)(2,1)S(1)}, bf16[33,4,1024]{2,1,0:T(4,128)(2,1)S(1)}, u32[]{:S(2)}, u32[]{:S(2)}) collective-permute-start(bf16[33,4,1024]{2,1,0:T(4,128)(2,1)S(1)} %get-tuple-element.63), channel_id=1, source_target_pairs={{4,8},{8,4},{6,10},{10,6},{5,9},{9,5},{7,11},{11,7},{20,24},{24,20... | collective-permute-start | bytes 811016 | tf_op jit(solution)/shard_map/ppermute | solution.py:500

commit v5 on v4

--- a/solution.py
+++ b/solution.py
@@ -167,24 +167,9 @@
     even_ref[...] = jnp.where(class_ref[here] % 2 == 0, 1.0 - frac, frac)
 
 
-def correct_rows(
-    flip,
-    bands_ref,
-    lut_ref,
-    edge_ref,
-    ext_ref,
-    hat_ref,
-    even_ref,
-    toa_ref,
-    class_ref,
-    corr_ref,
-    pos_ref,
-):
+def smooth_cols(bands_ref, edge_ref, ext_ref, pos_ref, levels_a):
     rows, cols = pos_ref.shape
-    base = pl.multiple_of(jnp.where(is_half(flip), rows, 0), rows)
     left = lax.axis_index("across") == 0
-    levels_w = hat_ref.shape[0]
-    levels_a = lut_ref.shape[1] // (2 * levels_w)
     block = bands_ref.shape[1]
     window = bands_ref.shape[2]
     lines = []
@@ -211,6 +196,13 @@
         aerosol = weighted / jnp.maximum(darkness, 1.0)
         pos_ref[:, at] = (levels_a - 1.0) / (1.0 + jnp.exp(-aerosol))
 
+
+def correct_rows(flip, first, lut_ref, hat_ref, even_ref, pos_ref, toa_ref, class_ref, corr_ref):
+    rows = corr_ref.shape[0]
+    half, cols = pos_ref.shape
+    base = pl.multiple_of(jnp.where(is_half(flip), half, 0) + first, rows)
+    levels_w = hat_ref.shape[0]
+    levels_a = lut_ref.shape[1] // (2 * levels_w)
     step = 256
     node_a = lax.broadcasted_iota(jnp.int32, (levels_a, step), 0).astype(F32)
     second = lax.broadcasted_iota(jnp.int32, (8, step), 0) >= 4
@@ -220,19 +212,18 @@
         at = slice(number * step, (number + 1) * step)
         pieces = []
         for k in range(2):
-            one = pl.ds(row + k, 1)
-            hat_a = jnp.maximum(0.0, 1.0 - jnp.abs(pos_ref[one, at] - node_a)).astype(BF16)
+            hat_a = jnp.maximum(0.0, 1.0 - jnp.abs(pos_ref[pl.ds(first + row + k, 1), at] - node_a)).astype(BF16)
             pieces += [
-                hat_a * jnp.broadcast_to(hat_ref[w, one, at], (levels_a, step)).astype(BF16) for w in range(levels_w)
+                hat_a * jnp.broadcast_to(hat_ref[w, pl.ds(first + row + k, 1), at], (levels_a, step)).astype(BF16) for w in range(levels_w)
             ]
         nodes = jnp.dot(lut, jnp.concatenate(pieces, axis=0), preferred_element_type=F32)
 
-        def both(ref, first):
-            one, two = (jnp.broadcast_to(ref[pl.ds(first + k, 1), at], (8, step)) for k in range(2))
+        def both(ref, begin):
+            one, two = (jnp.broadcast_to(ref[pl.ds(begin + k, 1), at], (8, step)) for k in range(2))
             return jnp.where(second, two, one)
 
         level = both(class_ref, base + row)
-        w_even = both(even_ref, row)
+        w_even = both(even_ref, first + row)
         w_odd = 1.0 - w_even
         below = [level < k for k in range(7)]
 
@@ -263,32 +254,40 @@
     lax.fori_loop(0, rows // group, group_step, 0)
 
 
-def correct_near_kernel(*refs):
-    correct_rows(0, *refs)
-
-
-def segment_list(near_ref, far_ref):
+def near_kernel(levels_a, bands_ref, lut_ref, edge_ref, ext_ref, hat_ref, even_ref, toa_ref, class_ref, corr_ref, pos_ref):
+    smooth_cols(bands_ref, edge_ref, ext_ref, pos_ref, levels_a)
+    correct_rows(0, 0, lut_ref, hat_ref, even_ref, pos_ref, toa_ref, class_ref, corr_ref)
+
+
+def next_kernel(first, lut_ref, hat_ref, even_ref, pos_ref, toa_ref, class_ref, *rest):
+    correct_rows(0, first, lut_ref, hat_ref, even_ref, pos_ref, toa_ref, class_ref, rest[-1])
+
+
+def segment_list(near_refs, far_ref):
     each = far_ref.shape[0] // SEG
     shift = jnp.where(is_half(0), each, 0)
-    return [(shift + k, near_ref, k) for k in range(each)] + [(each - shift + k, far_ref, k) for k in range(each)]
-
-
-def correct_far_kernel(routes_in_ref, starts_in_ref, *refs):
-    near_ref, corr_ref, sides = refs[8], refs[9], refs[10:14]
-    pos_ref, routes_ref, starts_ref, sems = refs[14:]
+    near = [(shift + k, near_refs[k], 0) for k in range(each)]
+    return near + [(each - shift + k, far_ref, k) for k in range(each)]
+
+
+def correct_far_kernel(levels_a, routes_in_ref, starts_in_ref, *refs):
+    near_refs, corr_ref, sides = refs[8:-9], refs[-9], refs[-8:-4]
+    pos_ref, routes_ref, starts_ref, sems = refs[-4:]
     copies = [
         pltpu.make_async_copy(routes_in_ref, routes_ref, sems.at[0]),
         pltpu.make_async_copy(starts_in_ref, starts_ref, sems.at[1]),
     ]
     for copy in copies:
         copy.start()
-    correct_rows(1, *refs[:8], corr_ref, pos_ref)
+    bands_ref, lut_ref, edge_ref, ext_ref, hat_ref, even_ref, toa_ref, class_ref = refs[:8]
+    smooth_cols(bands_ref, edge_ref, ext_ref, pos_ref, levels_a)
+    correct_rows(1, 0, lut_ref, hat_ref, even_ref, pos_ref, toa_ref, class_ref, corr_ref)
     for copy in copies:
         copy.wait()
     me = lax.axis_index("along")
     beside = 1 - 2 * (me % 2)
     beyond = 2 - 4 * ((me // 2) % 2)
-    listed = segment_list(near_ref, corr_ref)
+    listed = segment_list(near_refs, corr_ref)
     band = lax.broadcasted_iota(jnp.int32, corr_ref.shape[1:], 0)
     for target, out_ref in zip((me + beside, me - beside, me + beyond, me - beyond), sides):
         count = jnp.int32(0)
@@ -343,10 +342,11 @@
     return count
 
 
-def own_kernel(starts_ref, near_ref, far_ref, acc_ref, count_ref):
+def own_kernel(starts_ref, *refs):
+    far_ref, acc_ref, count_ref = refs[-3:]
     acc_ref[...] = jnp.zeros(acc_ref.shape, F32)
     count = jnp.zeros(count_ref.shape, F32)
-    listed = segment_list(near_ref, far_ref)
+    listed = segment_list(refs[:-3], far_ref)
     for segment, from_ref, place in listed:
         start = starts_ref[0, segment]
         count = count + covers(count.shape[0], start)
@@ -457,7 +457,6 @@
 
 
     corrected = jax.ShapeDtypeStruct((half, bands, cols), BF16)
-    scratch = [pltpu.VMEM((half, cols), F32)]
     sent, *near = smooth_rows(0, near_out, far_out, near_in)
     lut, col_bands = pl.pallas_call(
         functools.partial(tables_kernel, (bands, levels_e, levels_w, levels_a)),
@@ -470,29 +469,41 @@
         compiler_params=params(),
         name="tables",
     )(taps, *tables, sent)
-    near_corr = pl.pallas_call(
-        correct_near_kernel,
-        out_shape=corrected,
+    part = jax.ShapeDtypeStruct((SEG, bands, cols), BF16)
+    near_first, near_pos = pl.pallas_call(
+        functools.partial(near_kernel, levels_a),
+        out_shape=(part, jax.ShapeDtypeStruct((half, cols), F32)),
         in_specs=[VMEM] * 8,
-        out_specs=VMEM,
-        scratch_shapes=scratch,
+        out_specs=(VMEM, VMEM),
         compiler_params=params(),
         name="correct_near",
     )(col_bands, lut, *near, toa_bands, classes)
-    _, *far = smooth_rows(1, far_out, near_out, far_in, near_corr)
+    near_corr = [near_first]
+    sent, *far = smooth_rows(1, far_out, near_out, far_in, near_first)
+    for first in range(SEG, half, SEG):
+        near_corr.append(
+            pl.pallas_call(
+                functools.partial(next_kernel, first),
+                out_shape=part,
+                in_specs=[VMEM] * 7,
+                out_specs=VMEM,
+                compiler_params=params(),
+                name="correct_next",
+            )(lut, near[2], near[3], near_pos, toa_bands, classes, sent)
+        )
     segments = rows // SEG
     slots = jax.ShapeDtypeStruct((CAP * SEG + 1, bands, cols), BF16)
     far_corr, *sides = pl.pallas_call(
-        correct_far_kernel,
+        functools.partial(correct_far_kernel, levels_a),
         out_shape=(corrected,) + (slots,) * 4,
-        in_specs=[HBM, HBM] + [VMEM] * 9,
+        in_specs=[HBM, HBM] + [VMEM] * (8 + len(near_corr)),
         out_specs=(VMEM,) * 5,
-        scratch_shapes=scratch
+        scratch_shapes=[pltpu.VMEM((half, cols), F32)]
         + [pltpu.SMEM((2, segments), jnp.int32)] * 2
         + [pltpu.SemaphoreType.DMA((2,))],
         compiler_params=params(),
         name="correct_far",
-    )(*in_hbm(routes.T, starts.T), col_bands, lut, *far, toa_bands, classes, near_corr)
+    )(*in_hbm(routes.T, starts.T), col_bands, lut, *far, toa_bands, classes, *near_corr)
     moves = ((1, 0), (1, 1), (2, 0), (2, 1))
     got = [None] * 4
     for k in [0, 2, 1, 3]:
@@ -503,11 +514,11 @@
     acc, number = pl.pallas_call(
         own_kernel,
         out_shape=(total, counts),
-        in_specs=[SMEM, VMEM, VMEM],
+        in_specs=[SMEM] + [VMEM] * (1 + len(near_corr)),
         out_specs=(VMEM, VMEM),
         compiler_params=params(),
         name="own",
-    )(starts.T, near_corr, far_corr)
+    )(starts.T, *near_corr, far_corr)
     acc, number = pl.pallas_call(
         add_kernel,
         out_shape=(total, counts),

time: 35.6 us -> 35.1 us (0.986)
  waiting for transfers between devices: 10.3 us -> 9.46 us
    ppermute x2, waiting for transfers between devices: 1.24 us -> 0.58 us  [smooth_rows(): lax.ppermute(edge, 'across', swap_pairs(lax.axis_size('across'), 1, 0))]
    pallas_call x3 -> x4, Pallas kernels: 6.2 us -> 6.56 us  [the longest x1 2.88 us: body(): pl.pallas_call(functools.partial(correct_far_kernel, levels_a), out_shape...]
  transfers between devices with their start and end apart: 8 -> 8, of which waited for: 5 -> 4; matrix products, arithmetic and copies ran while one was open for 0% -> 0% of each run, Pallas kernels for 17% -> 18%
where the time goes in v5:
time: 35.1 us; the launch traced here: 34.9 us
  starting transfers between devices  13.4 us (38%)
  Pallas kernels  11.8 us (34%)
  waiting for transfers between devices  9.46 us (27%)
    ppermute x4, waiting for transfers between devices, body(): got[k] = lax.ppermute(sides[k], 'along', swap_pairs(count, step, offset))  8.88 us
    ppermute x4, starting transfers between devices, body(): got[k] = lax.ppermute(sides[k], 'along', swap_pairs(count, step, offset))  7.89 us
    ppermute x1, starting transfers between devices, body(): far_in = lax.ppermute(far_out, 'along', swap_pairs(count, 1, 1))  4.43 us
    pallas_call x1, Pallas kernels, body(): pl.pallas_call(functools.partial(correct_far_kernel, levels_a), out_shape...  2.88 us
    pallas_call x1, Pallas kernels, body(): pl.pallas_call(functools.partial(near_kernel, levels_a), out_shape=(part,...  1.85 us
    pallas_call x1, Pallas kernels, body(): pl.pallas_call(prep_kernel, out_shape=(fields, fields), in_specs=[HBM, HB...  1.32 us
    pallas_call x1, Pallas kernels, body(): pl.pallas_call(early_kernel, out_shape=(*brought, jax.ShapeDtypeStruct((2...  1.3 us
    pallas_call x1, Pallas kernels, body(): pl.pallas_call(functools.partial(next_kernel, first), out_shape=part, in_...  1.09 us
  transfers between devices with their start and end apart: 8, of which 4 were waited for; matrix products, arithmetic and copies ran while one was open for 0% of the time, Pallas kernels for 18%

profile of v5, /device:TPU:20, one launch (start us, length us, event | category | flops | bytes accessed | tf_op | source)
XLA Modules:
  0.0 34.9 jit_solution(14099258145912418209)
XLA Ops:
  0.0 1.3 %prep.1 = (bf16[2,32,1024]{2,1,0:T(8,128)(2,1)S(1)}, bf16[2,32,1024]{2,1,0:T(8,128)(2,1)S(1)}) custom-call(bf16[64,4,1024]{2,1,0:T(4,128)(2,1)} %refs_6_.1, s32[64,1024]{1,0:T(8,128)} %dark_ref.1), custom_call_target="tpu_custom_call" | custom-call | tf_op jit(solution)/shard_map/prep/pallas_call | solution.py:398
  1.3 0.6 %collective-permute-start = (bf16[2,32,1024]{2,1,0:T(8,128)(2,1)S(1)}, bf16[2,32,1024]{2,1,0:T(8,128)(2,1)S(1)}, u32[]{:S(2)}, u32[]{:S(2)}) collective-permute-start(bf16[2,32,1024]{2,1,0:T(8,128)(2,1)S(1)} %get-tuple-element.42.here_ref.beside_ref), channel_id=1, source_target_pairs={{0,2},{2,0},{4,6},{6,4},{8,10},{10,8},{12,14},{14,12},{1,3},{3,1},... | collective-permute-start | bytes 393224 | tf_op jit(solution)/shard_map/ppermute | solution.py:411
  1.9 4.4 %collective-permute-start.2 = (bf16[2,32,1024]{2,1,0:T(8,128)(2,1)S(1)}, bf16[2,32,1024]{2,1,0:T(8,128)(2,1)S(1)}, u32[]{:S(2)}, u32[]{:S(2)}) collective-permute-start(bf16[2,32,1024]{2,1,0:T(8,128)(2,1)S(1)} %get-tuple-element.43.beside_ref.here_ref), channel_id=1, source_target_pairs={{2,4},{4,2},{6,8},{8,6},{10,12},{12,10},{3,5},{5,3},{7,9},{9,7},{1... | collective-permute-start | bytes 393224 | tf_op jit(solution)/shard_map/ppermute | solution.py:412
  6.3 1.3 %early.1 = (bf16[256,16]{1,0:T(8,128)(2,1)S(1)}, bf16[256,16]{1,0:T(8,128)(2,1)S(1)}, bf16[256,16]{1,0:T(8,128)(2,1)S(1)}, f32[64,1024]{1,0:T(8,128)S(1)}, s32[6...) custom-call(f32[1,61]{1,0:T(1,128)} %bitcast.19, ...), custom_call_target="tpu_custom_call" | custom-call | tf_op jit(solution)/shard_map/early/pallas_call | solution.py:422
  7.7 0.3 vertical.2
  8.0 0.2 hats.2
  8.3 0.4 %tables.1 = (bf16[192,256]{1,0:T(8,128)(2,1)S(1)}, bf16[2,256,512]{2,1,0:T(8,128)(2,1)S(1)}) custom-call(f32[1,61]{1,0:T(1,128)S(1)} %get-tuple-element.37.taps_ref, bf16[256,16]{1,0:T(8,128)(2,1)S(1)} %get-tuple-element.38.gain_ref, bf16[256,16]{1,0:T(8,128)(2,1)S(1)} %get-tuple-element.39.path_ref, bf16[256,16]{1,0:T(8,128)(2,1)S(1)} %get-tuple-element.40.albedo_ref, ...), custom_call_target="tpu_custom_call" | custom-call | tf_op jit(solution)/shard_map/tables/pallas_call | solution.py:461
  8.6 0.6 %collective-permute-done.1.edge_ref = f32[2,32,128]{2,1,0:T(8,128)S(1)} collective-permute-done((f32[2,32,128]{2,1,0:T(8,128)S(1)}, f32[2,32,128]{2,1,0:T(8,128)S(1)}, u32[]{:S(2)}, u32[]{:S(2)}) %collective-permute-start.1) | collective-permute-done | bytes 32800 | tf_op jit(solution)/shard_map/ppermute | solution.py:456
  9.2 1.8 %correct_near.1 = (bf16[16,4,1024]{2,1,0:T(4,128)(2,1)S(1)}, f32[32,1024]{1,0:T(8,128)S(1)}) custom-call(bf16[2,256,512]{2,1,0:T(8,128)(2,1)S(1)} %get-tuple-element.45.bands_ref.refs_0_, bf16[192,256]{1,0:T(8,128)(2,1)S(1)} %get-tuple-element.46.lut_ref.refs_1_, f32[2,32,128]{2,1,0:T(8,128)S(1)} %collective-permute-done.1.edge_ref, ...), custom_call_target="tpu_custom_call" | custom-call | tf_op jit(solution)/shard_map/correct_near/pallas_call | solution.py:473
  11.1 0.3 vertical.3
  11.4 0.4 %collective-permute-start.3 = (f32[2,32,128]{2,1,0:T(8,128)S(1)}, f32[2,32,128]{2,1,0:T(8,128)S(1)}, u32[]{:S(2)}, u32[]{:S(2)}) collective-permute-start(f32[2,32,128]{2,1,0:T(8,128)S(1)} %get-tuple-element.55.rest_0_), channel_id=1, source_target_pairs={{0,1},{1,0},{2,3},{3,2},{4,5},{5,4},{6,7},{7,6},{8,9},{9,8},{10,11... | collective-permute-start | bytes 98312 | tf_op jit(solution)/shard_map/ppermute | solution.py:456
  11.8 0.2 hats.3
  12.0 1.1 %correct_next.1.refs_9_.refs_1_ = bf16[16,4,1024]{2,1,0:T(4,128)(2,1)S(1)} custom-call(bf16[192,256]{1,0:T(8,128)(2,1)S(1)} %get-tuple-element.46.lut_ref.refs_1_, f32[8,32,1024]{2,1,0:T(8,128)S(1)} %get-tuple-element.51.hat_ref, f32[32,1024]{1,0:T(8,128)S(1)} %get-tuple-element.52.even_ref, f32[32,1024]{1,0:T(8,128)S(1)} %get-tuple-element.54.pos_ref, ...), custom_call_target="tpu_custom_call" | custom-call | tf_op jit(solution)/shard_map/correct_next/pallas_call | solution.py:485
  13.1 2.9 %correct_far.1 = (bf16[32,4,1024]{2,1,0:T(4,128)(2,1)S(1)}, bf16[33,4,1024]{2,1,0:T(4,128)(2,1)S(1)}, bf16[33,4,1024]{2,1,0:T(4,128)(2,1)S(1)}, bf16[33,4,1024]{2,1,0:T(4,128)(2,1)S(1)}, bf16[33,4,1024]{2,1,0:T(4,128)(2,1)S(1)}) custom-call(s32[2,4]{1,0:T(2,128)} %bitcast.18, s32[2,4]{1,0:T(2,128)} %bitcast.13, ...), custom_call_target="tpu_custom_call" | custom-call | tf_op jit(solution)/shard_map/correct_far/pallas_call | solution.py:496
  16.0 0.1 collective-permute-start.4
  16.1 1.3 %collective-permute-start.5 = (bf16[33,4,1024]{2,1,0:T(4,128)(2,1)S(1)}, bf16[33,4,1024]{2,1,0:T(4,128)(2,1)S(1)}, u32[]{:S(2)}, u32[]{:S(2)}) collective-permute-start(bf16[33,4,1024]{2,1,0:T(4,128)(2,1)S(1)} %get-tuple-element.63), channel_id=1, source_target_pairs={{0,4},{4,0},{2,6},{6,2},{8,12},{12,8},{10,14},{14,10},{1,5},{5,1},... | collective-permute-start | bytes 811016 | tf_op jit(solution)/shard_map/ppermute | solution.py:511
  17.4 4.0 %collective-permute-start.6 = (bf16[33,4,1024]{2,1,0:T(4,128)(2,1)S(1)}, bf16[33,4,1024]{2,1,0:T(4,128)(2,1)S(1)}, u32[]{:S(2)}, u32[]{:S(2)}) collective-permute-start(bf16[33,4,1024]{2,1,0:T(4,128)(2,1)S(1)} %get-tuple-element.66), channel_id=1, source_target_pairs={{2,4},{4,2},{6,8},{8,6},{10,12},{12,10},{3,5},{5,3},{7,9},{9,7},{1... | collective-permute-start | bytes 811016 | tf_op jit(solution)/shard_map/ppermute | solution.py:511
  21.5 2.4 %collective-permute-start.7 = (bf16[33,4,1024]{2,1,0:T(4,128)(2,1)S(1)}, bf16[33,4,1024]{2,1,0:T(4,128)(2,1)S(1)}, u32[]{:S(2)}, u32[]{:S(2)}) collective-permute-start(bf16[33,4,1024]{2,1,0:T(4,128)(2,1)S(1)} %get-tuple-element.67), channel_id=1, source_target_pairs={{4,8},{8,4},{6,10},{10,6},{5,9},{9,5},{7,11},{11,7},{20,24},{24,20... | collective-permute-start | bytes 811016 | tf_op jit(solution)/shard_map/ppermute | solution.py:511
  23.9 0.7 %own.1 = (f32[64,4,1024]{2,1,0:T(4,128)S(1)}, f32[64,128]{1,0:T(8,128)S(1)}) custom-call(s32[2,4]{1,0:T(2,128)S(1)} %bitcast.14, bf16[16,4,1024]{2,1,0:T(4,128)(2,1)S(1)} %get-tuple-element.53.rest_0_.refs_8_.refs_0_, bf16[16,4,1024]{2,1,0:T(4,128)(2,1)S(1)} %correct_next.1.refs_9_.refs_1_, bf16[32,4,1024]{2,1,0:T(4,128)(2,1)S(1)} %get-tuple-element.59.refs_2_), custom_call_target="tpu_custom_call" | custom-call | tf_op jit(solution)/shard_map/own/pallas_call | solution.py:514
  24.7 3.3 %collective-permute-done.4.side0_ref = bf16[33,4,1024]{2,1,0:T(4,128)(2,1)S(1)} collective-permute-done((bf16[33,4,1024]{2,1,0:T(4,128)(2,1)S(1)}, bf16[33,4,1024]{2,1,0:T(4,128)(2,1)S(1)}, u32[]{:S(2)}, u32[]{:S(2)}) %collective-permute-start.4) | collective-permute-done | bytes 270368 | tf_op jit(solution)/shard_map/ppermute | solution.py:511
  27.9 0.2 add.1
  28.2 3.4 %collective-permute-done.6.side0_ref = bf16[33,4,1024]{2,1,0:T(4,128)(2,1)S(1)} collective-permute-done((bf16[33,4,1024]{2,1,0:T(4,128)(2,1)S(1)}, bf16[33,4,1024]{2,1,0:T(4,128)(2,1)S(1)}, u32[]{:S(2)}, u32[]{:S(2)}) %collective-permute-start.6) | collective-permute-done | bytes 270368 | tf_op jit(solution)/shard_map/ppermute | solution.py:511
  31.6 2.2 %collective-permute-done.7.side1_ref = bf16[33,4,1024]{2,1,0:T(4,128)(2,1)S(1)} collective-permute-done((bf16[33,4,1024]{2,1,0:T(4,128)(2,1)S(1)}, bf16[33,4,1024]{2,1,0:T(4,128)(2,1)S(1)}, u32[]{:S(2)}, u32[]{:S(2)}) %collective-permute-start.7) | collective-permute-done | bytes 270368 | tf_op jit(solution)/shard_map/ppermute | solution.py:511
  33.8 1.1 %last.1 = (f32[64,4,1024]{2,1,0:T(4,128)S(1)}, bf16[64,4,1024]{2,1,0:T(4,128)(2,1)}) custom-call(f32[64,4,1024]{2,1,0:T(4,128)S(1)} %get-tuple-element.64.acc_in_ref, f32[64,128]{1,0:T(8,128)S(1)} %get-tuple-element.65.count_in_ref, bf16[33,4,1024]{2,1,0:T(4,128)(2,1)S(1)} %collective-permute-done.6.side0_ref, ...), custom_call_target="tpu_custom_call", output_to_operand_aliasing={{0}: (0, {})} | custom-call | tf_op jit(solution)/shard_map/last/pallas_call | solution.py:531
  (9 shorter events, 0.1 us)
Async XLA Ops:
  1.3 6.3 %collective-permute-start = (bf16[2,32,1024]{2,1,0:T(8,128)(2,1)S(1)}, bf16[2,32,1024]{2,1,0:T(8,128)(2,1)S(1)}, u32[]{:S(2)}, u32[]{:S(2)}) collective-permute-start(bf16[2,32,1024]{2,1,0:T(8,128)(2,1)S(1)} %get-tuple-element.42.here_ref.beside_ref), channel_id=1, source_target_pairs={{0,2},{2,0},{4,6},{6,4},{8,10},{10,8},{12,14},{14,12},{1,3},{3,1},... | collective-permute-start | bytes 393224 | tf_op jit(solution)/shard_map/ppermute | solution.py:411
  1.9 9.2 %collective-permute-start.2 = (bf16[2,32,1024]{2,1,0:T(8,128)(2,1)S(1)}, bf16[2,32,1024]{2,1,0:T(8,128)(2,1)S(1)}, u32[]{:S(2)}, u32[]{:S(2)}) collective-permute-start(bf16[2,32,1024]{2,1,0:T(8,128)(2,1)S(1)} %get-tuple-element.43.beside_ref.here_ref), channel_id=1, source_target_pairs={{2,4},{4,2},{6,8},{8,6},{10,12},{12,10},{3,5},{5,3},{7,9},{9,7},{1... | collective-permute-start | bytes 393224 | tf_op jit(solution)/shard_map/ppermute | solution.py:412
  7.9 1.3 %collective-permute-start.1 = (f32[2,32,128]{2,1,0:T(8,128)S(1)}, f32[2,32,128]{2,1,0:T(8,128)S(1)}, u32[]{:S(2)}, u32[]{:S(2)}) collective-permute-start(f32[2,32,128]{2,1,0:T(8,128)S(1)} %get-tuple-element.44.rest_0_), channel_id=1, source_target_pairs={{0,1},{1,0},{2,3},{3,2},{4,5},{5,4},{6,7},{7,6},{8,9},{9,8},{10,11... | collective-permute-start | bytes 98312 | tf_op jit(solution)/shard_map/ppermute | solution.py:456
  8.0 1.2 %copy-start = (bf16[64,4,1024]{2,1,0:T(4,128)(2,1)S(1)}, bf16[64,4,1024]{2,1,0:T(4,128)(2,1)}, u32[]{:S(2)}) copy-start(bf16[64,4,1024]{2,1,0:T(4,128)(2,1)} %refs_6_.1) | copy-start | bytes 1572868
  11.4 1.7 %collective-permute-start.3 = (f32[2,32,128]{2,1,0:T(8,128)S(1)}, f32[2,32,128]{2,1,0:T(8,128)S(1)}, u32[]{:S(2)}, u32[]{:S(2)}) collective-permute-start(f32[2,32,128]{2,1,0:T(8,128)S(1)} %get-tuple-element.55.rest_0_), channel_id=1, source_target_pairs={{0,1},{1,0},{2,3},{3,2},{4,5},{5,4},{6,7},{7,6},{8,9},{9,8},{10,11... | collective-permute-start | bytes 98312 | tf_op jit(solution)/shard_map/ppermute | solution.py:456
  16.0 11.9 %collective-permute-start.4 = (bf16[33,4,1024]{2,1,0:T(4,128)(2,1)S(1)}, bf16[33,4,1024]{2,1,0:T(4,128)(2,1)S(1)}, u32[]{:S(2)}, u32[]{:S(2)}) collective-permute-start(bf16[33,4,1024]{2,1,0:T(4,128)(2,1)S(1)} %get-tuple-element.62), channel_id=1, source_target_pairs={{0,2},{2,0},{4,6},{6,4},{8,10},{10,8},{12,14},{14,12},{1,3},{3,1},... | collective-permute-start | bytes 811016 | tf_op jit(solution)/shard_map/ppermute | solution.py:511
  16.1 11.9 %collective-permute-start.5 = (bf16[33,4,1024]{2,1,0:T(4,128)(2,1)S(1)}, bf16[33,4,1024]{2,1,0:T(4,128)(2,1)S(1)}, u32[]{:S(2)}, u32[]{:S(2)}) collective-permute-start(bf16[33,4,1024]{2,1,0:T(4,128)(2,1)S(1)} %get-tuple-element.63), channel_id=1, source_target_pairs={{0,4},{4,0},{2,6},{6,2},{8,12},{12,8},{10,14},{14,10},{1,5},{5,1},... | collective-permute-start | bytes 811016 | tf_op jit(solution)/shard_map/ppermute | solution.py:511
  17.4 14.2 %collective-permute-start.6 = (bf16[33,4,1024]{2,1,0:T(4,128)(2,1)S(1)}, bf16[33,4,1024]{2,1,0:T(4,128)(2,1)S(1)}, u32[]{:S(2)}, u32[]{:S(2)}) collective-permute-start(bf16[33,4,1024]{2,1,0:T(4,128)(2,1)S(1)} %get-tuple-element.66), channel_id=1, source_target_pairs={{2,4},{4,2},{6,8},{8,6},{10,12},{12,10},{3,5},{5,3},{7,9},{9,7},{1... | collective-permute-start | bytes 811016 | tf_op jit(solution)/shard_map/ppermute | solution.py:511
  21.5 2.5 %copy-start.1 = (s32[4,2]{0,1:T(2,128)S(1)}, s32[4,2]{0,1:T(2,128)}, u32[]{:S(2)}) copy-start(s32[4,2]{0,1:T(2,128)} %param.21) | copy-start | bytes 100
  21.5 12.3 %collective-permute-start.7 = (bf16[33,4,1024]{2,1,0:T(4,128)(2,1)S(1)}, bf16[33,4,1024]{2,1,0:T(4,128)(2,1)S(1)}, u32[]{:S(2)}, u32[]{:S(2)}) collective-permute-start(bf16[33,4,1024]{2,1,0:T(4,128)(2,1)S(1)} %get-tuple-element.67), channel_id=1, source_target_pairs={{4,8},{8,4},{6,10},{10,6},{5,9},{9,5},{7,11},{11,7},{20,24},{24,20... | collective-permute-start | bytes 811016 | tf_op jit(solution)/shard_map/ppermute | solution.py:511

commit v6 on v5

--- a/solution.py
+++ b/solution.py
@@ -224,7 +224,6 @@
 
         level = both(class_ref, base + row)
         w_even = both(even_ref, first + row)
-        w_odd = 1.0 - w_even
         below = [level < k for k in range(7)]
 
         def coefficient(table):
@@ -235,9 +234,9 @@
             odd = jnp.where(
                 below[4], jnp.where(below[2], node[1], node[3]), jnp.where(below[6], node[5], node[7])
             )
-            return w_even * even + w_odd * odd
-
-        toa = jnp.concatenate([toa_ref[base + row + k, :, at].astype(F32) for k in range(2)], axis=0)
+            return odd + w_even * (even - odd)
+
+        toa = toa_ref[pl.ds(base + row, 2), :, at].astype(F32).reshape(8, step)
         scaled = coefficient(0) * toa - coefficient(1)
         surface = scaled / (1.0 + coefficient(2) * scaled)
         corr_ref[row, :, at] = surface[:4].astype(BF16)
@@ -452,7 +451,7 @@
             out_specs=(VMEM, VMEM),
             compiler_params=params(),
             name="hats",
-        )(vapours, classes, fracs, edge)
+        )(vapours, classes, fracs, after[0] if after else edge)
         return edge, lax.ppermute(edge, "across", swap_pairs(lax.axis_size("across"), 1, 0)), ext, *hats
 
 

time: 35.1 us -> 35 us (level)
  no operation moved by 1% of the time
where the time goes in v6:
time: 35 us; the launch traced here: 34.8 us
  starting transfers between devices  13.4 us (38%)
  Pallas kernels  11.8 us (34%)
  waiting for transfers between devices  9.48 us (27%)
    ppermute x4, waiting for transfers between devices, body(): got[k] = lax.ppermute(sides[k], 'along', swap_pairs(count, step, offset))  8.9 us
    ppermute x4, starting transfers between devices, body(): got[k] = lax.ppermute(sides[k], 'along', swap_pairs(count, step, offset))  7.9 us
    ppermute x1, starting transfers between devices, body(): far_in = lax.ppermute(far_out, 'along', swap_pairs(count, 1, 1))  4.43 us
    pallas_call x1, Pallas kernels, body(): pl.pallas_call(functools.partial(correct_far_kernel, levels_a), out_shape...  2.83 us
    pallas_call x1, Pallas kernels, body(): pl.pallas_call(functools.partial(near_kernel, levels_a), out_shape=(part,...  1.84 us
    pallas_call x1, Pallas kernels, body(): pl.pallas_call(prep_kernel, out_shape=(fields, fields), in_specs=[HBM, HB...  1.32 us
    pallas_call x1, Pallas kernels, body(): pl.pallas_call(early_kernel, out_shape=(*brought, jax.ShapeDtypeStruct((2...  1.3 us
    pallas_call x1, Pallas kernels, body(): pl.pallas_call(last_kernel, out_shape=(total, jax.ShapeDtypeStruct((rows,...  1.11 us
  transfers between devices with their start and end apart: 8, of which 4 were waited for; matrix products, arithmetic and copies ran while one was open for 0% of the time, Pallas kernels for 18%

profile of v6, /device:TPU:20, one launch (start us, length us, event | category | flops | bytes accessed | tf_op | source)
XLA Modules:
  0.0 34.8 jit_solution(4288015845806729253)
XLA Ops:
  0.0 1.3 %prep.1 = (bf16[2,32,1024]{2,1,0:T(8,128)(2,1)S(1)}, bf16[2,32,1024]{2,1,0:T(8,128)(2,1)S(1)}) custom-call(bf16[64,4,1024]{2,1,0:T(4,128)(2,1)} %refs_6_.1, s32[64,1024]{1,0:T(8,128)} %dark_ref.1), custom_call_target="tpu_custom_call" | custom-call | tf_op jit(solution)/shard_map/prep/pallas_call | solution.py:397
  1.3 0.6 %collective-permute-start = (bf16[2,32,1024]{2,1,0:T(8,128)(2,1)S(1)}, bf16[2,32,1024]{2,1,0:T(8,128)(2,1)S(1)}, u32[]{:S(2)}, u32[]{:S(2)}) collective-permute-start(bf16[2,32,1024]{2,1,0:T(8,128)(2,1)S(1)} %get-tuple-element.42.here_ref.beside_ref), channel_id=1, source_target_pairs={{0,2},{2,0},{4,6},{6,4},{8,10},{10,8},{12,14},{14,12},{1,3},{3,1},... | collective-permute-start | bytes 393224 | tf_op jit(solution)/shard_map/ppermute | solution.py:410
  1.9 4.4 %collective-permute-start.2 = (bf16[2,32,1024]{2,1,0:T(8,128)(2,1)S(1)}, bf16[2,32,1024]{2,1,0:T(8,128)(2,1)S(1)}, u32[]{:S(2)}, u32[]{:S(2)}) collective-permute-start(bf16[2,32,1024]{2,1,0:T(8,128)(2,1)S(1)} %get-tuple-element.43.beside_ref.here_ref), channel_id=1, source_target_pairs={{2,4},{4,2},{6,8},{8,6},{10,12},{12,10},{3,5},{5,3},{7,9},{9,7},{1... | collective-permute-start | bytes 393224 | tf_op jit(solution)/shard_map/ppermute | solution.py:411
  6.3 1.3 %early.1 = (bf16[256,16]{1,0:T(8,128)(2,1)S(1)}, bf16[256,16]{1,0:T(8,128)(2,1)S(1)}, bf16[256,16]{1,0:T(8,128)(2,1)S(1)}, f32[64,1024]{1,0:T(8,128)S(1)}, s32[6...) custom-call(f32[1,61]{1,0:T(1,128)} %bitcast.19, ...), custom_call_target="tpu_custom_call" | custom-call | tf_op jit(solution)/shard_map/early/pallas_call | solution.py:421
  7.7 0.3 vertical.2
  7.9 0.1 collective-permute-start.1
  8.0 0.2 hats.2
  8.3 0.4 %tables.1 = (bf16[192,256]{1,0:T(8,128)(2,1)S(1)}, bf16[2,256,512]{2,1,0:T(8,128)(2,1)S(1)}) custom-call(f32[1,61]{1,0:T(1,128)S(1)} %get-tuple-element.37.taps_ref, bf16[256,16]{1,0:T(8,128)(2,1)S(1)} %get-tuple-element.38.gain_ref, bf16[256,16]{1,0:T(8,128)(2,1)S(1)} %get-tuple-element.39.path_ref, bf16[256,16]{1,0:T(8,128)(2,1)S(1)} %get-tuple-element.40.albedo_ref, ...), custom_call_target="tpu_custom_call" | custom-call | tf_op jit(solution)/shard_map/tables/pallas_call | solution.py:460
  8.6 0.6 %collective-permute-done.1.edge_ref = f32[2,32,128]{2,1,0:T(8,128)S(1)} collective-permute-done((f32[2,32,128]{2,1,0:T(8,128)S(1)}, f32[2,32,128]{2,1,0:T(8,128)S(1)}, u32[]{:S(2)}, u32[]{:S(2)}) %collective-permute-start.1) | collective-permute-done | bytes 32800 | tf_op jit(solution)/shard_map/ppermute | solution.py:455
  9.2 1.8 %correct_near.1 = (bf16[16,4,1024]{2,1,0:T(4,128)(2,1)S(1)}, f32[32,1024]{1,0:T(8,128)S(1)}) custom-call(bf16[2,256,512]{2,1,0:T(8,128)(2,1)S(1)} %get-tuple-element.45.bands_ref.refs_0_, bf16[192,256]{1,0:T(8,128)(2,1)S(1)} %get-tuple-element.46.lut_ref.refs_1_, f32[2,32,128]{2,1,0:T(8,128)S(1)} %collective-permute-done.1.edge_ref, ...), custom_call_target="tpu_custom_call" | custom-call | tf_op jit(solution)/shard_map/correct_near/pallas_call | solution.py:472
  11.1 0.3 vertical.3
  11.4 0.4 %collective-permute-start.3 = (f32[2,32,128]{2,1,0:T(8,128)S(1)}, f32[2,32,128]{2,1,0:T(8,128)S(1)}, u32[]{:S(2)}, u32[]{:S(2)}) collective-permute-start(f32[2,32,128]{2,1,0:T(8,128)S(1)} %get-tuple-element.55.rest_0_), channel_id=1, source_target_pairs={{0,1},{1,0},{2,3},{3,2},{4,5},{5,4},{6,7},{7,6},{8,9},{9,8},{10,11... | collective-permute-start | bytes 98312 | tf_op jit(solution)/shard_map/ppermute | solution.py:455
  11.8 0.2 hats.3
  12.0 1.1 %correct_next.1.refs_9_.refs_1_ = bf16[16,4,1024]{2,1,0:T(4,128)(2,1)S(1)} custom-call(bf16[192,256]{1,0:T(8,128)(2,1)S(1)} %get-tuple-element.46.lut_ref.refs_1_, f32[8,32,1024]{2,1,0:T(8,128)S(1)} %get-tuple-element.51.hat_ref, f32[32,1024]{1,0:T(8,128)S(1)} %get-tuple-element.52.even_ref, f32[32,1024]{1,0:T(8,128)S(1)} %get-tuple-element.54.pos_ref, ...), custom_call_target="tpu_custom_call" | custom-call | tf_op jit(solution)/shard_map/correct_next/pallas_call | solution.py:484
  13.1 2.8 %correct_far.1 = (bf16[32,4,1024]{2,1,0:T(4,128)(2,1)S(1)}, bf16[33,4,1024]{2,1,0:T(4,128)(2,1)S(1)}, bf16[33,4,1024]{2,1,0:T(4,128)(2,1)S(1)}, bf16[33,4,1024]{2,1,0:T(4,128)(2,1)S(1)}, bf16[33,4,1024]{2,1,0:T(4,128)(2,1)S(1)}) custom-call(s32[2,4]{1,0:T(2,128)} %bitcast.18, s32[2,4]{1,0:T(2,128)} %bitcast.13, ...), custom_call_target="tpu_custom_call" | custom-call | tf_op jit(solution)/shard_map/correct_far/pallas_call | solution.py:495
  16.0 1.3 %collective-permute-start.5 = (bf16[33,4,1024]{2,1,0:T(4,128)(2,1)S(1)}, bf16[33,4,1024]{2,1,0:T(4,128)(2,1)S(1)}, u32[]{:S(2)}, u32[]{:S(2)}) collective-permute-start(bf16[33,4,1024]{2,1,0:T(4,128)(2,1)S(1)} %get-tuple-element.63), channel_id=1, source_target_pairs={{0,4},{4,0},{2,6},{6,2},{8,12},{12,8},{10,14},{14,10},{1,5},{5,1},... | collective-permute-start | bytes 811016 | tf_op jit(solution)/shard_map/ppermute | solution.py:510
  17.3 4.0 %collective-permute-start.6 = (bf16[33,4,1024]{2,1,0:T(4,128)(2,1)S(1)}, bf16[33,4,1024]{2,1,0:T(4,128)(2,1)S(1)}, u32[]{:S(2)}, u32[]{:S(2)}) collective-permute-start(bf16[33,4,1024]{2,1,0:T(4,128)(2,1)S(1)} %get-tuple-element.66), channel_id=1, source_target_pairs={{2,4},{4,2},{6,8},{8,6},{10,12},{12,10},{3,5},{5,3},{7,9},{9,7},{1... | collective-permute-start | bytes 811016 | tf_op jit(solution)/shard_map/ppermute | solution.py:510
  21.4 2.5 %collective-permute-start.7 = (bf16[33,4,1024]{2,1,0:T(4,128)(2,1)S(1)}, bf16[33,4,1024]{2,1,0:T(4,128)(2,1)S(1)}, u32[]{:S(2)}, u32[]{:S(2)}) collective-permute-start(bf16[33,4,1024]{2,1,0:T(4,128)(2,1)S(1)} %get-tuple-element.67), channel_id=1, source_target_pairs={{4,8},{8,4},{6,10},{10,6},{5,9},{9,5},{7,11},{11,7},{20,24},{24,20... | collective-permute-start | bytes 811016 | tf_op jit(solution)/shard_map/ppermute | solution.py:510
  23.8 0.7 %own.1 = (f32[64,4,1024]{2,1,0:T(4,128)S(1)}, f32[64,128]{1,0:T(8,128)S(1)}) custom-call(s32[2,4]{1,0:T(2,128)S(1)} %bitcast.14, bf16[16,4,1024]{2,1,0:T(4,128)(2,1)S(1)} %get-tuple-element.53.rest_0_.refs_8_.refs_0_, bf16[16,4,1024]{2,1,0:T(4,128)(2,1)S(1)} %correct_next.1.refs_9_.refs_1_, bf16[32,4,1024]{2,1,0:T(4,128)(2,1)S(1)} %get-tuple-element.59.refs_2_), custom_call_target="tpu_custom_call" | custom-call | tf_op jit(solution)/shard_map/own/pallas_call | solution.py:513
  24.6 3.3 %collective-permute-done.4.side0_ref = bf16[33,4,1024]{2,1,0:T(4,128)(2,1)S(1)} collective-permute-done((bf16[33,4,1024]{2,1,0:T(4,128)(2,1)S(1)}, bf16[33,4,1024]{2,1,0:T(4,128)(2,1)S(1)}, u32[]{:S(2)}, u32[]{:S(2)}) %collective-permute-start.4) | collective-permute-done | bytes 270368 | tf_op jit(solution)/shard_map/ppermute | solution.py:510
  27.8 0.2 add.1
  28.1 3.4 %collective-permute-done.6.side0_ref = bf16[33,4,1024]{2,1,0:T(4,128)(2,1)S(1)} collective-permute-done((bf16[33,4,1024]{2,1,0:T(4,128)(2,1)S(1)}, bf16[33,4,1024]{2,1,0:T(4,128)(2,1)S(1)}, u32[]{:S(2)}, u32[]{:S(2)}) %collective-permute-start.6) | collective-permute-done | bytes 270368 | tf_op jit(solution)/shard_map/ppermute | solution.py:510
  31.5 2.2 %collective-permute-done.7.side1_ref = bf16[33,4,1024]{2,1,0:T(4,128)(2,1)S(1)} collective-permute-done((bf16[33,4,1024]{2,1,0:T(4,128)(2,1)S(1)}, bf16[33,4,1024]{2,1,0:T(4,128)(2,1)S(1)}, u32[]{:S(2)}, u32[]{:S(2)}) %collective-permute-start.7) | collective-permute-done | bytes 270368 | tf_op jit(solution)/shard_map/ppermute | solution.py:510
  33.7 1.1 %last.1 = (f32[64,4,1024]{2,1,0:T(4,128)S(1)}, bf16[64,4,1024]{2,1,0:T(4,128)(2,1)}) custom-call(f32[64,4,1024]{2,1,0:T(4,128)S(1)} %get-tuple-element.64.acc_in_ref, f32[64,128]{1,0:T(8,128)S(1)} %get-tuple-element.65.count_in_ref, bf16[33,4,1024]{2,1,0:T(4,128)(2,1)S(1)} %collective-permute-done.6.side0_ref, ...), custom_call_target="tpu_custom_call", output_to_operand_aliasing={{0}: (0, {})} | custom-call | tf_op jit(solution)/shard_map/last/pallas_call | solution.py:530
  (9 shorter events, 0.1 us)
Async XLA Ops:
  1.3 6.3 %collective-permute-start = (bf16[2,32,1024]{2,1,0:T(8,128)(2,1)S(1)}, bf16[2,32,1024]{2,1,0:T(8,128)(2,1)S(1)}, u32[]{:S(2)}, u32[]{:S(2)}) collective-permute-start(bf16[2,32,1024]{2,1,0:T(8,128)(2,1)S(1)} %get-tuple-element.42.here_ref.beside_ref), channel_id=1, source_target_pairs={{0,2},{2,0},{4,6},{6,4},{8,10},{10,8},{12,14},{14,12},{1,3},{3,1},... | collective-permute-start | bytes 393224 | tf_op jit(solution)/shard_map/ppermute | solution.py:410
  1.9 9.2 %collective-permute-start.2 = (bf16[2,32,1024]{2,1,0:T(8,128)(2,1)S(1)}, bf16[2,32,1024]{2,1,0:T(8,128)(2,1)S(1)}, u32[]{:S(2)}, u32[]{:S(2)}) collective-permute-start(bf16[2,32,1024]{2,1,0:T(8,128)(2,1)S(1)} %get-tuple-element.43.beside_ref.here_ref), channel_id=1, source_target_pairs={{2,4},{4,2},{6,8},{8,6},{10,12},{12,10},{3,5},{5,3},{7,9},{9,7},{1... | collective-permute-start | bytes 393224 | tf_op jit(solution)/shard_map/ppermute | solution.py:411
  7.9 1.3 %collective-permute-start.1 = (f32[2,32,128]{2,1,0:T(8,128)S(1)}, f32[2,32,128]{2,1,0:T(8,128)S(1)}, u32[]{:S(2)}, u32[]{:S(2)}) collective-permute-start(f32[2,32,128]{2,1,0:T(8,128)S(1)} %get-tuple-element.44.rest_0_), channel_id=1, source_target_pairs={{0,1},{1,0},{2,3},{3,2},{4,5},{5,4},{6,7},{7,6},{8,9},{9,8},{10,11... | collective-permute-start | bytes 98312 | tf_op jit(solution)/shard_map/ppermute | solution.py:455
  8.0 1.2 %copy-start = (bf16[64,4,1024]{2,1,0:T(4,128)(2,1)S(1)}, bf16[64,4,1024]{2,1,0:T(4,128)(2,1)}, u32[]{:S(2)}) copy-start(bf16[64,4,1024]{2,1,0:T(4,128)(2,1)} %refs_6_.1) | copy-start | bytes 1572868
  11.4 1.7 %collective-permute-start.3 = (f32[2,32,128]{2,1,0:T(8,128)S(1)}, f32[2,32,128]{2,1,0:T(8,128)S(1)}, u32[]{:S(2)}, u32[]{:S(2)}) collective-permute-start(f32[2,32,128]{2,1,0:T(8,128)S(1)} %get-tuple-element.55.rest_0_), channel_id=1, source_target_pairs={{0,1},{1,0},{2,3},{3,2},{4,5},{5,4},{6,7},{7,6},{8,9},{9,8},{10,11... | collective-permute-start | bytes 98312 | tf_op jit(solution)/shard_map/ppermute | solution.py:455
  15.9 11.9 %collective-permute-start.4 = (bf16[33,4,1024]{2,1,0:T(4,128)(2,1)S(1)}, bf16[33,4,1024]{2,1,0:T(4,128)(2,1)S(1)}, u32[]{:S(2)}, u32[]{:S(2)}) collective-permute-start(bf16[33,4,1024]{2,1,0:T(4,128)(2,1)S(1)} %get-tuple-element.62), channel_id=1, source_target_pairs={{0,2},{2,0},{4,6},{6,4},{8,10},{10,8},{12,14},{14,12},{1,3},{3,1},... | collective-permute-start | bytes 811016 | tf_op jit(solution)/shard_map/ppermute | solution.py:510
  16.0 11.9 %collective-permute-start.5 = (bf16[33,4,1024]{2,1,0:T(4,128)(2,1)S(1)}, bf16[33,4,1024]{2,1,0:T(4,128)(2,1)S(1)}, u32[]{:S(2)}, u32[]{:S(2)}) collective-permute-start(bf16[33,4,1024]{2,1,0:T(4,128)(2,1)S(1)} %get-tuple-element.63), channel_id=1, source_target_pairs={{0,4},{4,0},{2,6},{6,2},{8,12},{12,8},{10,14},{14,10},{1,5},{5,1},... | collective-permute-start | bytes 811016 | tf_op jit(solution)/shard_map/ppermute | solution.py:510
  17.3 14.2 %collective-permute-start.6 = (bf16[33,4,1024]{2,1,0:T(4,128)(2,1)S(1)}, bf16[33,4,1024]{2,1,0:T(4,128)(2,1)S(1)}, u32[]{:S(2)}, u32[]{:S(2)}) collective-permute-start(bf16[33,4,1024]{2,1,0:T(4,128)(2,1)S(1)} %get-tuple-element.66), channel_id=1, source_target_pairs={{2,4},{4,2},{6,8},{8,6},{10,12},{12,10},{3,5},{5,3},{7,9},{9,7},{1... | collective-permute-start | bytes 811016 | tf_op jit(solution)/shard_map/ppermute | solution.py:510
  21.4 2.5 %copy-start.1 = (s32[4,2]{0,1:T(2,128)S(1)}, s32[4,2]{0,1:T(2,128)}, u32[]{:S(2)}) copy-start(s32[4,2]{0,1:T(2,128)} %param.21) | copy-start | bytes 100
  21.4 12.3 %collective-permute-start.7 = (bf16[33,4,1024]{2,1,0:T(4,128)(2,1)S(1)}, bf16[33,4,1024]{2,1,0:T(4,128)(2,1)S(1)}, u32[]{:S(2)}, u32[]{:S(2)}) collective-permute-start(bf16[33,4,1024]{2,1,0:T(4,128)(2,1)S(1)} %get-tuple-element.67), channel_id=1, source_target_pairs={{4,8},{8,4},{6,10},{10,6},{5,9},{9,5},{7,11},{11,7},{20,24},{24,20... | collective-permute-start | bytes 811016 | tf_op jit(solution)/shard_map/ppermute | solution.py:510
